TPU v7x, 32 devices: a whole 2x2x4 slice. The times are simulated.
32 devices in a mesh: parts: 2 (over y), row: 4 (over z), frame: 4 (over x, core).
Axes of the slice: x: 2, y: 2, z: 4, core: 2. Of those that a mesh axis runs over, the one named last changes fastest.
Arguments:
- latent: bfloat16 [8, 8, 16, 512], P(('parts', 'frame'), 'row'), parts along dimension 0, may hold values from -15 to 15
- qkv_weight: bfloat16 [3, 512, 512], P(None, 'frame'), may hold values from -0.125 to 0.125
- out_weight: bfloat16 [512, 512], P('frame'), may hold values from -0.25 to 0.25
- attn_gain: float32 [512], replicated, may hold values from 0.1 to 1.9
- in_weight: bfloat16 [512, 2, 2048], P(None, None, 'frame'), may hold values from -0.25 to 0.25
- depth_weight: float32 [3, 3, 2, 2048], replicated, may hold values from -2 to 2
- down_weight: bfloat16 [2048, 512], P('frame'), may hold values from -0.125 to 0.125
- mlp_gain: float32 [512], replicated, may hold values from 0.1 to 1.9
- conv_first: bfloat16 [3, 3, 3, 512, 512], P(None, None, None, 'frame'), may hold values from -0.0546875 to 0.0546875
- conv_second: bfloat16 [3, 3, 3, 512, 512], P(None, None, None, 'frame'), may hold values from -0.0546875 to 0.0546875
Outputs:
- decoded: bfloat16 [8, 8, 16, 512], P('parts', 'row', 'frame'), parts along dimension 0
There are 2 independent parts, one for each index of `parts`. A program takes and returns all parts, laid end to end along the dimension named above; an argument that names none is the same for every part. Nothing has to cross between parts.
All inputs are finite; a program needn't handle non-finite values.
Results may differ from a plain program's by a relative error of at most 0.015.
Values may be sent and summed in bfloat16 or wider, within the bound.
No kernel may reach another device: no remote copies, remote signals or barrier semaphores. Data moves between devices by JAX's collectives and lax.ppermute only.
A program may use at most 128 MiB of HBM per device.

v0:
```python
import jax
import jax.numpy as jnp
from jax import lax
from jax.sharding import PartitionSpec as P

HEAD = 32


def padded_2(cells, sides, width):
    for axis, dim in sides:
        count = lax.axis_size(axis)
        ends = count - 1
        head = lax.slice_in_dim(cells, 0, width, axis=dim)
        tail = lax.slice_in_dim(cells, cells.shape[dim] - width, cells.shape[dim], axis=dim)
        cells = jnp.concatenate(
            [
                lax.ppermute(tail, axis, [(i, (i + 1) % count) for i in range(ends)]),
                cells,
                lax.ppermute(head, axis, [((i + 1) % count, i) for i in range(ends)]),
            ],
            axis=dim,
        )
    return cells


def norm_rows(values, gain):
    return values * lax.rsqrt(jnp.mean(values * values, axis=-1, keepdims=True) + 1e-05) * gain


def attend(packed):
    frames, height, columns = (packed.shape[0], packed.shape[1], packed.shape[2])
    width = packed.shape[4]
    heads = width // HEAD
    flat = packed.reshape(frames, height * columns, 3, heads, HEAD)
    query = jnp.maximum(flat[:, :, 0], 0)
    keys = jnp.maximum(flat[:, :, 1], 0)
    values = flat[:, :, 2]
    state = jnp.einsum("fnhd,fnhe->fhde", keys, values, preferred_element_type=jnp.float32)
    key_total = jnp.sum(keys.astype(jnp.float32), axis=1)
    state, key_total = (
        lax.psum(state.astype(jnp.bfloat16), "row").astype(jnp.float32),
        lax.psum(key_total.astype(jnp.bfloat16), "row").astype(jnp.float32),
    )
    count = height * lax.axis_size("row") * columns
    state = state / count
    key_mean = key_total / count
    query_wide = query.astype(jnp.float32)
    numer = jnp.einsum("fnhd,fhde->fnhe", query_wide, state, precision=lax.Precision.HIGHEST)
    denom = jnp.maximum(
        jnp.einsum("fnhd,fhd->fnh", query_wide, key_mean, precision=lax.Precision.HIGHEST), 1.0
    )
    return (numer / denom[..., None]).astype(jnp.bfloat16).reshape(frames, height, columns, width)


def depth_mix(inner, depth_local):
    height, columns = (inner.shape[1], inner.shape[2])
    extended = padded_2(inner, (("row", 1),), 1)
    padded = jnp.pad(extended, ((0, 0), (0, 0), (1, 1), (0, 0), (0, 0)))
    spread = jnp.zeros(inner.shape, jnp.float32)
    for shift_row in range(3):
        for shift_col in range(3):
            spread = (
                spread
                + padded[:, shift_row : shift_row + height, shift_col : shift_col + columns].astype(
                    jnp.float32
                )
                * depth_local[shift_row, shift_col]
            )
    return (spread[..., 0, :] * jax.nn.silu(spread[..., 1, :])).astype(jnp.bfloat16)


def conv_tile(extended, kernel):
    frames, padded_rows, columns, width = extended.shape
    height = padded_rows - 2
    out_width = kernel.shape[3]
    padded = jnp.pad(extended, ((1, 1), (0, 0), (1, 1), (0, 0)))
    result = jnp.zeros((frames * height * columns, out_width), jnp.float32)
    for shift_time in range(3):
        for shift_row in range(3):
            slab = padded[shift_time : shift_time + frames, shift_row : shift_row + height]
            stacked = jnp.stack(
                [slab[:, :, shift_col : shift_col + columns] for shift_col in range(3)], axis=3
            )
            result = result + jnp.einsum(
                "nci,coi->no",
                stacked.reshape(-1, 3, width),
                kernel[shift_time, shift_row],
                preferred_element_type=jnp.float32,
            )
    return result.reshape(frames, height, columns, out_width)


def local(
    latent,
    qkv_weight,
    out_weight,
    attn_gain,
    in_weight,
    depth_weight,
    down_weight,
    mlp_gain,
    conv_first,
    conv_second,
):
    frames, height, columns, width = latent.shape
    place = lax.axis_index("frame")
    packed = jnp.einsum(
        "frwc,kjc->frwkj",
        latent,
        lax.all_gather(qkv_weight, "frame", axis=1, tiled=True),
        preferred_element_type=jnp.float32,
    ).astype(jnp.bfloat16)
    mixed = attend(packed)
    section = mixed
    attn_out = jnp.einsum(
        "frwj,jc->frwc",
        section,
        lax.all_gather(out_weight, "frame", axis=0, tiled=True),
        preferred_element_type=jnp.float32,
    )
    first = (latent.astype(jnp.float32) + norm_rows(attn_out, attn_gain)).astype(jnp.bfloat16)
    inner = jax.nn.silu(
        jnp.einsum(
            "frwc,ckj->frwkj",
            first,
            lax.all_gather(in_weight, "frame", axis=2, tiled=True),
            preferred_element_type=jnp.float32,
        )
    ).astype(jnp.bfloat16)
    gated = depth_mix(inner, depth_weight)
    section = gated
    mlp_out = jnp.einsum(
        "frwj,jc->frwc",
        section,
        lax.all_gather(down_weight, "frame", axis=0, tiled=True),
        preferred_element_type=jnp.float32,
    )
    second = (first.astype(jnp.float32) + norm_rows(mlp_out, mlp_gain)).astype(jnp.bfloat16)
    gathered = lax.all_gather(second, "frame", axis=0, tiled=True)
    out_share = conv_first.shape[3]
    extended = padded_2(gathered, (("row", 1),), 2)
    activated = jax.nn.silu(conv_tile(extended, conv_first))
    global_row = lax.axis_index("row") * height - 1 + lax.iota(jnp.int32, height + 2)
    inside = ((global_row >= 0) & (global_row < height * lax.axis_size("row"))).astype(jnp.float32)
    hidden_conv = (activated * inside[None, :, None, None]).astype(jnp.bfloat16)
    joined = lax.all_gather(hidden_conv, "frame", axis=3, tiled=True)
    result = conv_tile(joined, conv_second)
    own_part = lax.dynamic_slice_in_dim(gathered, place * out_share, out_share, 3)
    final = (own_part.astype(jnp.float32) + result).astype(jnp.bfloat16)
    return lax.all_to_all(final, "frame", split_axis=2, concat_axis=3, tiled=True)


def solution(mesh):
    in_specs = (
        P(("parts", "frame"), "row", None, None),
        P(None, "frame", None),
        P("frame", None),
        P(),
        P(None, None, "frame"),
        P(),
        P("frame", None),
        P(),
        P(None, None, None, "frame", None),
        P(None, None, None, "frame", None),
    )
    out_specs = P("parts", "row", "frame", None)
    return jax.shard_map(local, mesh=mesh, in_specs=in_specs, out_specs=out_specs, check_vma=False)
```

profile of v0, /device:TPU:0, one launch (start us, length us, event | category | flops | bytes accessed | tf_op | source)
XLA Modules:
  0.0 137.9 jit_solution(649510478248561732)
XLA Ops:
  6.5 0.7 all-gather.4.cloned.1.call-update
  7.3 2.4 %copy.34 = bf16[512,2,512]{2,0,1:T(8,128)(2,1)} copy(bf16[512,2,512]{2,1,0:T(2,128)(2,1)} %param.14) | data formatting | bytes 2097152 | tf_op args[4]
  9.8 0.7 all-gather.8.cloned.1.call-update
  10.5 8.6 %all_gather.19 = bf16[512,512]{1,0:T(8,128)(2,1)S(1)} all-gather(bf16[128,512]{1,0:T(8,128)(2,1)S(1)} %copy-done.1), channel_id=1, replica_groups=mesh['parts'=2,'row'=4,'frame'=4] {'frame'}, dimensions={0}, use_global_device_ids=true | all-gather | bytes 655360 | tf_op jit(solution)/shard_map/all_gather | solution.py:118
  19.1 12.2 %all-gather.4.cloned.1.call-done = bf16[3,512,512]{2,1,0:T(8,128)(2,1)} async-done(((bf16[3,128,512]{2,1,0:T(8,128)(2,1)}), bf16[3,512,512]{2,1,0:T(8,128)(2,1)}) %all-gather.4.cloned.1.call-update) | async-done | bytes 1572880 | tf_op jit(solution)/shard_map/all_gather | solution.py:110
  31.3 2.0 %fusion.7 = bf16[2,16,3,512]{3,1,2,0:T(8,128)(2,1)S(1)} fusion(bf16[3,512,512]{2,1,0:T(8,128)(2,1)} %all-gather.4.cloned.1.call-done, bf16[1,2,16,512]{3,2,1,0:T(8,128)(2,1)S(1)} %copy-done.2), kind=kOutput, calls=%fused_computation.59 | convolution fusion | flops 50380800 | bytes 1703936 | tf_op jit(solution)/shard_map/frwc,kjc->frwkj/dot_general | solution.py:107
  34.1 21.3 %all-reduce.3 = (bf16[1,16,32,32]{3,2,1,0:T(8,128)(2,1)S(1)}, bf16[1,16,32]{2,1,0:T(8,128)(2,1)S(1)}) all-reduce(bf16[1,16,32,32]{3,2,1,0:T(8,128)(2,1)S(1)} %fusion.10, bf16[1,16,32]{2,1,0:T(8,128)(2,1)S(1)} %bitcast.373), channel_id=1, replica_groups=mesh['parts'=2,'row'=4,'frame'=4] {'row'}, use_global_device_ids=true, to_apply=%region_0.0 | all-reduce | flops 16896 | bytes 67584 | tf_op jit(solution)/shard_map/psum | solution.py:41
  56.9 10.4 %all-gather.6.cloned.1.call-done = bf16[512,2,2048]{2,0,1:T(8,128)(2,1)} async-done(((bf16[512,2,512]{2,0,1:T(8,128)(2,1)}), bf16[512,2,2048]{2,0,1:T(8,128)(2,1)}) %all-gather.6.cloned.1.call-update) | async-done | bytes 4194320 | tf_op jit(solution)/shard_map/all_gather | solution.py:126
  67.4 3.0 %multiply_convert_fusion = bf16[2,16,2,2048]{3,1,2,0:T(8,128)(2,1)S(1)} fusion(bf16[512,2,2048]{2,0,1:T(8,128)(2,1)} %all-gather.6.cloned.1.call-done, bf16[1,2,16,512]{3,2,1,0:T(8,128)(2,1)S(1)} %fusion.184), kind=kOutput, calls=%fused_computation.154 | convolution fusion | flops 134873088 | bytes 4489216 | tf_op jit(solution)/shard_map/frwc,ckj->frwkj/dot_general | solution.py:123
  70.5 3.4 %collective-permute-start = (bf16[1,1,16,2,2048]{4,2,3,1,0:T(8,128)(2,1)S(1)}, bf16[1,1,16,2,2048]{4,2,3,1,0:T(8,128)(2,1)S(1)}, u32[]{:S(2)}, u32[]{:S(2)}) collective-permute-start(bf16[1,1,16,2,2048]{4,2,3,1,0:T(8,128)(2,1)S(1)} %get-tuple-element.62), channel_id=1, source_target_pairs={{0,4},{4,8},{8,12},{1,5},{5,9},{9,13},{2,6},{6,10},{10,14},{3,7},{... | collective-permute-start | bytes 393224 | tf_op jit(solution)/shard_map/ppermute | solution.py:17
  73.9 1.3 collective-permute-start.1
  75.2 1.8 %collective-permute-done = bf16[1,1,16,2,2048]{4,2,3,1,0:T(8,128)(2,1)S(1)} collective-permute-done((bf16[1,1,16,2,2048]{4,2,3,1,0:T(8,128)(2,1)S(1)}, bf16[1,1,16,2,2048]{4,2,3,1,0:T(8,128)(2,1)S(1)}, u32[]{:S(2)}, u32[]{:S(2)}) %collective-permute-start) | collective-permute-done | bytes 131104 | tf_op jit(solution)/shard_map/ppermute | solution.py:17
  77.0 4.1 %collective-permute-done.1 = bf16[1,1,16,2,2048]{4,2,3,1,0:T(8,128)(2,1)S(1)} collective-permute-done((bf16[1,1,16,2,2048]{4,2,3,1,0:T(8,128)(2,1)S(1)}, bf16[1,1,16,2,2048]{4,2,3,1,0:T(8,128)(2,1)S(1)}, u32[]{:S(2)}, u32[]{:S(2)}) %collective-permute-start.1) | collective-permute-done | bytes 131104 | tf_op jit(solution)/shard_map/ppermute | solution.py:19
  81.9 9.7 %all-gather.8.cloned.1.call-done = bf16[2048,512]{1,0:T(8,128)(2,1)} async-done(((bf16[512,512]{1,0:T(8,128)(2,1)}), bf16[2048,512]{1,0:T(8,128)(2,1)}) %all-gather.8.cloned.1.call-update) | async-done | bytes 2097168 | tf_op jit(solution)/shard_map/all_gather | solution.py:135
  91.6 2.1 %multiply_reduce_fusion = (f32[2,16]{1,0:T(2,128)S(1)}, f32[2,16,512]{2,1,0:T(8,128)S(1)}) fusion(bf16[2048,512]{1,0:T(8,128)(2,1)} %all-gather.8.cloned.1.call-done, f32[1,2,16,2,2048]{4,2,3,1,0:T(8,128)S(1)} %fusion.82), kind=kOutput, calls=%fused_computation.264 | convolution fusion | flops 67534816 | bytes 2687104 | tf_op jit(solution)/shard_map/frwj,jc->frwc/dot_general | solution.py:132
  93.8 5.4 %all_gather.22 = bf16[4,2,16,512]{3,2,1,0:T(8,128)(2,1)S(1)} all-gather(bf16[1,2,16,512]{3,2,1,0:T(8,128)(2,1)S(1)} %fusion.183), channel_id=1, replica_groups=mesh['parts'=2,'row'=4,'frame'=4] {'frame'}, dimensions={0}, use_global_device_ids=true | all-gather | bytes 163840 | tf_op jit(solution)/shard_map/all_gather | solution.py:139
  99.2 3.4 %collective-permute-start.2 = (bf16[4,2,16,512]{3,2,1,0:T(8,128)(2,1)S(1)}, bf16[4,2,16,512]{3,2,1,0:T(8,128)(2,1)S(1)}, u32[]{:S(2)}, u32[]{:S(2)}) collective-permute-start(bf16[4,2,16,512]{3,2,1,0:T(8,128)(2,1)S(1)} %all_gather.22), channel_id=1, source_target_pairs={{0,4},{4,8},{8,12},{1,5},{5,9},{9,13},{2,6},{6,10},{10,14},{3,7},{... | collective-permute-start | bytes 393224 | tf_op jit(solution)/shard_map/ppermute | solution.py:17
  102.6 1.3 collective-permute-start.3
  103.9 1.9 %collective-permute-done.2 = bf16[4,2,16,512]{3,2,1,0:T(8,128)(2,1)S(1)} collective-permute-done((bf16[4,2,16,512]{3,2,1,0:T(8,128)(2,1)S(1)}, bf16[4,2,16,512]{3,2,1,0:T(8,128)(2,1)S(1)}, u32[]{:S(2)}, u32[]{:S(2)}) %collective-permute-start.2) | collective-permute-done | bytes 131104 | tf_op jit(solution)/shard_map/ppermute | solution.py:17
  105.9 4.1 %collective-permute-done.3 = bf16[4,2,16,512]{3,2,1,0:T(8,128)(2,1)S(1)} collective-permute-done((bf16[4,2,16,512]{3,2,1,0:T(8,128)(2,1)S(1)}, bf16[4,2,16,512]{3,2,1,0:T(8,128)(2,1)S(1)}, u32[]{:S(2)}, u32[]{:S(2)}) %collective-permute-start.3) | collective-permute-done | bytes 131104 | tf_op jit(solution)/shard_map/ppermute | solution.py:19
  110.0 0.8 pad_slice_fusion.23
  110.9 1.0 copy-done.5
  115.5 5.9 %all_gather.23 = bf16[4,4,16,512]{3,2,1,0:T(8,128)(2,1)S(1)} all-gather(bf16[4,4,16,128]{3,2,1,0:T(8,128)(2,1)S(1)} %multiply_convert_fusion.1), channel_id=1, replica_groups=mesh['parts'=2,'row'=4,'frame'=4] {'frame'}, dimensions={3}, use_global_device_ids=true | all-gather | bytes 327680 | tf_op jit(solution)/shard_map/all_gather | solution.py:146
  124.5 6.3 %all_to_all.18 = bf16[4,2,16,128]{3,1,0,2:T(2,128)(2,1)S(1)} all-to-all(bf16[4,2,16,128]{3,1,0,2:T(2,128)(2,1)S(1)} %copy.36), channel_id=1, replica_groups=mesh['parts'=2,'row'=4,'frame'=4] {'frame'}, dimensions={2} | all-to-all | bytes 65536 | tf_op jit(solution)/shard_map/all_to_all | solution.py:150
  (70 shorter events, 10.5 us)
Async XLA Ops:
  6.5 4.0 %copy-start.1 = (bf16[128,512]{1,0:T(8,128)(2,1)S(1)}, bf16[128,512]{1,0:T(8,128)(2,1)}, u32[]{:S(2)}) copy-start(bf16[128,512]{1,0:T(8,128)(2,1)} %param.12) | copy-start | bytes 393220
  6.5 24.8 %copy-start.2 = (bf16[1,2,16,512]{3,2,1,0:T(8,128)(2,1)S(1)}, bf16[1,2,16,512]{3,2,1,0:T(8,128)(2,1)}, u32[]{:S(2)}) copy-start(bf16[1,2,16,512]{3,2,1,0:T(8,128)(2,1)} %param.10) | copy-start | bytes 98308
  6.5 24.8 %all-gather.4.cloned.1.call-start = ((), (), s32[]{:S(2)}) async-start(), calls=%async_computation.1 | async-start | bytes 1966080 | tf_op jit(solution)/shard_map/all_gather | solution.py:110
  7.3 60.1 %all-gather.6.cloned.1.call-start = ((), (), s32[]{:S(2)}) async-start(), calls=%async_computation.2 | async-start | bytes 5242880 | tf_op jit(solution)/shard_map/all_gather | solution.py:126
  9.7 81.8 %all-gather.8.cloned.1.call-start = ((), (), s32[]{:S(2)}) async-start(), calls=%async_computation.3 | async-start | bytes 2621440 | tf_op jit(solution)/shard_map/all_gather | solution.py:135
  19.1 37.7 %copy-start.3 = (f32[512]{0:T(512)S(1)}, f32[512]{0:T(512)}, u32[]{:S(2)}) copy-start(f32[512]{0:T(512)} %param.13) | copy-start | bytes 6148
  56.9 18.2 %copy-start = (f32[3,3,2,2048]{3,2,1,0:T(2,128)S(1)}, f32[3,3,2,2048]{3,2,1,0:T(2,128)}, u32[]{:S(2)}) copy-start(f32[3,3,2,2048]{3,2,1,0:T(2,128)} %param.15) | copy-start | bytes 442372
  70.5 6.5 %collective-permute-start = (bf16[1,1,16,2,2048]{4,2,3,1,0:T(8,128)(2,1)S(1)}, bf16[1,1,16,2,2048]{4,2,3,1,0:T(8,128)(2,1)S(1)}, u32[]{:S(2)}, u32[]{:S(2)}) collective-permute-start(bf16[1,1,16,2,2048]{4,2,3,1,0:T(8,128)(2,1)S(1)} %get-tuple-element.62), channel_id=1, source_target_pairs={{0,4},{4,8},{8,12},{1,5},{5,9},{9,13},{2,6},{6,10},{10,14},{3,7},{... | collective-permute-start | bytes 393224 | tf_op jit(solution)/shard_map/ppermute | solution.py:17
  73.9 7.3 %collective-permute-start.1 = (bf16[1,1,16,2,2048]{4,2,3,1,0:T(8,128)(2,1)S(1)}, bf16[1,1,16,2,2048]{4,2,3,1,0:T(8,128)(2,1)S(1)}, u32[]{:S(2)}, u32[]{:S(2)}) collective-permute-start(bf16[1,1,16,2,2048]{4,2,3,1,0:T(8,128)(2,1)S(1)} %get-tuple-element.63), channel_id=1, source_target_pairs={{4,0},{8,4},{12,8},{5,1},{9,5},{13,9},{6,2},{10,6},{14,10},{7,3},{... | collective-permute-start | bytes 393224 | tf_op jit(solution)/shard_map/ppermute | solution.py:19
  75.2 18.5 %copy-start.4 = (f32[512]{0:T(512)S(1)}, f32[512]{0:T(512)}, u32[]{:S(2)}) copy-start(f32[512]{0:T(512)} %param.17) | copy-start | bytes 6148
  99.2 6.6 %collective-permute-start.2 = (bf16[4,2,16,512]{3,2,1,0:T(8,128)(2,1)S(1)}, bf16[4,2,16,512]{3,2,1,0:T(8,128)(2,1)S(1)}, u32[]{:S(2)}, u32[]{:S(2)}) collective-permute-start(bf16[4,2,16,512]{3,2,1,0:T(8,128)(2,1)S(1)} %all_gather.22), channel_id=1, source_target_pairs={{0,4},{4,8},{8,12},{1,5},{5,9},{9,13},{2,6},{6,10},{10,14},{3,7},{... | collective-permute-start | bytes 393224 | tf_op jit(solution)/shard_map/ppermute | solution.py:17
  102.6 7.4 %collective-permute-start.3 = (bf16[4,2,16,512]{3,2,1,0:T(8,128)(2,1)S(1)}, bf16[4,2,16,512]{3,2,1,0:T(8,128)(2,1)S(1)}, u32[]{:S(2)}, u32[]{:S(2)}) collective-permute-start(bf16[4,2,16,512]{3,2,1,0:T(8,128)(2,1)S(1)} %all_gather.22), channel_id=1, source_target_pairs={{4,0},{8,4},{12,8},{5,1},{9,5},{13,9},{6,2},{10,6},{14,10},{7,3},{... | collective-permute-start | bytes 393224 | tf_op jit(solution)/shard_map/ppermute | solution.py:19
  110.0 2.0 %copy-start.5 = (bf16[3,3,3,128,512]{4,3,2,1,0:T(8,128)(2,1)S(1)}, bf16[3,3,3,128,512]{4,3,2,1,0:T(8,128)(2,1)}, u32[]{:S(2)}) copy-start(bf16[3,3,3,128,512]{4,3,2,1,0:T(8,128)(2,1)} %param.18) | copy-start | bytes 10616836
  115.0 6.9 %copy-start.6 = (bf16[3,3,3,128,512]{4,3,2,1,0:T(8,128)(2,1)S(1)}, bf16[3,3,3,128,512]{4,3,2,1,0:T(8,128)(2,1)}, u32[]{:S(2)}) copy-start(bf16[3,3,3,128,512]{4,3,2,1,0:T(8,128)(2,1)} %param.19) | copy-start | bytes 10616836
Sparse Core Ops, SparseCore 0:
  8.9 22.3 all-gather.3
  32.9 34.4 all-gather.5
  69.0 22.5 all-gather.7
where the time goes:
time: 138 us
  blocking collectives  47.6 us (34%)
  waiting for transfers between devices  45.7 us (33%)
  matrix products  13.8 us (10%)
  between operations  13.6 us (10%)
  starting transfers between devices  9.45 us (7%)
  local copies, waits for them, and re-layouts  6.56 us (5%)
    psum x1, blocking collectives, attend(): lax.psum(state.astype(jnp.bfloat16), 'row').astype(jnp.float32)  21.3 us
    all_gather x1, waiting for transfers between devices, local(): lax.all_gather(qkv_weight, 'frame', axis=1, tiled=True)  12.2 us
    all_gather x1, waiting for transfers between devices, local(): lax.all_gather(in_weight, 'frame', axis=2, tiled=True)  10.4 us
    all_gather x1, waiting for transfers between devices, local(): lax.all_gather(down_weight, 'frame', axis=0, tiled=True)  9.71 us
    all_gather x1, blocking collectives, local(): lax.all_gather(out_weight, 'frame', axis=0, tiled=True)  8.62 us
    ppermute x2, waiting for transfers between devices, padded_2(): lax.ppermute(head, axis, [((i + 1) % count, i) for i in range(ends)])  8.23 us
    ppermute x2, starting transfers between devices, padded_2(): lax.ppermute(tail, axis, [(i, (i + 1) % count) for i in range(ends)])  6.78 us
    all_to_all x1, blocking collectives, local(): lax.all_to_all(final, 'frame', split_axis=2, concat_axis=3, tiled=True)  6.3 us
  transfers between devices with their start and end apart: 7, of which 7 were waited for; matrix products, arithmetic and copies ran while one was open for 8% of the time, Pallas kernels for 0%

commit v1 on v0

--- a/solution.py
+++ b/solution.py
@@ -150,7 +150,146 @@
     return lax.all_to_all(final, "frame", split_axis=2, concat_axis=3, tiled=True)
 
 
+def swap(cells, mask):
+    count = lax.axis_size("frame")
+    return lax.ppermute(cells, "frame", [(i, i ^ mask) for i in range(count)])
+
+
+def in_order(pieces, place, dim):
+    step = 1
+    while step < len(pieces):
+        flip = (place & step) != 0
+        pieces = [
+            jnp.where(flip, pieces[i ^ step], pieces[i]) for i in range(len(pieces))
+        ]
+        step *= 2
+    return jnp.concatenate(pieces, axis=dim)
+
+
+def gathered_by_mask(cells):
+    count = lax.axis_size("frame")
+    pieces = [None] * count
+    pieces[0] = cells
+    masks = list(range(3, count, 2))
+    for mask in masks:
+        pieces[mask] = swap(cells, mask)
+    both = swap(jnp.stack([pieces[m] for m in [0] + masks]), 1)
+    for i, mask in enumerate([0] + masks):
+        pieces[mask ^ 1] = both[i]
+    return pieces
+
+
+def silu(values):
+    return values / (1.0 + jnp.exp(-values))
+
+
+def by_frames(
+    latent,
+    qkv_weight,
+    out_weight,
+    attn_gain,
+    in_weight,
+    depth_weight,
+    down_weight,
+    mlp_gain,
+    conv_first,
+    conv_second,
+):
+    count = lax.axis_size("frame")
+    level, place = (lax.axis_index("row"), lax.axis_index("frame"))
+    rows, columns, width = latent.shape[1:]
+    height = rows * count
+    tokens = height * columns
+    share = qkv_weight.shape[1]
+    own = latent.reshape(rows * columns, width)
+    pieces = [None] * count
+    masks = [1] + list(range(2, count, 2))
+    for mask in masks:
+        pairs = [
+            (z * count + f, f * count + (z ^ mask)) for z in range(count) for f in range(count)
+        ]
+        pieces[mask] = lax.ppermute(own, ("row", "frame"), pairs)
+    both = swap(jnp.stack([pieces[m] for m in masks]), 1)
+    for i, mask in enumerate(masks):
+        pieces[mask ^ 1] = both[i]
+    cells = in_order(pieces, place, 0)
+    out_pieces = gathered_by_mask(out_weight)
+    packed = jnp.einsum(
+        "tc,kjc->tkj", cells, qkv_weight, preferred_element_type=jnp.float32
+    ).astype(jnp.bfloat16)
+    query = jnp.maximum(packed[:, 0], 0)
+    keys = jnp.maximum(packed[:, 1], 0)
+    values = packed[:, 2]
+    head_of = lax.iota(jnp.int32, share) // HEAD
+    same = head_of[:, None] == head_of[None, :]
+    state = jnp.einsum("td,te->de", keys, values, preferred_element_type=jnp.float32) / tokens
+    key_mean = jnp.sum(keys.astype(jnp.float32), axis=0) / tokens
+    table = jnp.concatenate(
+        [jnp.where(same, state, 0.0), jnp.where(same, key_mean[:, None], 0.0)], axis=1
+    )
+    both = jnp.einsum("td,de->te", query.astype(jnp.float32), table, precision=lax.Precision.HIGHEST)
+    mixed = (both[:, :share] / jnp.maximum(both[:, share:], 1.0)).astype(jnp.bfloat16)
+    mixed_pieces = gathered_by_mask(mixed)
+    attn_out = sum(
+        jnp.dot(a, b, preferred_element_type=jnp.float32)
+        for a, b in zip(mixed_pieces, out_pieces)
+    )
+    first = (cells.astype(jnp.float32) + norm_rows(attn_out, attn_gain)).astype(jnp.bfloat16)
+    units = in_weight.shape[2]
+    inner = silu(
+        jnp.einsum("tc,ckj->tkj", first, in_weight, preferred_element_type=jnp.float32)
+    ).astype(jnp.bfloat16)
+    taps = lax.dynamic_slice_in_dim(depth_weight, place * units, units, 3)
+    padded = jnp.pad(
+        inner.reshape(height, columns, 2, units), ((1, 1), (1, 1), (0, 0), (0, 0))
+    ).astype(jnp.float32)
+    spread = sum(
+        padded[i : i + height, j : j + columns] * taps[i, j] for i in range(3) for j in range(3)
+    )
+    gated = (spread[:, :, 0] * silu(spread[:, :, 1])).astype(jnp.bfloat16)
+    partial = jnp.einsum(
+        "rwj,jc->rwc", gated, down_weight, preferred_element_type=jnp.float32
+    )
+    half = columns // 2
+    mine = (place ^ (place >> 1)) & 1
+    kept = lax.dynamic_slice_in_dim(partial, mine * half, half, 1)
+    sent = lax.dynamic_slice_in_dim(partial, (1 - mine) * half, half, 1)
+    total = kept + swap(sent, 1)
+    far = [swap(total.astype(jnp.bfloat16), mask).astype(jnp.float32) for mask in range(3, count, 2)]
+    mlp_out = total + sum(far)
+    first_half = lax.dynamic_slice_in_dim(
+        first.reshape(height, columns, width), mine * half, half, 1
+    )
+    second = (first_half.astype(jnp.float32) + norm_rows(mlp_out, mlp_gain)).astype(jnp.bfloat16)
+    framed = jnp.pad(second, ((2, 2), (0, 0), (0, 0)))
+    parts = []
+    for mask in range(count):
+        piece = lax.dynamic_slice_in_dim(framed, (level ^ mask) * rows, rows + 4, 0)
+        if mask:
+            piece = lax.ppermute(piece, "row", [(i, i ^ mask) for i in range(count)])
+        parts.append(piece[None])
+    window = in_order(parts, level, 0)
+    other = swap(window, 1)
+    lead = jnp.where(mine == 0, window, other)
+    tail = jnp.where(mine == 0, other, window)
+    window = jnp.concatenate([lead, tail], axis=2)
+    activated = silu(conv_tile(window, conv_first))
+    global_row = level * rows - 1 + lax.iota(jnp.int32, rows + 2)
+    inside = ((global_row >= 0) & (global_row < height)).astype(jnp.float32)
+    hidden = (activated * inside[None, :, None, None]).astype(jnp.bfloat16)
+    joined = in_order(gathered_by_mask(hidden), place, 3)
+    result = conv_tile(joined, conv_second)
+    own_part = lax.dynamic_slice_in_dim(window[:, 2 : 2 + rows], place * share, share, 3)
+    final = (own_part.astype(jnp.float32) + result).astype(jnp.bfloat16)
+    strip = columns // count
+    def strip_of(mask):
+        return lax.dynamic_slice_in_dim(final, (place ^ mask) * strip, strip, 2)
+    outs = [strip_of(0)] + [swap(strip_of(mask), mask) for mask in range(1, count)]
+    return in_order(outs, place, 3)
+
+
 def solution(mesh):
+    body = by_frames if mesh.shape["row"] == mesh.shape["frame"] else local
     in_specs = (
         P(("parts", "frame"), "row", None, None),
         P(None, "frame", None),
@@ -164,4 +303,4 @@
         P(None, None, None, "frame", None),
     )
     out_specs = P("parts", "row", "frame", None)
-    return jax.shard_map(local, mesh=mesh, in_specs=in_specs, out_specs=out_specs, check_vma=False)
+    return jax.shard_map(body, mesh=mesh, in_specs=in_specs, out_specs=out_specs, check_vma=False)

time: 138 us -> 56.3 us (0.41)
  blocking collectives: 47.6 us -> 0 us
  waiting for transfers between devices: 45.7 us -> 19.3 us
  between operations: 13.6 us -> 0.49 us
  starting transfers between devices: 9.45 us -> 19.2 us
  matrix products: 13.8 us -> 9.67 us
  local copies, waits for them, and re-layouts: 6.56 us -> 4.11 us
  other arithmetic: 1.23 us -> 3.21 us
    all_gather x3 -> x0, waiting for transfers between devices: 32.3 us -> none  [the longest x1 12.2 us: local(): lax.all_gather(qkv_weight, 'frame', axis=1, tiled=True)]
    psum x1 -> x0, blocking collectives: 21.3 us -> none  [attend(): lax.psum(state.astype(jnp.bfloat16), 'row').astype(jnp.float32)]
    all_gather x3 -> x0, blocking collectives: 20 us -> none  [the longest x1 8.62 us: local(): lax.all_gather(out_weight, 'frame', axis=0, tiled=True)]
    ppermute x4 -> x18, starting transfers between devices: 9.37 us -> 19.2 us  [the longest x13 9.78 us: swap(): return lax.ppermute(cells, 'frame', [(i, i ^ mask) for i in range(count)])]
    ppermute x4 -> x18, waiting for transfers between devices: 11.9 us -> 19.3 us  [the longest x13 14.5 us: swap(): return lax.ppermute(cells, 'frame', [(i, i ^ mask) for i in range(count)])]
    all_to_all x1 -> x0, blocking collectives: 6.3 us -> none  [local(): lax.all_to_all(final, 'frame', split_axis=2, concat_axis=3, tiled=True)]
    dot_general x7 -> x9, matrix products: 8.12 us -> 3.93 us  [the longest x4 1.66 us: by_frames(): jnp.dot(a, b, preferred_element_type=jnp.float32)]
    unnamed x19 -> x12, local copies, waits for them, and re-layouts: 3.87 us -> 1.79 us
  transfers between devices with their start and end apart: 7 -> 18, of which waited for: 7 -> 12; matrix products, arithmetic and copies ran while one was open for 8% -> 9% of each run, Pallas kernels for 0% -> 0%
where the time goes in v1:
time: 56.3 us; the launch traced here: 56 us
  waiting for transfers between devices  19.3 us (34%)
  starting transfers between devices  19.2 us (34%)
  matrix products  9.67 us (17%)
  local copies, waits for them, and re-layouts  4.11 us (7%)
  other arithmetic  3.21 us (6%)
    ppermute x13, waiting for transfers between devices, swap(): return lax.ppermute(cells, 'frame', [(i, i ^ mask) for i in range(count)])  14.5 us
    ppermute x13, starting transfers between devices, swap(): return lax.ppermute(cells, 'frame', [(i, i ^ mask) for i in range(count)])  9.78 us
    dot_general x18, matrix products, conv_tile(): jnp.einsum('nci,coi->no', stacked.reshape(-1, 3, width), kernel[shift_tim...  5.73 us
    ppermute x2, starting transfers between devices, by_frames(): pieces[mask] = lax.ppermute(own, ('row', 'frame'), pairs)  4.94 us
    ppermute x3, waiting for transfers between devices, by_frames(): piece = lax.ppermute(piece, 'row', [(i, i ^ mask) for i in range(count)])  4.81 us
    ppermute x3, starting transfers between devices, by_frames(): piece = lax.ppermute(piece, 'row', [(i, i ^ mask) for i in range(count)])  4.45 us
    unnamed x12, local copies, waits for them, and re-layouts  1.79 us
    dot_general x4, matrix products, by_frames(): jnp.dot(a, b, preferred_element_type=jnp.float32)  1.66 us
  transfers between devices with their start and end apart: 18, of which 12 were waited for; matrix products, arithmetic and copies ran while one was open for 9% of the time, Pallas kernels for 0%

profile of v1, /device:TPU:0, one launch (start us, length us, event | category | flops | bytes accessed | tf_op | source)
XLA Modules:
  0.0 56.0 jit_solution(2055122614575919462)
XLA Ops:
  0.5 4.5 %collective-permute-start.1 = (bf16[32,512]{1,0:T(8,128)(2,1)}, bf16[32,512]{1,0:T(8,128)(2,1)S(1)}, u32[]{:S(2)}, u32[]{:S(2)}) collective-permute-start(bf16[32,512]{1,0:T(8,128)(2,1)} %bitcast.390), channel_id=1, source_target_pairs={{0,2},{1,6},{2,10},{3,14},{4,3},{5,7},{6,11},{7,15},{8,0},{9,4},{1... | collective-permute-start | bytes 98312 | tf_op jit(solution)/shard_map/ppermute | solution.py:211
  4.9 1.8 %collective-permute-start.5 = (bf16[128,512]{1,0:T(8,128)(2,1)}, bf16[128,512]{1,0:T(8,128)(2,1)S(1)}, u32[]{:S(2)}, u32[]{:S(2)}) collective-permute-start(bf16[128,512]{1,0:T(8,128)(2,1)} %param.12), channel_id=1, source_target_pairs={{0,3},{1,2},{2,1},{3,0},{4,7},{5,6},{6,5},{7,4},{8,11},{9,10},{10,... | collective-permute-start | bytes 393224 | tf_op jit(solution)/shard_map/ppermute | solution.py:155
  7.6 1.2 %collective-permute-start.2 = (bf16[2,32,512]{2,1,0:T(8,128)(2,1)S(1)}, bf16[2,32,512]{2,1,0:T(8,128)(2,1)S(1)}, u32[]{:S(2)}, u32[]{:S(2)}) collective-permute-start(bf16[2,32,512]{2,1,0:T(8,128)(2,1)S(1)} %pad_maximum_fusion.6), channel_id=1, source_target_pairs={{0,1},{1,0},{2,3},{3,2},{4,5},{5,4},{6,7},{7,6},{8,9},{9,8},{10,11... | collective-permute-start | bytes 196616 | tf_op jit(solution)/shard_map/ppermute | solution.py:155
  8.8 0.9 %collective-permute-done.2 = bf16[2,32,512]{2,1,0:T(8,128)(2,1)S(1)} collective-permute-done((bf16[2,32,512]{2,1,0:T(8,128)(2,1)S(1)}, bf16[2,32,512]{2,1,0:T(8,128)(2,1)S(1)}, u32[]{:S(2)}, u32[]{:S(2)}) %collective-permute-start.2) | collective-permute-done | bytes 65568 | tf_op jit(solution)/shard_map/ppermute | solution.py:155
  9.7 1.3 %convolution_convert_fusion = bf16[128,3,128]{2,0,1:T(8,128)(2,1)S(1)} fusion(bf16[3,128,512]{2,1,0:T(8,128)(2,1)} %param.11, bf16[32,512]{1,0:T(8,128)(2,1)S(1)} %get-tuple-element.83, bf16[32,512]{1,0:T(8,128)(2,1)S(1)} %get-tuple-element.82, bf16[32,512]{1,0:T(8,128)(2,1)S(1)} %get-tuple-element.81, bf16[32,512]{1,0:T(8,128)(2,1)S(1)} %get-tuple-element.80), kind=kOutput, calls=%fused_computation.51 | convolution fusion | flops 50905088 | bytes 622592 | tf_op jit(solution)/shard_map/tc,kjc->tkj/dot_general | solution.py:217
  11.6 1.9 %collective-permute-start.3 = (bf16[128,128]{1,0:T(8,128)(2,1)S(1)}, bf16[128,128]{1,0:T(8,128)(2,1)S(1)}, u32[]{:S(2)}, u32[]{:S(2)}) collective-permute-start(bf16[128,128]{1,0:T(8,128)(2,1)S(1)} %fusion.172), channel_id=1, source_target_pairs={{0,3},{1,2},{2,1},{3,0},{4,7},{5,6},{6,5},{7,4},{8,11},{9,10},{10,... | collective-permute-start | bytes 98312 | tf_op jit(solution)/shard_map/ppermute | solution.py:155
  13.5 1.1 %fusion.212 = f32[128,512]{1,0:T(8,128)S(1)} fusion(bf16[128,128]{1,0:T(8,128)(2,1)S(1)} %fusion.172, bf16[128,512]{1,0:T(8,128)(2,1)} %param.12), kind=kOutput, calls=%fused_computation.391 | convolution fusion | flops 16777216 | bytes 425984 | tf_op jit(solution)/shard_map/dot_general | solution.py:234
  14.6 0.9 %pad_maximum_fusion.1 = bf16[2,128,512]{2,1,0:T(8,128)(2,1)S(1)} fusion(bf16[1,128,512]{2,1,0:T(8,128)(2,1)S(1)} %bitcast.327, bf16[1,128,512]{2,1,0:T(8,128)(2,1)} %bitcast.326), kind=kLoop, calls=%fused_computation.253 | loop fusion | flops 131072 | bytes 524288 | tf_op jit(solution)/shard_map/stack | solution.py:176
  19.8 1.1 %collective-permute-done.7 = f32[8,8,512]{2,1,0:T(8,128)S(1)} collective-permute-done((f32[8,8,512]{2,1,0:T(8,128)S(1)}, f32[8,8,512]{2,1,0:T(8,128)S(1)}, u32[]{:S(2)}, u32[]{:S(2)}) %collective-permute-start.7) | collective-permute-done | bytes 131104 | tf_op jit(solution)/shard_map/ppermute | solution.py:155
  20.9 1.0 %collective-permute-start.8 = (bf16[8,8,512]{2,1,0:T(8,128)(2,1)S(1)}, bf16[8,8,512]{2,1,0:T(8,128)(2,1)S(1)}, u32[]{:S(2)}, u32[]{:S(2)}) collective-permute-start(bf16[8,8,512]{2,1,0:T(8,128)(2,1)S(1)} %get-tuple-element.5), channel_id=1, source_target_pairs={{0,3},{1,2},{2,1},{3,0},{4,7},{5,6},{6,5},{7,4},{8,11},{9,10},{10,... | collective-permute-start | bytes 196616 | tf_op jit(solution)/shard_map/ppermute | solution.py:155
  21.9 3.2 %collective-permute-done.8 = bf16[8,8,512]{2,1,0:T(8,128)(2,1)S(1)} collective-permute-done((bf16[8,8,512]{2,1,0:T(8,128)(2,1)S(1)}, bf16[8,8,512]{2,1,0:T(8,128)(2,1)S(1)}, u32[]{:S(2)}, u32[]{:S(2)}) %collective-permute-start.8) | collective-permute-done | bytes 65568 | tf_op jit(solution)/shard_map/ppermute | solution.py:155
  25.4 1.1 %collective-permute-start.10 = (bf16[6,8,512]{2,1,0:T(8,128)(2,1)S(1)}, bf16[6,8,512]{2,1,0:T(8,128)(2,1)S(1)}, u32[]{:S(2)}, u32[]{:S(2)}) collective-permute-start(bf16[6,8,512]{2,1,0:T(8,128)(2,1)S(1)} %get-tuple-element.85), channel_id=1, source_target_pairs={{0,8},{4,12},{8,0},{12,4},{1,9},{5,13},{9,1},{13,5},{2,10},{6,14},... | collective-permute-start | bytes 147464 | tf_op jit(solution)/shard_map/ppermute | solution.py:269
  26.5 2.3 %collective-permute-start.11 = (bf16[6,8,512]{2,1,0:T(8,128)(2,1)S(1)}, bf16[6,8,512]{2,1,0:T(8,128)(2,1)S(1)}, u32[]{:S(2)}, u32[]{:S(2)}) collective-permute-start(bf16[6,8,512]{2,1,0:T(8,128)(2,1)S(1)} %get-tuple-element.84), channel_id=1, source_target_pairs={{0,4},{4,0},{8,12},{12,8},{1,5},{5,1},{9,13},{13,9},{2,6},{6,2},{1... | collective-permute-start | bytes 147464 | tf_op jit(solution)/shard_map/ppermute | solution.py:269
  28.7 1.1 %collective-permute-start.9 = (bf16[6,8,512]{2,1,0:T(8,128)(2,1)S(1)}, bf16[6,8,512]{2,1,0:T(8,128)(2,1)S(1)}, u32[]{:S(2)}, u32[]{:S(2)}) collective-permute-start(bf16[6,8,512]{2,1,0:T(8,128)(2,1)S(1)} %get-tuple-element.86), channel_id=1, source_target_pairs={{0,12},{4,8},{8,4},{12,0},{1,13},{5,9},{9,5},{13,1},{2,14},{6,10},... | collective-permute-start | bytes 147464 | tf_op jit(solution)/shard_map/ppermute | solution.py:269
  29.8 1.6 %collective-permute-done.10 = bf16[6,8,512]{2,1,0:T(8,128)(2,1)S(1)} collective-permute-done((bf16[6,8,512]{2,1,0:T(8,128)(2,1)S(1)}, bf16[6,8,512]{2,1,0:T(8,128)(2,1)S(1)}, u32[]{:S(2)}, u32[]{:S(2)}) %collective-permute-start.10) | collective-permute-done | bytes 49184 | tf_op jit(solution)/shard_map/ppermute | solution.py:269
  31.6 3.0 %collective-permute-done.9 = bf16[6,8,512]{2,1,0:T(8,128)(2,1)S(1)} collective-permute-done((bf16[6,8,512]{2,1,0:T(8,128)(2,1)S(1)}, bf16[6,8,512]{2,1,0:T(8,128)(2,1)S(1)}, u32[]{:S(2)}, u32[]{:S(2)}) %collective-permute-start.9) | collective-permute-done | bytes 49184 | tf_op jit(solution)/shard_map/ppermute | solution.py:269
  34.8 1.4 %collective-permute-done.12 = bf16[4,6,8,512]{3,2,1,0:T(8,128)(2,1)S(1)} collective-permute-done((bf16[4,6,8,512]{3,2,1,0:T(8,128)(2,1)S(1)}, bf16[4,6,8,512]{3,2,1,0:T(8,128)(2,1)S(1)}, u32[]{:S(2)}, u32[]{:S(2)}) %collective-permute-start.12) | collective-permute-done | bytes 196640 | tf_op jit(solution)/shard_map/ppermute | solution.py:155
  37.3 1.1 %copy-done.3 = bf16[3,3,3,128,512]{4,3,2,1,0:T(8,128)(2,1)S(1)} copy-done((bf16[3,3,3,128,512]{4,3,2,1,0:T(8,128)(2,1)S(1)}, bf16[3,3,3,128,512]{4,3,2,1,0:T(8,128)(2,1)}, u32[]{:S(2)}) %copy-start.3) | copy-done | bytes 3538968
  42.6 3.4 %collective-permute-done.13 = bf16[4,4,16,128]{3,2,1,0:T(8,128)(2,1)S(1)} collective-permute-done((bf16[4,4,16,128]{3,2,1,0:T(8,128)(2,1)S(1)}, bf16[4,4,16,128]{3,2,1,0:T(8,128)(2,1)S(1)}, u32[]{:S(2)}, u32[]{:S(2)}) %collective-permute-start.13) | collective-permute-done | bytes 65568 | tf_op jit(solution)/shard_map/ppermute | solution.py:155
  46.2 1.2 %collective-permute-done.14 = bf16[2,4,4,16,128]{4,3,2,1,0:T(8,128)(2,1)S(1)} collective-permute-done((bf16[2,4,4,16,128]{4,3,2,1,0:T(8,128)(2,1)S(1)}, bf16[2,4,4,16,128]{4,3,2,1,0:T(8,128)(2,1)S(1)}, u32[]{:S(2)}, u32[]{:S(2)}) %collective-permute-start.14) | collective-permute-done | bytes 131104 | tf_op jit(solution)/shard_map/ppermute | solution.py:155
  50.8 0.9 %collective-permute-start.15 = (bf16[4,2,4,128]{3,2,1,0:T(4,128)(2,1)S(1)}, bf16[4,2,4,128]{3,2,1,0:T(4,128)(2,1)S(1)}, u32[]{:S(2)}, u32[]{:S(2)}) collective-permute-start(bf16[4,2,4,128]{3,2,1,0:T(4,128)(2,1)S(1)} %get-tuple-element.93), channel_id=1, source_target_pairs={{0,3},{1,2},{2,1},{3,0},{4,7},{5,6},{6,5},{7,4},{8,11},{9,10},{10,... | collective-permute-start | bytes 24584 | tf_op jit(solution)/shard_map/ppermute | solution.py:155
  51.7 1.2 %collective-permute-start.16 = (bf16[4,2,4,128]{3,2,1,0:T(4,128)(2,1)S(1)}, bf16[4,2,4,128]{3,2,1,0:T(4,128)(2,1)S(1)}, u32[]{:S(2)}, u32[]{:S(2)}) collective-permute-start(bf16[4,2,4,128]{3,2,1,0:T(4,128)(2,1)S(1)} %get-tuple-element.92), channel_id=1, source_target_pairs={{0,2},{1,3},{2,0},{3,1},{4,6},{5,7},{6,4},{7,5},{8,10},{9,11},{10,... | collective-permute-start | bytes 24584 | tf_op jit(solution)/shard_map/ppermute | solution.py:155
  52.8 1.1 %collective-permute-done.15 = bf16[4,2,4,128]{3,2,1,0:T(4,128)(2,1)S(1)} collective-permute-done((bf16[4,2,4,128]{3,2,1,0:T(4,128)(2,1)S(1)}, bf16[4,2,4,128]{3,2,1,0:T(4,128)(2,1)S(1)}, u32[]{:S(2)}, u32[]{:S(2)}) %collective-permute-start.15) | collective-permute-done | bytes 8224 | tf_op jit(solution)/shard_map/ppermute | solution.py:155
  53.9 1.4 %collective-permute-done.16 = bf16[4,2,4,128]{3,2,1,0:T(4,128)(2,1)S(1)} collective-permute-done((bf16[4,2,4,128]{3,2,1,0:T(4,128)(2,1)S(1)}, bf16[4,2,4,128]{3,2,1,0:T(4,128)(2,1)S(1)}, u32[]{:S(2)}, u32[]{:S(2)}) %collective-permute-start.16) | collective-permute-done | bytes 8224 | tf_op jit(solution)/shard_map/ppermute | solution.py:155
  (92 shorter events, 16.0 us)
Async XLA Ops:
  0.0 17.8 %copy-start = (bf16[512,2,512]{2,1,0:T(2,128)(2,1)S(1)}, bf16[512,2,512]{2,1,0:T(2,128)(2,1)}, u32[]{:S(2)}) copy-start(bf16[512,2,512]{2,1,0:T(2,128)(2,1)} %param.14) | copy-start | bytes 3145732
  0.0 17.7 %copy-start.1 = (f32[512]{0:T(512)S(1)}, f32[512]{0:T(512)}, u32[]{:S(2)}) copy-start(f32[512]{0:T(512)} %param.13) | copy-start | bytes 6148
  0.0 7.5 %collective-permute-start = (bf16[32,512]{1,0:T(8,128)(2,1)}, bf16[32,512]{1,0:T(8,128)(2,1)S(1)}, u32[]{:S(2)}, u32[]{:S(2)}) collective-permute-start(bf16[32,512]{1,0:T(8,128)(2,1)} %bitcast.389), channel_id=1, source_target_pairs={{0,1},{1,5},{2,9},{3,13},{4,0},{5,4},{6,8},{7,12},{8,3},{9,7},{10,... | collective-permute-start | bytes 98312 | tf_op jit(solution)/shard_map/ppermute | solution.py:211
  0.5 7.1 %collective-permute-start.1 = (bf16[32,512]{1,0:T(8,128)(2,1)}, bf16[32,512]{1,0:T(8,128)(2,1)S(1)}, u32[]{:S(2)}, u32[]{:S(2)}) collective-permute-start(bf16[32,512]{1,0:T(8,128)(2,1)} %bitcast.390), channel_id=1, source_target_pairs={{0,2},{1,6},{2,10},{3,14},{4,3},{5,7},{6,11},{7,15},{8,0},{9,4},{1... | collective-permute-start | bytes 98312 | tf_op jit(solution)/shard_map/ppermute | solution.py:211
  4.9 9.6 %collective-permute-start.5 = (bf16[128,512]{1,0:T(8,128)(2,1)}, bf16[128,512]{1,0:T(8,128)(2,1)S(1)}, u32[]{:S(2)}, u32[]{:S(2)}) collective-permute-start(bf16[128,512]{1,0:T(8,128)(2,1)} %param.12), channel_id=1, source_target_pairs={{0,3},{1,2},{2,1},{3,0},{4,7},{5,6},{6,5},{7,4},{8,11},{9,10},{10,... | collective-permute-start | bytes 393224 | tf_op jit(solution)/shard_map/ppermute | solution.py:155
  7.6 2.1 %collective-permute-start.2 = (bf16[2,32,512]{2,1,0:T(8,128)(2,1)S(1)}, bf16[2,32,512]{2,1,0:T(8,128)(2,1)S(1)}, u32[]{:S(2)}, u32[]{:S(2)}) collective-permute-start(bf16[2,32,512]{2,1,0:T(8,128)(2,1)S(1)} %pad_maximum_fusion.6), channel_id=1, source_target_pairs={{0,1},{1,0},{2,3},{3,2},{4,5},{5,4},{6,7},{7,6},{8,9},{9,8},{10,11... | collective-permute-start | bytes 196616 | tf_op jit(solution)/shard_map/ppermute | solution.py:155
  11.6 4.1 %collective-permute-start.3 = (bf16[128,128]{1,0:T(8,128)(2,1)S(1)}, bf16[128,128]{1,0:T(8,128)(2,1)S(1)}, u32[]{:S(2)}, u32[]{:S(2)}) collective-permute-start(bf16[128,128]{1,0:T(8,128)(2,1)S(1)} %fusion.172), channel_id=1, source_target_pairs={{0,3},{1,2},{2,1},{3,0},{4,7},{5,6},{6,5},{7,4},{8,11},{9,10},{10,... | collective-permute-start | bytes 98312 | tf_op jit(solution)/shard_map/ppermute | solution.py:155
  15.5 1.7 %collective-permute-start.6 = (bf16[2,128,512]{2,1,0:T(8,128)(2,1)S(1)}, bf16[2,128,512]{2,1,0:T(8,128)(2,1)S(1)}, u32[]{:S(2)}, u32[]{:S(2)}) collective-permute-start(bf16[2,128,512]{2,1,0:T(8,128)(2,1)S(1)} %pad_maximum_fusion.1), channel_id=1, source_target_pairs={{0,1},{1,0},{2,3},{3,2},{4,5},{5,4},{6,7},{7,6},{8,9},{9,8},{10,11... | collective-permute-start | bytes 786440 | tf_op jit(solution)/shard_map/ppermute | solution.py:155
  15.8 1.5 %collective-permute-start.4 = (bf16[2,128,128]{2,1,0:T(8,128)(2,1)S(1)}, bf16[2,128,128]{2,1,0:T(8,128)(2,1)S(1)}, u32[]{:S(2)}, u32[]{:S(2)}) collective-permute-start(bf16[2,128,128]{2,1,0:T(8,128)(2,1)S(1)} %pad_maximum_fusion.7), channel_id=1, source_target_pairs={{0,1},{1,0},{2,3},{3,2},{4,5},{5,4},{6,7},{7,6},{8,9},{9,8},{10,11... | collective-permute-start | bytes 196616 | tf_op jit(solution)/shard_map/ppermute | solution.py:155
  18.2 1.0 %copy-start.5 = (bf16[512,512]{1,0:T(8,128)(2,1)S(1)}, bf16[512,512]{1,0:T(8,128)(2,1)}, u32[]{:S(2)}) copy-start(bf16[512,512]{1,0:T(8,128)(2,1)} %param.16) | copy-start | bytes 1572868
  18.3 6.9 %copy-start.2 = (f32[512]{0:T(512)S(1)}, f32[512]{0:T(512)}, u32[]{:S(2)}) copy-start(f32[512]{0:T(512)} %param.17) | copy-start | bytes 6148
  19.5 1.4 %collective-permute-start.7 = (f32[8,8,512]{2,1,0:T(8,128)S(1)}, f32[8,8,512]{2,1,0:T(8,128)S(1)}, u32[]{:S(2)}, u32[]{:S(2)}) collective-permute-start(f32[8,8,512]{2,1,0:T(8,128)S(1)} %constant_dynamic-slice_fusion.11), channel_id=1, source_target_pairs={{0,1},{1,0},{2,3},{3,2},{4,5},{5,4},{6,7},{7,6},{8,9},{9,8},{10,11... | collective-permute-start | bytes 393224 | tf_op jit(solution)/shard_map/ppermute | solution.py:155
  20.9 4.2 %collective-permute-start.8 = (bf16[8,8,512]{2,1,0:T(8,128)(2,1)S(1)}, bf16[8,8,512]{2,1,0:T(8,128)(2,1)S(1)}, u32[]{:S(2)}, u32[]{:S(2)}) collective-permute-start(bf16[8,8,512]{2,1,0:T(8,128)(2,1)S(1)} %get-tuple-element.5), channel_id=1, source_target_pairs={{0,3},{1,2},{2,1},{3,0},{4,7},{5,6},{6,5},{7,4},{8,11},{9,10},{10,... | collective-permute-start | bytes 196616 | tf_op jit(solution)/shard_map/ppermute | solution.py:155
  25.4 6.0 %collective-permute-start.10 = (bf16[6,8,512]{2,1,0:T(8,128)(2,1)S(1)}, bf16[6,8,512]{2,1,0:T(8,128)(2,1)S(1)}, u32[]{:S(2)}, u32[]{:S(2)}) collective-permute-start(bf16[6,8,512]{2,1,0:T(8,128)(2,1)S(1)} %get-tuple-element.85), channel_id=1, source_target_pairs={{0,8},{4,12},{8,0},{12,4},{1,9},{5,13},{9,1},{13,5},{2,10},{6,14},... | collective-permute-start | bytes 147464 | tf_op jit(solution)/shard_map/ppermute | solution.py:269
  26.5 5.1 %collective-permute-start.11 = (bf16[6,8,512]{2,1,0:T(8,128)(2,1)S(1)}, bf16[6,8,512]{2,1,0:T(8,128)(2,1)S(1)}, u32[]{:S(2)}, u32[]{:S(2)}) collective-permute-start(bf16[6,8,512]{2,1,0:T(8,128)(2,1)S(1)} %get-tuple-element.84), channel_id=1, source_target_pairs={{0,4},{4,0},{8,12},{12,8},{1,5},{5,1},{9,13},{13,9},{2,6},{6,2},{1... | collective-permute-start | bytes 147464 | tf_op jit(solution)/shard_map/ppermute | solution.py:269
  28.7 5.9 %collective-permute-start.9 = (bf16[6,8,512]{2,1,0:T(8,128)(2,1)S(1)}, bf16[6,8,512]{2,1,0:T(8,128)(2,1)S(1)}, u32[]{:S(2)}, u32[]{:S(2)}) collective-permute-start(bf16[6,8,512]{2,1,0:T(8,128)(2,1)S(1)} %get-tuple-element.86), channel_id=1, source_target_pairs={{0,12},{4,8},{8,4},{12,0},{1,13},{5,9},{9,5},{13,1},{2,14},{6,10},... | collective-permute-start | bytes 147464 | tf_op jit(solution)/shard_map/ppermute | solution.py:269
  34.7 1.5 %collective-permute-start.12 = (bf16[4,6,8,512]{3,2,1,0:T(8,128)(2,1)S(1)}, bf16[4,6,8,512]{3,2,1,0:T(8,128)(2,1)S(1)}, u32[]{:S(2)}, u32[]{:S(2)}) collective-permute-start(bf16[4,6,8,512]{3,2,1,0:T(8,128)(2,1)S(1)} %pad_maximum_fusion.3), channel_id=1, source_target_pairs={{0,1},{1,0},{2,3},{3,2},{4,5},{5,4},{6,7},{7,6},{8,9},{9,8},{10,11... | collective-permute-start | bytes 589832 | tf_op jit(solution)/shard_map/ppermute | solution.py:155
  36.4 2.0 %copy-start.3 = (bf16[3,3,3,128,512]{4,3,2,1,0:T(8,128)(2,1)S(1)}, bf16[3,3,3,128,512]{4,3,2,1,0:T(8,128)(2,1)}, u32[]{:S(2)}) copy-start(bf16[3,3,3,128,512]{4,3,2,1,0:T(8,128)(2,1)} %param.18) | copy-start | bytes 10616836
  41.8 4.1 %collective-permute-start.13 = (bf16[4,4,16,128]{3,2,1,0:T(8,128)(2,1)S(1)}, bf16[4,4,16,128]{3,2,1,0:T(8,128)(2,1)S(1)}, u32[]{:S(2)}, u32[]{:S(2)}) collective-permute-start(bf16[4,4,16,128]{3,2,1,0:T(8,128)(2,1)S(1)} %multiply_convert_fusion.1), channel_id=1, source_target_pairs={{0,3},{1,2},{2,1},{3,0},{4,7},{5,6},{6,5},{7,4},{8,11},{9,10},{10,... | collective-permute-start | bytes 196616 | tf_op jit(solution)/shard_map/ppermute | solution.py:155
  46.0 1.4 %collective-permute-start.14 = (bf16[2,4,4,16,128]{4,3,2,1,0:T(8,128)(2,1)S(1)}, bf16[2,4,4,16,128]{4,3,2,1,0:T(8,128)(2,1)S(1)}, u32[]{:S(2)}, u32[]{:S(2)}) collective-permute-start(bf16[2,4,4,16,128]{4,3,2,1,0:T(8,128)(2,1)S(1)} %pad_maximum_fusion.5), channel_id=1, source_target_pairs={{0,1},{1,0},{2,3},{3,2},{4,5},{5,4},{6,7},{7,6},{8,9},{9,8},{10,11... | collective-permute-start | bytes 393224 | tf_op jit(solution)/shard_map/ppermute | solution.py:155
  46.2 2.0 %copy-start.4 = (bf16[3,3,3,128,512]{4,3,2,1,0:T(8,128)(2,1)S(1)}, bf16[3,3,3,128,512]{4,3,2,1,0:T(8,128)(2,1)}, u32[]{:S(2)}) copy-start(bf16[3,3,3,128,512]{4,3,2,1,0:T(8,128)(2,1)} %param.19) | copy-start | bytes 10616836
  50.8 3.2 %collective-permute-start.15 = (bf16[4,2,4,128]{3,2,1,0:T(4,128)(2,1)S(1)}, bf16[4,2,4,128]{3,2,1,0:T(4,128)(2,1)S(1)}, u32[]{:S(2)}, u32[]{:S(2)}) collective-permute-start(bf16[4,2,4,128]{3,2,1,0:T(4,128)(2,1)S(1)} %get-tuple-element.93), channel_id=1, source_target_pairs={{0,3},{1,2},{2,1},{3,0},{4,7},{5,6},{6,5},{7,4},{8,11},{9,10},{10,... | collective-permute-start | bytes 24584 | tf_op jit(solution)/shard_map/ppermute | solution.py:155
  51.7 3.7 %collective-permute-start.16 = (bf16[4,2,4,128]{3,2,1,0:T(4,128)(2,1)S(1)}, bf16[4,2,4,128]{3,2,1,0:T(4,128)(2,1)S(1)}, u32[]{:S(2)}, u32[]{:S(2)}) collective-permute-start(bf16[4,2,4,128]{3,2,1,0:T(4,128)(2,1)S(1)} %get-tuple-element.92), channel_id=1, source_target_pairs={{0,2},{1,3},{2,0},{3,1},{4,6},{5,7},{6,4},{7,5},{8,10},{9,11},{10,... | collective-permute-start | bytes 24584 | tf_op jit(solution)/shard_map/ppermute | solution.py:155
  52.8 2.5 %collective-permute-start.17 = (bf16[4,2,4,128]{3,2,1,0:T(4,128)(2,1)S(1)}, bf16[4,2,4,128]{3,2,1,0:T(4,128)(2,1)S(1)}, u32[]{:S(2)}, u32[]{:S(2)}) collective-permute-start(bf16[4,2,4,128]{3,2,1,0:T(4,128)(2,1)S(1)} %get-tuple-element.91), channel_id=1, source_target_pairs={{0,1},{1,0},{2,3},{3,2},{4,5},{5,4},{6,7},{7,6},{8,9},{9,8},{10,11... | collective-permute-start | bytes 24584 | tf_op jit(solution)/shard_map/ppermute | solution.py:155

commit v2 on v0

--- a/solution.py
+++ b/solution.py
@@ -1,6 +1,10 @@
+import functools
+
 import jax
 import jax.numpy as jnp
 from jax import lax
+from jax.experimental import pallas as pl
+from jax.experimental.pallas import tpu as pltpu
 from jax.sharding import PartitionSpec as P
 
 HEAD = 32
@@ -150,7 +154,300 @@
     return lax.all_to_all(final, "frame", split_axis=2, concat_axis=3, tiled=True)
 
 
+def swap(cells, mask):
+    count = lax.axis_size("frame")
+    return lax.ppermute(cells, "frame", [(i, i ^ mask) for i in range(count)])
+
+
+def in_order(pieces, place, dim):
+    step = 1
+    while step < len(pieces):
+        flip = (place & step) != 0
+        pieces = [jnp.where(flip, pieces[i ^ step], pieces[i]) for i in range(len(pieces))]
+        step *= 2
+    return jnp.concatenate(pieces, axis=dim)
+
+
+def gathered_by_mask(cells):
+    count = lax.axis_size("frame")
+    pieces = [None] * count
+    pieces[0] = cells
+    masks = list(range(3, count, 2))
+    for mask in masks:
+        pieces[mask] = swap(cells, mask)
+    for mask in [0] + masks:
+        pieces[mask ^ 1] = swap(pieces[mask], 1)
+    return pieces
+
+
+def silu(values):
+    return values / (1.0 + jnp.exp(-values))
+
+
+def half_of(place):
+    return (place ^ (place >> 1)) & 1
+
+
+def call(body, operands, outs, scratch=(), flops=0):
+    moved = sum(o.size * o.dtype.itemsize for o in operands)
+    return pl.pallas_call(
+        body,
+        out_shape=[jax.ShapeDtypeStruct(shape, kind) for shape, kind in outs],
+        scratch_shapes=[pltpu.VMEM(shape, kind) for shape, kind in scratch],
+        compiler_params=pltpu.CompilerParams(vmem_limit_bytes=40 * 1024 * 1024),
+        cost_estimate=pl.CostEstimate(flops=flops, bytes_accessed=moved, transcendentals=0),
+    )(*operands)
+
+
+def attend_body(count, *refs):
+    pieces, (weight, mixed_ref, cells_ref) = refs[:count], refs[count:]
+    place = lax.axis_index("frame")
+    rows = pieces[0].shape[0]
+    for mask, piece in enumerate(pieces):
+        at = pl.multiple_of((place ^ mask) * rows, rows)
+        cells_ref[pl.ds(at, rows)] = piece[...]
+    tokens, share = mixed_ref.shape
+    packed = lax.dot_general(
+        cells_ref[...],
+        weight[...].reshape(3 * share, weight.shape[2]),
+        (((1,), (1,)), ((), ())),
+        preferred_element_type=jnp.float32,
+    ).astype(jnp.bfloat16)
+    query = jnp.maximum(packed[:, :share], 0)
+    keys = jnp.maximum(packed[:, share : 2 * share], 0)
+    values = packed[:, 2 * share :]
+    joined = jnp.concatenate([values, jnp.ones_like(values)], axis=1)
+    table = lax.dot_general(
+        keys, joined, (((0,), (0,)), ((), ())), preferred_element_type=jnp.float32
+    ) * (1.0 / tokens)
+    head_in = lax.broadcasted_iota(jnp.int32, table.shape, 0) // HEAD
+    head_out = lax.rem(lax.broadcasted_iota(jnp.int32, table.shape, 1), share) // HEAD
+    table = jnp.where(head_in == head_out, table, 0.0)
+    high = table.astype(jnp.bfloat16)
+    low = (table - high.astype(jnp.float32)).astype(jnp.bfloat16)
+    both = jnp.dot(query, high, preferred_element_type=jnp.float32) + jnp.dot(
+        query, low, preferred_element_type=jnp.float32
+    )
+    mixed_ref[...] = (both[:, :share] / jnp.maximum(both[:, share:], 1.0)).astype(jnp.bfloat16)
+
+
+def mlp_body(count, columns, *refs):
+    mixed, out_weight = refs[:count], refs[count : 2 * count]
+    cells, gain, in_weight, depth, down, kept_ref, sent_ref, first_ref, field = refs[2 * count :]
+    place = lax.axis_index("frame")
+    tokens, width = cells.shape
+    units = down.shape[0]
+    height = tokens // columns
+    attn_out = sum(
+        jnp.dot(a[...], b[...], preferred_element_type=jnp.float32)
+        for a, b in zip(mixed, out_weight)
+    )
+    first = (cells[...].astype(jnp.float32) + norm_rows(attn_out, gain[...])).astype(jnp.bfloat16)
+    at = pl.multiple_of(place * units, units)
+    column = lax.rem(lax.broadcasted_iota(jnp.int32, (tokens, units), 0), columns)
+    blank = jnp.zeros((columns, units), jnp.float32)
+    spread = []
+    for part in range(2):
+        inner = silu(jnp.dot(first, in_weight[part], preferred_element_type=jnp.float32))
+        field[pl.ds(0, columns)] = blank
+        field[pl.ds(columns, tokens)] = inner.astype(jnp.bfloat16).astype(jnp.float32)
+        field[pl.ds(columns + tokens, columns)] = blank
+        sides = []
+        for shift_col in range(3):
+            sides.append(
+                sum(
+                    field[pl.ds(shift_row * columns, tokens)]
+                    * depth[shift_row, shift_col, part : part + 1, pl.ds(at, units)]
+                    for shift_row in range(3)
+                )
+            )
+        spread.append(
+            jnp.where(column > 0, pltpu.roll(sides[0], 1, 0), 0.0)
+            + sides[1]
+            + jnp.where(column < columns - 1, pltpu.roll(sides[2], tokens - 1, 0), 0.0)
+        )
+    gated = (spread[0] * silu(spread[1])).astype(jnp.bfloat16)
+    partial = jnp.dot(gated, down[...], preferred_element_type=jnp.float32)
+    partial = partial.reshape(height // 2, 2, columns, width)
+    first = first.reshape(height // 2, 2, columns, width)
+    odd = half_of(place) == 1
+    kept_ref[...] = jnp.where(odd, partial[:, 1], partial[:, 0])
+    sent_ref[...] = jnp.where(odd, partial[:, 0], partial[:, 1])
+    first_ref[...] = jnp.where(odd, first[:, 1], first[:, 0])
+
+
+def norm_body(far_count, step, *refs):
+    total, first, gain = refs[:3]
+    far, outs, framed = refs[3 : 3 + far_count], refs[3 + far_count : -1], refs[-1]
+    level = lax.axis_index("row")
+    mlp_out = total[...]
+    for piece in far:
+        mlp_out = mlp_out + piece[...].astype(jnp.float32)
+    second = first[...].astype(jnp.float32) + norm_rows(mlp_out, gain[...].reshape(1, 1, -1))
+    rows = second.shape[0]
+    blank = jnp.zeros(framed.shape[1:], framed.dtype)
+    framed[0] = blank
+    framed[rows + 1] = blank
+    framed[1 : rows + 1] = second.astype(jnp.bfloat16)
+    for mask, out in enumerate(outs):
+        out[...] = framed[pl.ds((level ^ mask) * step, step + 2)]
+
+
+def conv_rows(field, kernel):
+    frames, rows = field.shape[0] - 2, field.shape[1] - 2
+    columns, width = field.shape[2:]
+    share = kernel.shape[3]
+    tokens = frames * rows * columns
+    total = None
+    for shift_time in range(3):
+        for shift_row in range(3):
+            slab = field[shift_time : shift_time + frames, shift_row : shift_row + rows]
+            term = lax.dot_general(
+                slab.reshape(tokens, width),
+                kernel[shift_time, shift_row].reshape(3 * share, width),
+                (((1,), (1,)), ((), ())),
+                preferred_element_type=jnp.float32,
+            )
+            total = term if total is None else total + term
+    column = lax.rem(lax.broadcasted_iota(jnp.int32, (tokens, share), 0), columns)
+    before = jnp.where(column > 0, pltpu.roll(total[:, :share], 1, 0), 0.0)
+    after = jnp.where(column < columns - 1, pltpu.roll(total[:, 2 * share :], tokens - 1, 0), 0.0)
+    return (before + total[:, share : 2 * share] + after).reshape(frames, rows, columns, share)
+
+
+def clear_ends(field):
+    edge = jnp.zeros(field.shape[1:], field.dtype)
+    field[0] = edge
+    field[field.shape[0] - 1] = edge
+
+
+def first_conv_body(height, *refs):
+    kernel, hidden_ref, part_ref, field = refs[-4:]
+    pieces = refs[:-4]
+    count = len(pieces) // 2
+    level, place = lax.axis_index("row"), lax.axis_index("frame")
+    clear_ends(field)
+    for index, piece in enumerate(pieces):
+        frame = (level ^ (index % count)) + 1
+        parity = half_of(place) ^ (index // count)
+        for row in range(piece.shape[0]):
+            field[frame, 2 * row + parity] = piece[row]
+    activated = silu(conv_rows(field, kernel))
+    frames, band, columns, share = hidden_ref.shape
+    rows = band - 2
+    global_row = level * rows - 1 + lax.broadcasted_iota(jnp.int32, activated.shape, 1)
+    inside = (global_row >= 0) & (global_row < height)
+    hidden_ref[...] = jnp.where(inside, activated, 0.0).astype(jnp.bfloat16)
+    at = pl.multiple_of(place * share, share)
+    part_ref[...] = field[1 : frames + 1, 2 : 2 + rows, :, pl.ds(at, share)]
+
+
+def second_conv_body(*refs):
+    part, kernel, out_ref, field = refs[-4:]
+    pieces = refs[:-4]
+    place = lax.axis_index("frame")
+    clear_ends(field)
+    share = part.shape[3]
+    frames = part.shape[0]
+    for mask, piece in enumerate(pieces):
+        at = pl.multiple_of((place ^ mask) * share, share)
+        field[1 : frames + 1, :, :, pl.ds(at, share)] = piece[...]
+    result = conv_rows(field, kernel)
+    out_ref[...] = (part[...].astype(jnp.float32) + result).astype(jnp.bfloat16)
+
+
+def by_frames(
+    latent,
+    qkv_weight,
+    out_weight,
+    attn_gain,
+    in_weight,
+    depth_weight,
+    down_weight,
+    mlp_gain,
+    conv_first,
+    conv_second,
+):
+    count = lax.axis_size("frame")
+    place = lax.axis_index("frame")
+    rows, columns, width = latent.shape[1:]
+    height = rows * count
+    tokens = height * columns
+    share = qkv_weight.shape[1]
+    units = down_weight.shape[0]
+    half = height // 2
+    bf16, f32 = jnp.bfloat16, jnp.float32
+    own = latent.reshape(rows * columns, width)
+    pieces = [None] * count
+    masks = [1] + list(range(2, count, 2))
+    for mask in masks:
+        pairs = [
+            (z * count + f, f * count + (z ^ mask)) for z in range(count) for f in range(count)
+        ]
+        pieces[mask] = lax.ppermute(own, ("row", "frame"), pairs)
+    for mask in masks:
+        pieces[mask ^ 1] = swap(pieces[mask], 1)
+    out_pieces = gathered_by_mask(out_weight)
+    in_parts = jnp.transpose(in_weight, (1, 0, 2))
+    mixed, cells = call(
+        functools.partial(attend_body, count),
+        [*pieces, qkv_weight],
+        [((tokens, share), bf16), ((tokens, width), bf16)],
+        flops=2 * tokens * width * 3 * share,
+    )
+    kept, sent, first = call(
+        functools.partial(mlp_body, count, columns),
+        [
+            *gathered_by_mask(mixed),
+            *out_pieces,
+            cells,
+            attn_gain.reshape(1, width),
+            in_parts,
+            depth_weight,
+            down_weight,
+        ],
+        [((half, columns, width), f32)] * 2 + [((half, columns, width), bf16)],
+        scratch=[((tokens + 2 * columns, units), f32)],
+        flops=2 * tokens * width * (width + 3 * units),
+    )
+    total = kept + swap(sent, 1)
+    far = [swap(total.astype(bf16), mask) for mask in range(3, count, 2)]
+    step = rows // 2
+    windows = call(
+        functools.partial(norm_body, len(far), step),
+        [total, first, mlp_gain.reshape(1, width), *far],
+        [((step + 2, columns, width), bf16)] * count,
+        scratch=[((half + 2, columns, width), bf16)],
+        flops=8 * total.size,
+    )
+    windows = list(windows)
+    for mask in range(1, count):
+        windows[mask] = lax.ppermute(windows[mask], "row", [(i, i ^ mask) for i in range(count)])
+    others = [swap(window, 1) for window in windows]
+    hidden, own_part = call(
+        functools.partial(first_conv_body, height),
+        [*windows, *others, conv_first],
+        [((count, rows + 2, columns, share), bf16), ((count, rows, columns, share), bf16)],
+        scratch=[((count + 2, rows + 4, columns, width), bf16)],
+        flops=2 * count * (rows + 2) * columns * 27 * width * share,
+    )
+    (final,) = call(
+        second_conv_body,
+        [*gathered_by_mask(hidden), own_part, conv_second],
+        [((count, rows, columns, share), bf16)],
+        scratch=[((count + 2, rows + 2, columns, width), bf16)],
+        flops=2 * count * rows * columns * 27 * width * share,
+    )
+    strip = columns // count
+    strips = [
+        lax.dynamic_slice_in_dim(final, (place ^ mask) * strip, strip, 2) for mask in range(count)
+    ]
+    outs = [strips[0]] + [swap(strips[mask], mask) for mask in range(1, count)]
+    return in_order(outs, place, 3)
+
+
 def solution(mesh):
+    body = by_frames if mesh.shape["row"] == mesh.shape["frame"] else local
     in_specs = (
         P(("parts", "frame"), "row", None, None),
         P(None, "frame", None),
@@ -164,4 +461,4 @@
         P(None, None, None, "frame", None),
     )
     out_specs = P("parts", "row", "frame", None)
-    return jax.shard_map(local, mesh=mesh, in_specs=in_specs, out_specs=out_specs, check_vma=False)
+    return jax.shard_map(body, mesh=mesh, in_specs=in_specs, out_specs=out_specs, check_vma=False)

time: 138 us -> 58.9 us (0.43)
  blocking collectives: 47.6 us -> 0 us
  waiting for transfers between devices: 45.7 us -> 20 us
  matrix products: 13.8 us -> 0 us
  between operations: 13.6 us -> 0.11 us
  starting transfers between devices: 9.45 us -> 21.1 us
  Pallas kernels: 0 us -> 6.88 us
  local copies, waits for them, and re-layouts: 6.56 us -> 8.79 us
    all_gather x3 -> x0, waiting for transfers between devices: 32.3 us -> none  [the longest x1 12.2 us: local(): lax.all_gather(qkv_weight, 'frame', axis=1, tiled=True)]
    psum x1 -> x0, blocking collectives: 21.3 us -> none  [attend(): lax.psum(state.astype(jnp.bfloat16), 'row').astype(jnp.float32)]
    all_gather x3 -> x0, blocking collectives: 20 us -> none  [the longest x1 8.62 us: local(): lax.all_gather(out_weight, 'frame', axis=0, tiled=True)]
    dot_general x25 -> x0, matrix products: 13.8 us -> none  [the longest x18 5.73 us: conv_tile(): jnp.einsum('nci,coi->no', stacked.reshape(-1, 3, width), kernel[shift_tim...]
    ppermute x4 -> x25, starting transfers between devices: 9.37 us -> 21.1 us  [the longest x20 12.4 us: swap(): return lax.ppermute(cells, 'frame', [(i, i ^ mask) for i in range(count)])]
    ppermute x4 -> x25, waiting for transfers between devices: 11.9 us -> 20 us  [the longest x20 14.2 us: swap(): return lax.ppermute(cells, 'frame', [(i, i ^ mask) for i in range(count)])]
    pallas_call x0 -> x5, Pallas kernels: none -> 6.88 us  [call(): pl.pallas_call(body, out_shape=[jax.ShapeDtypeStruct(shape, kind) for sha...]
    all_to_all x1 -> x0, blocking collectives: 6.3 us -> none  [local(): lax.all_to_all(final, 'frame', split_axis=2, concat_axis=3, tiled=True)]
  transfers between devices with their start and end apart: 7 -> 25, of which waited for: 7 -> 13; matrix products, arithmetic and copies ran while one was open for 8% -> 2% of each run, Pallas kernels for 0% -> 1%
where the time goes in v2:
time: 58.9 us; the launch traced here: 58.3 us
  starting transfers between devices  21.1 us (36%)
  waiting for transfers between devices  20 us (34%)
  local copies, waits for them, and re-layouts  8.79 us (15%)
  Pallas kernels  6.88 us (12%)
  other arithmetic  1.39 us (2%)
    ppermute x20, waiting for transfers between devices, swap(): return lax.ppermute(cells, 'frame', [(i, i ^ mask) for i in range(count)])  14.2 us
    ppermute x20, starting transfers between devices, swap(): return lax.ppermute(cells, 'frame', [(i, i ^ mask) for i in range(count)])  12.4 us
    unnamed x21, local copies, waits for them, and re-layouts  7.98 us
    pallas_call x5, Pallas kernels, call(): pl.pallas_call(body, out_shape=[jax.ShapeDtypeStruct(shape, kind) for sha...  6.88 us
    ppermute x3, starting transfers between devices, by_frames(): lax.ppermute(windows[mask], 'row', [(i, i ^ mask) for i in range(count)])  4.45 us
    ppermute x2, starting transfers between devices, by_frames(): pieces[mask] = lax.ppermute(own, ('row', 'frame'), pairs)  4.33 us
    ppermute x3, waiting for transfers between devices, by_frames(): lax.ppermute(windows[mask], 'row', [(i, i ^ mask) for i in range(count)])  4.1 us
    ppermute x2, waiting for transfers between devices, by_frames(): pieces[mask] = lax.ppermute(own, ('row', 'frame'), pairs)  1.71 us
  transfers between devices with their start and end apart: 25, of which 13 were waited for; matrix products, arithmetic and copies ran while one was open for 2% of the time, Pallas kernels for 1%

profile of v2, /device:TPU:0, one launch (start us, length us, event | category | flops | bytes accessed | tf_op | source)
XLA Modules:
  0.0 58.3 jit_solution(15594447302786074086)
XLA Ops:
  0.0 2.4 %collective-permute-start.8 = (bf16[128,512]{1,0:T(8,128)(2,1)}, bf16[128,512]{1,0:T(8,128)(2,1)S(1)}, u32[]{:S(2)}, u32[]{:S(2)}) collective-permute-start(bf16[128,512]{1,0:T(8,128)(2,1)} %refs_4_.3), channel_id=1, source_target_pairs={{0,3},{1,2},{2,1},{3,0},{4,7},{5,6},{6,5},{7,4},{8,11},{9,10},{10,... | collective-permute-start | bytes 393224 | tf_op jit(solution)/shard_map/ppermute | solution.py:159
  3.1 3.7 %collective-permute-start.2 = (bf16[32,512]{1,0:T(8,128)(2,1)}, bf16[32,512]{1,0:T(8,128)(2,1)S(1)}, u32[]{:S(2)}, u32[]{:S(2)}) collective-permute-start(bf16[32,512]{1,0:T(8,128)(2,1)} %bitcast.10), channel_id=1, source_target_pairs={{0,2},{1,6},{2,10},{3,14},{4,3},{5,7},{6,11},{7,15},{8,0},{9,4},{1... | collective-permute-start | bytes 98312 | tf_op jit(solution)/shard_map/ppermute | solution.py:387
  7.5 1.7 %collective-permute-done.2.refs_2_ = bf16[32,512]{1,0:T(8,128)(2,1)S(1)} collective-permute-done((bf16[32,512]{1,0:T(8,128)(2,1)}, bf16[32,512]{1,0:T(8,128)(2,1)S(1)}, u32[]{:S(2)}, u32[]{:S(2)}) %collective-permute-start.2) | collective-permute-done | bytes 32800 | tf_op jit(solution)/shard_map/ppermute | solution.py:387
  10.6 1.0 %copy-done.3 = bf16[3,128,512]{2,1,0:T(8,128)(2,1)S(1)} copy-done((bf16[3,128,512]{2,1,0:T(8,128)(2,1)S(1)}, bf16[3,128,512]{2,1,0:T(8,128)(2,1)}, u32[]{:S(2)}) %copy-start.3) | copy-done | bytes 393240
  12.2 2.6 %collective-permute-start.5 = (bf16[128,128]{1,0:T(8,128)(2,1)S(1)}, bf16[128,128]{1,0:T(8,128)(2,1)S(1)}, u32[]{:S(2)}, u32[]{:S(2)}) collective-permute-start(bf16[128,128]{1,0:T(8,128)(2,1)S(1)} %get-tuple-element.16.refs_0_), channel_id=1, source_target_pairs={{0,3},{1,2},{2,1},{3,0},{4,7},{5,6},{6,5},{7,4},{8,11},{9,10},{10,... | collective-permute-start | bytes 98312 | tf_op jit(solution)/shard_map/ppermute | solution.py:159
  15.0 1.4 %collective-permute-done.5.refs_3_ = bf16[128,128]{1,0:T(8,128)(2,1)S(1)} collective-permute-done((bf16[128,128]{1,0:T(8,128)(2,1)S(1)}, bf16[128,128]{1,0:T(8,128)(2,1)S(1)}, u32[]{:S(2)}, u32[]{:S(2)}) %collective-permute-start.5) | collective-permute-done | bytes 32800 | tf_op jit(solution)/shard_map/ppermute | solution.py:159
  16.6 1.4 %copy.13 = bf16[512,2,512]{2,0,1:T(8,128)(2,1)S(1)} copy(bf16[512,2,512]{2,1,0:T(2,128)(2,1)} %param.14) | data formatting | bytes 2097152 | tf_op args[4]
  18.1 1.0 %copy-done.2 = bf16[512,512]{1,0:T(8,128)(2,1)S(1)} copy-done((bf16[512,512]{1,0:T(8,128)(2,1)S(1)}, bf16[512,512]{1,0:T(8,128)(2,1)}, u32[]{:S(2)}) %copy-start.2) | copy-done | bytes 524312
  21.6 1.3 %shard_map.101 = (f32[4,16,512]{2,1,0:T(8,128)S(1)}, f32[4,16,512]{2,1,0:T(8,128)S(1)}, bf16[4,16,512]{2,1,0:T(8,128)(2,1)S(1)}) custom-call(bf16[128,128]{1,0:T(8,128)(2,1)S(1)} %get-tuple-element.16.refs_0_, bf16[128,128]{1,0:T(8,128)(2,1)S(1)} %collective-permute-done.4.refs_1_, bf16[128,128]{1,0:T(8,128)(2,1)S(1)} %collective-permute-done.6.refs_2_, ...), custom_call_target="tpu_custom_call" | custom-call | flops 268435456 | bytes 2508800 | tf_op jit(solution)/shard_map/pallas_call | solution.py:193
  23.3 1.0 %collective-permute-done.10 = f32[4,16,512]{2,1,0:T(8,128)S(1)} collective-permute-done((f32[4,16,512]{2,1,0:T(8,128)S(1)}, f32[4,16,512]{2,1,0:T(8,128)S(1)}, u32[]{:S(2)}, u32[]{:S(2)}) %collective-permute-start.10) | collective-permute-done | bytes 131104 | tf_op jit(solution)/shard_map/ppermute | solution.py:159
  24.3 1.8 %collective-permute-start.11 = (bf16[4,16,512]{2,1,0:T(8,128)(2,1)S(1)}, bf16[4,16,512]{2,1,0:T(8,128)(2,1)S(1)}, u32[]{:S(2)}, u32[]{:S(2)}) collective-permute-start(bf16[4,16,512]{2,1,0:T(8,128)(2,1)S(1)} %get-tuple-element.27), channel_id=1, source_target_pairs={{0,3},{1,2},{2,1},{3,0},{4,7},{5,6},{6,5},{7,4},{8,11},{9,10},{10,... | collective-permute-start | bytes 196616 | tf_op jit(solution)/shard_map/ppermute | solution.py:159
  26.1 2.2 %collective-permute-done.11.refs_3_ = bf16[4,16,512]{2,1,0:T(8,128)(2,1)S(1)} collective-permute-done((bf16[4,16,512]{2,1,0:T(8,128)(2,1)S(1)}, bf16[4,16,512]{2,1,0:T(8,128)(2,1)S(1)}, u32[]{:S(2)}, u32[]{:S(2)}) %collective-permute-start.11) | collective-permute-done | bytes 65568 | tf_op jit(solution)/shard_map/ppermute | solution.py:159
  29.8 2.5 %collective-permute-start.13 = (bf16[3,16,512]{2,1,0:T(8,128)(2,1)S(1)}, bf16[3,16,512]{2,1,0:T(8,128)(2,1)S(1)}, u32[]{:S(2)}, u32[]{:S(2)}) collective-permute-start(bf16[3,16,512]{2,1,0:T(8,128)(2,1)S(1)} %get-tuple-element.23), channel_id=1, source_target_pairs={{0,8},{4,12},{8,0},{12,4},{1,9},{5,13},{9,1},{13,5},{2,10},{6,14},... | collective-permute-start | bytes 147464 | tf_op jit(solution)/shard_map/ppermute | solution.py:425
  32.3 1.3 %collective-permute-start.14 = (bf16[3,16,512]{2,1,0:T(8,128)(2,1)S(1)}, bf16[3,16,512]{2,1,0:T(8,128)(2,1)S(1)}, u32[]{:S(2)}, u32[]{:S(2)}) collective-permute-start(bf16[3,16,512]{2,1,0:T(8,128)(2,1)S(1)} %get-tuple-element.24), channel_id=1, source_target_pairs={{0,12},{4,8},{8,4},{12,0},{1,13},{5,9},{9,5},{13,1},{2,14},{6,10},... | collective-permute-start | bytes 147464 | tf_op jit(solution)/shard_map/ppermute | solution.py:425
  34.1 2.1 %collective-permute-done.13.refs_2_ = bf16[3,16,512]{2,1,0:T(8,128)(2,1)S(1)} collective-permute-done((bf16[3,16,512]{2,1,0:T(8,128)(2,1)S(1)}, bf16[3,16,512]{2,1,0:T(8,128)(2,1)S(1)}, u32[]{:S(2)}, u32[]{:S(2)}) %collective-permute-start.13) | collective-permute-done | bytes 49184 | tf_op jit(solution)/shard_map/ppermute | solution.py:425
  36.2 2.0 %collective-permute-done.14.refs_3_ = bf16[3,16,512]{2,1,0:T(8,128)(2,1)S(1)} collective-permute-done((bf16[3,16,512]{2,1,0:T(8,128)(2,1)S(1)}, bf16[3,16,512]{2,1,0:T(8,128)(2,1)S(1)}, u32[]{:S(2)}, u32[]{:S(2)}) %collective-permute-start.14) | collective-permute-done | bytes 49184 | tf_op jit(solution)/shard_map/ppermute | solution.py:425
  38.2 1.2 %collective-permute-done.18.refs_7_ = bf16[3,16,512]{2,1,0:T(8,128)(2,1)S(1)} collective-permute-done((bf16[3,16,512]{2,1,0:T(8,128)(2,1)S(1)}, bf16[3,16,512]{2,1,0:T(8,128)(2,1)S(1)}, u32[]{:S(2)}, u32[]{:S(2)}) %collective-permute-start.18) | collective-permute-done | bytes 49184 | tf_op jit(solution)/shard_map/ppermute | solution.py:159
  39.4 2.1 %shard_map.103 = (bf16[4,4,16,128]{3,2,1,0:T(8,128)(2,1)}, bf16[4,2,16,128]{3,2,1,0:T(8,128)(2,1)S(1)}) custom-call(bf16[3,16,512]{2,1,0:T(8,128)(2,1)S(1)} %get-tuple-element.21.refs_0_, bf16[3,16,512]{2,1,0:T(8,128)(2,1)S(1)} %collective-permute-done.12.refs_1_, bf16[3,16,512]{2,1,0:T(8,128)(2,1)S(1)} %collective-permute-done.13.refs_2_, ...), custom_call_target="tpu_custom_call" | custom-call | flops 905969664 | bytes 3932160 | tf_op jit(solution)/shard_map/pallas_call | solution.py:193
  43.3 3.2 %collective-permute-done.20.refs_3_ = bf16[4,4,16,128]{3,2,1,0:T(8,128)(2,1)} collective-permute-done((bf16[4,4,16,128]{3,2,1,0:T(8,128)(2,1)}, bf16[4,4,16,128]{3,2,1,0:T(8,128)(2,1)}, u32[]{:S(2)}, u32[]{:S(2)}) %collective-permute-start.20) | collective-permute-done | bytes 65568 | tf_op jit(solution)/shard_map/ppermute | solution.py:159
  46.6 1.4 %collective-permute-done.21.refs_2_ = bf16[4,4,16,128]{3,2,1,0:T(8,128)(2,1)} collective-permute-done((bf16[4,4,16,128]{3,2,1,0:T(8,128)(2,1)}, bf16[4,4,16,128]{3,2,1,0:T(8,128)(2,1)}, u32[]{:S(2)}, u32[]{:S(2)}) %collective-permute-start.21) | collective-permute-done | bytes 65568 | tf_op jit(solution)/shard_map/ppermute | solution.py:159
  48.8 2.7 %shard_map.104 = bf16[4,2,16,128]{3,2,1,0:T(8,128)(2,1)} custom-call(bf16[4,4,16,128]{3,2,1,0:T(8,128)(2,1)} %get-tuple-element.25.refs_0_, bf16[4,4,16,128]{3,2,1,0:T(8,128)(2,1)} %collective-permute-done.19.refs_1_, bf16[4,4,16,128]{3,2,1,0:T(8,128)(2,1)} %collective-permute-done.21.refs_2_, bf16[4,4,16,128]{3,2,1,0:T(8,128)(2,1)} %collective-permute-done.20.refs_3_, ...), custom_call_target="tpu_custom_call" | custom-call | flops 452984832 | bytes 3833856 | tf_op jit(solution)/shard_map/pallas_call | solution.py:193
  53.3 0.9 %collective-permute-start.23 = (bf16[4,2,4,128]{3,2,1,0:T(4,128)(2,1)S(1)}, bf16[4,2,4,128]{3,2,1,0:T(4,128)(2,1)S(1)}, u32[]{:S(2)}, u32[]{:S(2)}) collective-permute-start(bf16[4,2,4,128]{3,2,1,0:T(4,128)(2,1)S(1)} %get-tuple-element.34), channel_id=1, source_target_pairs={{0,2},{1,3},{2,0},{3,1},{4,6},{5,7},{6,4},{7,5},{8,10},{9,11},{10,... | collective-permute-start | bytes 24584 | tf_op jit(solution)/shard_map/ppermute | solution.py:159
  54.3 1.2 %collective-permute-done.22 = bf16[4,2,4,128]{3,2,1,0:T(4,128)(2,1)S(1)} collective-permute-done((bf16[4,2,4,128]{3,2,1,0:T(4,128)(2,1)S(1)}, bf16[4,2,4,128]{3,2,1,0:T(4,128)(2,1)S(1)}, u32[]{:S(2)}, u32[]{:S(2)}) %collective-permute-start.22) | collective-permute-done | bytes 8224 | tf_op jit(solution)/shard_map/ppermute | solution.py:159
  55.5 1.4 %collective-permute-done.23 = bf16[4,2,4,128]{3,2,1,0:T(4,128)(2,1)S(1)} collective-permute-done((bf16[4,2,4,128]{3,2,1,0:T(4,128)(2,1)S(1)}, bf16[4,2,4,128]{3,2,1,0:T(4,128)(2,1)S(1)}, u32[]{:S(2)}, u32[]{:S(2)}) %collective-permute-start.23) | collective-permute-done | bytes 8224 | tf_op jit(solution)/shard_map/ppermute | solution.py:159
  (56 shorter events, 14.7 us)
Async XLA Ops:
  0.0 7.0 %collective-permute-start.8 = (bf16[128,512]{1,0:T(8,128)(2,1)}, bf16[128,512]{1,0:T(8,128)(2,1)S(1)}, u32[]{:S(2)}, u32[]{:S(2)}) collective-permute-start(bf16[128,512]{1,0:T(8,128)(2,1)} %refs_4_.3), channel_id=1, source_target_pairs={{0,3},{1,2},{2,1},{3,0},{4,7},{5,6},{6,5},{7,4},{8,11},{9,10},{10,... | collective-permute-start | bytes 393224 | tf_op jit(solution)/shard_map/ppermute | solution.py:159
  2.4 4.9 %collective-permute-start = (bf16[32,512]{1,0:T(8,128)(2,1)}, bf16[32,512]{1,0:T(8,128)(2,1)S(1)}, u32[]{:S(2)}, u32[]{:S(2)}) collective-permute-start(bf16[32,512]{1,0:T(8,128)(2,1)} %bitcast.9), channel_id=1, source_target_pairs={{0,1},{1,5},{2,9},{3,13},{4,0},{5,4},{6,8},{7,12},{8,3},{9,7},{10,... | collective-permute-start | bytes 98312 | tf_op jit(solution)/shard_map/ppermute | solution.py:387
  3.1 6.1 %collective-permute-start.2 = (bf16[32,512]{1,0:T(8,128)(2,1)}, bf16[32,512]{1,0:T(8,128)(2,1)S(1)}, u32[]{:S(2)}, u32[]{:S(2)}) collective-permute-start(bf16[32,512]{1,0:T(8,128)(2,1)} %bitcast.10), channel_id=1, source_target_pairs={{0,2},{1,6},{2,10},{3,14},{4,3},{5,7},{6,11},{7,15},{8,0},{9,4},{1... | collective-permute-start | bytes 98312 | tf_op jit(solution)/shard_map/ppermute | solution.py:387
  6.7 11.3 %collective-permute-start.7 = (bf16[128,512]{1,0:T(8,128)(2,1)}, bf16[128,512]{1,0:T(8,128)(2,1)S(1)}, u32[]{:S(2)}, u32[]{:S(2)}) collective-permute-start(bf16[128,512]{1,0:T(8,128)(2,1)} %refs_4_.3), channel_id=1, source_target_pairs={{0,1},{1,0},{2,3},{3,2},{4,5},{5,4},{6,7},{7,6},{8,9},{9,8},{10,11... | collective-permute-start | bytes 393224 | tf_op jit(solution)/shard_map/ppermute | solution.py:159
  7.0 11.1 %collective-permute-start.9 = (bf16[128,512]{1,0:T(8,128)(2,1)S(1)}, bf16[128,512]{1,0:T(8,128)(2,1)S(1)}, u32[]{:S(2)}, u32[]{:S(2)}) collective-permute-start(bf16[128,512]{1,0:T(8,128)(2,1)S(1)} %collective-permute-done.8.refs_7_), channel_id=1, source_target_pairs={{0,1},{1,0},{2,3},{3,2},{4,5},{5,4},{6,7},{7,6},{8,9},{9,8},{10,11... | collective-permute-start | bytes 393224 | tf_op jit(solution)/shard_map/ppermute | solution.py:159
  7.2 2.5 %collective-permute-start.1 = (bf16[32,512]{1,0:T(8,128)(2,1)S(1)}, bf16[32,512]{1,0:T(8,128)(2,1)S(1)}, u32[]{:S(2)}, u32[]{:S(2)}) collective-permute-start(bf16[32,512]{1,0:T(8,128)(2,1)S(1)} %collective-permute-done.refs_1_), channel_id=1, source_target_pairs={{0,1},{1,0},{2,3},{3,2},{4,5},{5,4},{6,7},{7,6},{8,9},{9,8},{10,11... | collective-permute-start | bytes 98312 | tf_op jit(solution)/shard_map/ppermute | solution.py:159
  9.2 1.4 %collective-permute-start.3 = (bf16[32,512]{1,0:T(8,128)(2,1)S(1)}, bf16[32,512]{1,0:T(8,128)(2,1)S(1)}, u32[]{:S(2)}, u32[]{:S(2)}) collective-permute-start(bf16[32,512]{1,0:T(8,128)(2,1)S(1)} %collective-permute-done.2.refs_2_), channel_id=1, source_target_pairs={{0,1},{1,0},{2,3},{3,2},{4,5},{5,4},{6,7},{7,6},{8,9},{9,8},{10,11... | collective-permute-start | bytes 98312 | tf_op jit(solution)/shard_map/ppermute | solution.py:159
  12.2 4.2 %collective-permute-start.5 = (bf16[128,128]{1,0:T(8,128)(2,1)S(1)}, bf16[128,128]{1,0:T(8,128)(2,1)S(1)}, u32[]{:S(2)}, u32[]{:S(2)}) collective-permute-start(bf16[128,128]{1,0:T(8,128)(2,1)S(1)} %get-tuple-element.16.refs_0_), channel_id=1, source_target_pairs={{0,3},{1,2},{2,1},{3,0},{4,7},{5,6},{6,5},{7,4},{8,11},{9,10},{10,... | collective-permute-start | bytes 98312 | tf_op jit(solution)/shard_map/ppermute | solution.py:159
  14.8 3.2 %collective-permute-start.4 = (bf16[128,128]{1,0:T(8,128)(2,1)S(1)}, bf16[128,128]{1,0:T(8,128)(2,1)S(1)}, u32[]{:S(2)}, u32[]{:S(2)}) collective-permute-start(bf16[128,128]{1,0:T(8,128)(2,1)S(1)} %get-tuple-element.16.refs_0_), channel_id=1, source_target_pairs={{0,1},{1,0},{2,3},{3,2},{4,5},{5,4},{6,7},{7,6},{8,9},{9,8},{10,11... | collective-permute-start | bytes 98312 | tf_op jit(solution)/shard_map/ppermute | solution.py:159
  16.4 1.6 %collective-permute-start.6 = (bf16[128,128]{1,0:T(8,128)(2,1)S(1)}, bf16[128,128]{1,0:T(8,128)(2,1)S(1)}, u32[]{:S(2)}, u32[]{:S(2)}) collective-permute-start(bf16[128,128]{1,0:T(8,128)(2,1)S(1)} %collective-permute-done.5.refs_3_), channel_id=1, source_target_pairs={{0,1},{1,0},{2,3},{3,2},{4,5},{5,4},{6,7},{7,6},{8,9},{9,8},{10,11... | collective-permute-start | bytes 98312 | tf_op jit(solution)/shard_map/ppermute | solution.py:159
  22.9 1.4 %collective-permute-start.10 = (f32[4,16,512]{2,1,0:T(8,128)S(1)}, f32[4,16,512]{2,1,0:T(8,128)S(1)}, u32[]{:S(2)}, u32[]{:S(2)}) collective-permute-start(f32[4,16,512]{2,1,0:T(8,128)S(1)} %get-tuple-element.19), channel_id=1, source_target_pairs={{0,1},{1,0},{2,3},{3,2},{4,5},{5,4},{6,7},{7,6},{8,9},{9,8},{10,11... | collective-permute-start | bytes 393224 | tf_op jit(solution)/shard_map/ppermute | solution.py:159
  24.3 4.0 %collective-permute-start.11 = (bf16[4,16,512]{2,1,0:T(8,128)(2,1)S(1)}, bf16[4,16,512]{2,1,0:T(8,128)(2,1)S(1)}, u32[]{:S(2)}, u32[]{:S(2)}) collective-permute-start(bf16[4,16,512]{2,1,0:T(8,128)(2,1)S(1)} %get-tuple-element.27), channel_id=1, source_target_pairs={{0,3},{1,2},{2,1},{3,0},{4,7},{5,6},{6,5},{7,4},{8,11},{9,10},{10,... | collective-permute-start | bytes 196616 | tf_op jit(solution)/shard_map/ppermute | solution.py:159
  29.1 4.5 %collective-permute-start.12 = (bf16[3,16,512]{2,1,0:T(8,128)(2,1)S(1)}, bf16[3,16,512]{2,1,0:T(8,128)(2,1)S(1)}, u32[]{:S(2)}, u32[]{:S(2)}) collective-permute-start(bf16[3,16,512]{2,1,0:T(8,128)(2,1)S(1)} %get-tuple-element.22), channel_id=1, source_target_pairs={{0,4},{4,0},{8,12},{12,8},{1,5},{5,1},{9,13},{13,9},{2,6},{6,2},{1... | collective-permute-start | bytes 147464 | tf_op jit(solution)/shard_map/ppermute | solution.py:425
  29.8 6.4 %collective-permute-start.13 = (bf16[3,16,512]{2,1,0:T(8,128)(2,1)S(1)}, bf16[3,16,512]{2,1,0:T(8,128)(2,1)S(1)}, u32[]{:S(2)}, u32[]{:S(2)}) collective-permute-start(bf16[3,16,512]{2,1,0:T(8,128)(2,1)S(1)} %get-tuple-element.23), channel_id=1, source_target_pairs={{0,8},{4,12},{8,0},{12,4},{1,9},{5,13},{9,1},{13,5},{2,10},{6,14},... | collective-permute-start | bytes 147464 | tf_op jit(solution)/shard_map/ppermute | solution.py:425
  32.3 5.9 %collective-permute-start.14 = (bf16[3,16,512]{2,1,0:T(8,128)(2,1)S(1)}, bf16[3,16,512]{2,1,0:T(8,128)(2,1)S(1)}, u32[]{:S(2)}, u32[]{:S(2)}) collective-permute-start(bf16[3,16,512]{2,1,0:T(8,128)(2,1)S(1)} %get-tuple-element.24), channel_id=1, source_target_pairs={{0,12},{4,8},{8,4},{12,0},{1,13},{5,9},{9,5},{13,1},{2,14},{6,10},... | collective-permute-start | bytes 147464 | tf_op jit(solution)/shard_map/ppermute | solution.py:425
  33.6 4.6 %collective-permute-start.15 = (bf16[3,16,512]{2,1,0:T(8,128)(2,1)S(1)}, bf16[3,16,512]{2,1,0:T(8,128)(2,1)S(1)}, u32[]{:S(2)}, u32[]{:S(2)}) collective-permute-start(bf16[3,16,512]{2,1,0:T(8,128)(2,1)S(1)} %get-tuple-element.21.refs_0_), channel_id=1, source_target_pairs={{0,1},{1,0},{2,3},{3,2},{4,5},{5,4},{6,7},{7,6},{8,9},{9,8},{10,11... | collective-permute-start | bytes 147464 | tf_op jit(solution)/shard_map/ppermute | solution.py:159
  33.6 4.6 %collective-permute-start.16 = (bf16[3,16,512]{2,1,0:T(8,128)(2,1)S(1)}, bf16[3,16,512]{2,1,0:T(8,128)(2,1)S(1)}, u32[]{:S(2)}, u32[]{:S(2)}) collective-permute-start(bf16[3,16,512]{2,1,0:T(8,128)(2,1)S(1)} %collective-permute-done.12.refs_1_), channel_id=1, source_target_pairs={{0,1},{1,0},{2,3},{3,2},{4,5},{5,4},{6,7},{7,6},{8,9},{9,8},{10,11... | collective-permute-start | bytes 147464 | tf_op jit(solution)/shard_map/ppermute | solution.py:159
  36.2 2.0 %collective-permute-start.17 = (bf16[3,16,512]{2,1,0:T(8,128)(2,1)S(1)}, bf16[3,16,512]{2,1,0:T(8,128)(2,1)S(1)}, u32[]{:S(2)}, u32[]{:S(2)}) collective-permute-start(bf16[3,16,512]{2,1,0:T(8,128)(2,1)S(1)} %collective-permute-done.13.refs_2_), channel_id=1, source_target_pairs={{0,1},{1,0},{2,3},{3,2},{4,5},{5,4},{6,7},{7,6},{8,9},{9,8},{10,11... | collective-permute-start | bytes 147464 | tf_op jit(solution)/shard_map/ppermute | solution.py:159
  42.1 4.4 %collective-permute-start.20 = (bf16[4,4,16,128]{3,2,1,0:T(8,128)(2,1)}, bf16[4,4,16,128]{3,2,1,0:T(8,128)(2,1)}, u32[]{:S(2)}, u32[]{:S(2)}) collective-permute-start(bf16[4,4,16,128]{3,2,1,0:T(8,128)(2,1)} %get-tuple-element.25.refs_0_), channel_id=1, source_target_pairs={{0,3},{1,2},{2,1},{3,0},{4,7},{5,6},{6,5},{7,4},{8,11},{9,10},{10,... | collective-permute-start | bytes 196616 | tf_op jit(solution)/shard_map/ppermute | solution.py:159
  42.9 3.7 %collective-permute-start.19 = (bf16[4,4,16,128]{3,2,1,0:T(8,128)(2,1)}, bf16[4,4,16,128]{3,2,1,0:T(8,128)(2,1)}, u32[]{:S(2)}, u32[]{:S(2)}) collective-permute-start(bf16[4,4,16,128]{3,2,1,0:T(8,128)(2,1)} %get-tuple-element.25.refs_0_), channel_id=1, source_target_pairs={{0,1},{1,0},{2,3},{3,2},{4,5},{5,4},{6,7},{7,6},{8,9},{9,8},{10,11... | collective-permute-start | bytes 196616 | tf_op jit(solution)/shard_map/ppermute | solution.py:159
  46.5 1.6 %collective-permute-start.21 = (bf16[4,4,16,128]{3,2,1,0:T(8,128)(2,1)}, bf16[4,4,16,128]{3,2,1,0:T(8,128)(2,1)}, u32[]{:S(2)}, u32[]{:S(2)}) collective-permute-start(bf16[4,4,16,128]{3,2,1,0:T(8,128)(2,1)} %collective-permute-done.20.refs_3_), channel_id=1, source_target_pairs={{0,1},{1,0},{2,3},{3,2},{4,5},{5,4},{6,7},{7,6},{8,9},{9,8},{10,11... | collective-permute-start | bytes 196616 | tf_op jit(solution)/shard_map/ppermute | solution.py:159
  52.4 3.1 %collective-permute-start.22 = (bf16[4,2,4,128]{3,2,1,0:T(4,128)(2,1)S(1)}, bf16[4,2,4,128]{3,2,1,0:T(4,128)(2,1)S(1)}, u32[]{:S(2)}, u32[]{:S(2)}) collective-permute-start(bf16[4,2,4,128]{3,2,1,0:T(4,128)(2,1)S(1)} %get-tuple-element.35), channel_id=1, source_target_pairs={{0,3},{1,2},{2,1},{3,0},{4,7},{5,6},{6,5},{7,4},{8,11},{9,10},{10,... | collective-permute-start | bytes 24584 | tf_op jit(solution)/shard_map/ppermute | solution.py:159
  53.3 3.7 %collective-permute-start.23 = (bf16[4,2,4,128]{3,2,1,0:T(4,128)(2,1)S(1)}, bf16[4,2,4,128]{3,2,1,0:T(4,128)(2,1)S(1)}, u32[]{:S(2)}, u32[]{:S(2)}) collective-permute-start(bf16[4,2,4,128]{3,2,1,0:T(4,128)(2,1)S(1)} %get-tuple-element.34), channel_id=1, source_target_pairs={{0,2},{1,3},{2,0},{3,1},{4,6},{5,7},{6,4},{7,5},{8,10},{9,11},{10,... | collective-permute-start | bytes 24584 | tf_op jit(solution)/shard_map/ppermute | solution.py:159
  54.2 2.7 %collective-permute-start.24 = (bf16[4,2,4,128]{3,2,1,0:T(4,128)(2,1)S(1)}, bf16[4,2,4,128]{3,2,1,0:T(4,128)(2,1)S(1)}, u32[]{:S(2)}, u32[]{:S(2)}) collective-permute-start(bf16[4,2,4,128]{3,2,1,0:T(4,128)(2,1)S(1)} %get-tuple-element.33), channel_id=1, source_target_pairs={{0,1},{1,0},{2,3},{3,2},{4,5},{5,4},{6,7},{7,6},{8,9},{9,8},{10,11... | collective-permute-start | bytes 24584 | tf_op jit(solution)/shard_map/ppermute | solution.py:159
  (11 other events, 73.7 us)

commit v3 on v2

--- a/solution.py
+++ b/solution.py
@@ -188,13 +188,13 @@
     return (place ^ (place >> 1)) & 1
 
 
-def call(body, operands, outs, scratch=(), flops=0):
+def call(body, operands, outs, scratch=(), flops=0, room=4):
     moved = sum(o.size * o.dtype.itemsize for o in operands)
     return pl.pallas_call(
         body,
         out_shape=[jax.ShapeDtypeStruct(shape, kind) for shape, kind in outs],
         scratch_shapes=[pltpu.VMEM(shape, kind) for shape, kind in scratch],
-        compiler_params=pltpu.CompilerParams(vmem_limit_bytes=40 * 1024 * 1024),
+        compiler_params=pltpu.CompilerParams(vmem_limit_bytes=room * 1024 * 1024),
         cost_estimate=pl.CostEstimate(flops=flops, bytes_accessed=moved, transcendentals=0),
     )(*operands)
 
@@ -209,7 +209,7 @@
     tokens, share = mixed_ref.shape
     packed = lax.dot_general(
         cells_ref[...],
-        weight[...].reshape(3 * share, weight.shape[2]),
+        weight[pl.ds(0, 3 * share)],
         (((1,), (1,)), ((), ())),
         preferred_element_type=jnp.float32,
     ).astype(jnp.bfloat16)
@@ -232,23 +232,25 @@
 
 
 def mlp_body(count, columns, *refs):
-    mixed, out_weight = refs[:count], refs[count : 2 * count]
-    cells, gain, in_weight, depth, down, kept_ref, sent_ref, first_ref, field = refs[2 * count :]
+    mixed, out_weight = refs[:count], refs[count : 2 * count - 1]
+    cells, weights, scales, kept_ref, sent_ref, first_ref, field = refs[2 * count - 1 :]
     place = lax.axis_index("frame")
     tokens, width = cells.shape
-    units = down.shape[0]
+    units = field.shape[1]
+    share = mixed[0].shape[1]
+    starts = [3 * share, 4 * share, 4 * share + units, 4 * share + units + width]
+    own_out, down = weights[pl.ds(starts[0], share)], weights[pl.ds(starts[1], units)]
     height = tokens // columns
     attn_out = sum(
-        jnp.dot(a[...], b[...], preferred_element_type=jnp.float32)
-        for a, b in zip(mixed, out_weight)
-    )
-    first = (cells[...].astype(jnp.float32) + norm_rows(attn_out, gain[...])).astype(jnp.bfloat16)
-    at = pl.multiple_of(place * units, units)
+        jnp.dot(a[...], b, preferred_element_type=jnp.float32)
+        for a, b in zip(mixed, [own_out] + [piece[...] for piece in out_weight])
+    )
+    first = (cells[...].astype(jnp.float32) + norm_rows(attn_out, scales[18:19])).astype(jnp.bfloat16)
     column = lax.rem(lax.broadcasted_iota(jnp.int32, (tokens, units), 0), columns)
     blank = jnp.zeros((columns, units), jnp.float32)
     spread = []
     for part in range(2):
-        inner = silu(jnp.dot(first, in_weight[part], preferred_element_type=jnp.float32))
+        inner = silu(jnp.dot(first, weights[pl.ds(starts[2 + part], width)], preferred_element_type=jnp.float32))
         field[pl.ds(0, columns)] = blank
         field[pl.ds(columns, tokens)] = inner.astype(jnp.bfloat16).astype(jnp.float32)
         field[pl.ds(columns + tokens, columns)] = blank
@@ -257,8 +259,8 @@
             sides.append(
                 sum(
                     field[pl.ds(shift_row * columns, tokens)]
-                    * depth[shift_row, shift_col, part : part + 1, pl.ds(at, units)]
-                    for shift_row in range(3)
+                    * scales[tap : tap + 1]
+                    for shift_row, tap in enumerate(range(2 * shift_col + part, 18, 6))
                 )
             )
         spread.append(
@@ -267,7 +269,7 @@
             + jnp.where(column < columns - 1, pltpu.roll(sides[2], tokens - 1, 0), 0.0)
         )
     gated = (spread[0] * silu(spread[1])).astype(jnp.bfloat16)
-    partial = jnp.dot(gated, down[...], preferred_element_type=jnp.float32)
+    partial = jnp.dot(gated, down, preferred_element_type=jnp.float32)
     partial = partial.reshape(height // 2, 2, columns, width)
     first = first.reshape(height // 2, 2, columns, width)
     odd = half_of(place) == 1
@@ -283,7 +285,7 @@
     mlp_out = total[...]
     for piece in far:
         mlp_out = mlp_out + piece[...].astype(jnp.float32)
-    second = first[...].astype(jnp.float32) + norm_rows(mlp_out, gain[...].reshape(1, 1, -1))
+    second = first[...].astype(jnp.float32) + norm_rows(mlp_out, gain[19:20].reshape(1, 1, -1))
     rows = second.shape[0]
     blank = jnp.zeros(framed.shape[1:], framed.dtype)
     framed[0] = blank
@@ -343,8 +345,9 @@
 
 
 def second_conv_body(*refs):
-    part, kernel, out_ref, field = refs[-4:]
-    pieces = refs[:-4]
+    pieces = refs[: (len(refs) - 4) // 2]
+    part, kernel = refs[len(pieces) : len(pieces) + 2]
+    outs, field, final = refs[len(pieces) + 2 : -2], refs[-2], refs[-1]
     place = lax.axis_index("frame")
     clear_ends(field)
     share = part.shape[3]
@@ -352,8 +355,32 @@
     for mask, piece in enumerate(pieces):
         at = pl.multiple_of((place ^ mask) * share, share)
         field[1 : frames + 1, :, :, pl.ds(at, share)] = piece[...]
-    result = conv_rows(field, kernel)
-    out_ref[...] = (part[...].astype(jnp.float32) + result).astype(jnp.bfloat16)
+    final[...] = part[...].astype(jnp.float32) + conv_rows(field, kernel)
+    lines = final.shape[0] * final.shape[1]
+    strip = outs[0].shape[0] // lines
+    for mask, out in enumerate(outs):
+        at = pl.multiple_of((place ^ mask) * strip, strip)
+        out[...] = jnp.concatenate(
+            [
+                final[line // final.shape[1], line % final.shape[1], pl.ds(at, strip)]
+                for line in range(lines)
+            ],
+            axis=0,
+        ).astype(jnp.bfloat16)
+
+
+def join_body(*refs):
+    pieces, out_ref = refs[:-1], refs[-1]
+    place = lax.axis_index("frame")
+    share = pieces[0].shape[1]
+    frames, rows, strip = out_ref.shape[:3]
+    for mask, piece in enumerate(pieces):
+        at = pl.multiple_of((place ^ mask) * share, share)
+        cells = piece[...].astype(jnp.float32)
+        for line in range(frames * rows):
+            out_ref[line // rows, line % rows, :, pl.ds(at, share)] = cells[
+                line * strip : (line + 1) * strip
+            ].astype(jnp.bfloat16)
 
 
 def by_frames(
@@ -388,10 +415,19 @@
     for mask in masks:
         pieces[mask ^ 1] = swap(pieces[mask], 1)
     out_pieces = gathered_by_mask(out_weight)
-    in_parts = jnp.transpose(in_weight, (1, 0, 2))
+    weights = jnp.concatenate(
+        [
+            qkv_weight.reshape(3 * share, width),
+            out_weight,
+            down_weight,
+            jnp.transpose(in_weight, (1, 0, 2)).reshape(-1, units),
+        ]
+    )
+    taps = lax.dynamic_slice_in_dim(depth_weight, place * units, units, 3)
+    scales = jnp.concatenate([taps.reshape(-1, units), attn_gain[None], mlp_gain[None]])
     mixed, cells = call(
         functools.partial(attend_body, count),
-        [*pieces, qkv_weight],
+        [*pieces, weights],
         [((tokens, share), bf16), ((tokens, width), bf16)],
         flops=2 * tokens * width * 3 * share,
     )
@@ -399,23 +435,22 @@
         functools.partial(mlp_body, count, columns),
         [
             *gathered_by_mask(mixed),
-            *out_pieces,
+            *out_pieces[1:],
             cells,
-            attn_gain.reshape(1, width),
-            in_parts,
-            depth_weight,
-            down_weight,
+            weights,
+            scales,
         ],
         [((half, columns, width), f32)] * 2 + [((half, columns, width), bf16)],
         scratch=[((tokens + 2 * columns, units), f32)],
         flops=2 * tokens * width * (width + 3 * units),
+        room=8,
     )
     total = kept + swap(sent, 1)
     far = [swap(total.astype(bf16), mask) for mask in range(3, count, 2)]
     step = rows // 2
     windows = call(
         functools.partial(norm_body, len(far), step),
-        [total, first, mlp_gain.reshape(1, width), *far],
+        [total, first, scales, *far],
         [((step + 2, columns, width), bf16)] * count,
         scratch=[((half + 2, columns, width), bf16)],
         flops=8 * total.size,
@@ -430,20 +465,23 @@
         [((count, rows + 2, columns, share), bf16), ((count, rows, columns, share), bf16)],
         scratch=[((count + 2, rows + 4, columns, width), bf16)],
         flops=2 * count * (rows + 2) * columns * 27 * width * share,
-    )
-    (final,) = call(
+        room=8,
+    )
+    strip = columns // count
+    strips = call(
         second_conv_body,
         [*gathered_by_mask(hidden), own_part, conv_second],
-        [((count, rows, columns, share), bf16)],
-        scratch=[((count + 2, rows + 2, columns, width), bf16)],
+        [((count * rows * strip, share), bf16)] * count,
+        scratch=[
+            ((count + 2, rows + 2, columns, width), bf16),
+            ((count, rows, columns, share), f32),
+        ],
         flops=2 * count * rows * columns * 27 * width * share,
-    )
-    strip = columns // count
-    strips = [
-        lax.dynamic_slice_in_dim(final, (place ^ mask) * strip, strip, 2) for mask in range(count)
-    ]
+        room=8,
+    )
     outs = [strips[0]] + [swap(strips[mask], mask) for mask in range(1, count)]
-    return in_order(outs, place, 3)
+    (decoded,) = call(join_body, outs, [((count, rows, strip, width), bf16)])
+    return decoded
 
 
 def solution(mesh):

time: 58.9 us -> 46.7 us (0.79)
  local copies, waits for them, and re-layouts: 8.79 us -> 1.45 us
  starting transfers between devices: 21.1 us -> 19.4 us
  Pallas kernels: 6.88 us -> 5.3 us
  waiting for transfers between devices: 20 us -> 18.9 us
    unnamed x21 -> x10, local copies, waits for them, and re-layouts: 7.98 us -> 0.03 us
    ppermute x20, starting transfers between devices: 12.4 us -> 9.97 us  [swap(): return lax.ppermute(cells, 'frame', [(i, i ^ mask) for i in range(count)])]
    ppermute x2, waiting for transfers between devices: 1.71 us -> 0.01 us  [by_frames(): pieces[mask] = lax.ppermute(own, ('row', 'frame'), pairs)]
    pallas_call x5 -> x6, Pallas kernels: 6.88 us -> 5.3 us  [call(): pl.pallas_call(body, out_shape=[jax.ShapeDtypeStruct(shape, kind) for sha...]
    transpose x0 -> x1, local copies, waits for them, and re-layouts: none -> 1.39 us  [by_frames(): jnp.transpose(in_weight, (1, 0, 2)).reshape(-1, units)]
    ppermute x3, waiting for transfers between devices: 4.1 us -> 5.37 us  [by_frames(): lax.ppermute(windows[mask], 'row', [(i, i ^ mask) for i in range(count)])]
    dynamic_slice x1, local copies, waits for them, and re-layouts: 0.81 us -> 0.01 us  [by_frames(): taps = lax.dynamic_slice_in_dim(depth_weight, place * units, units, 3)]
    select_n x1 -> x0, other arithmetic: 0.74 us -> none  [in_order(): jnp.where(flip, pieces[i ^ step], pieces[i])]
  transfers between devices with their start and end apart: 25 -> 25, of which waited for: 13 -> 10; matrix products, arithmetic and copies ran while one was open for 2% -> 6% of each run, Pallas kernels for 1% -> 1%
where the time goes in v3:
time: 46.7 us; the launch traced here: 46.6 us
  starting transfers between devices  19.4 us (42%)
  waiting for transfers between devices  18.9 us (40%)
  Pallas kernels  5.3 us (11%)
  local copies, waits for them, and re-layouts  1.45 us (3%)
  other arithmetic  1.36 us (3%)
    ppermute x20, waiting for transfers between devices, swap(): return lax.ppermute(cells, 'frame', [(i, i ^ mask) for i in range(count)])  13.5 us
    ppermute x20, starting transfers between devices, swap(): return lax.ppermute(cells, 'frame', [(i, i ^ mask) for i in range(count)])  9.97 us
    ppermute x3, waiting for transfers between devices, by_frames(): lax.ppermute(windows[mask], 'row', [(i, i ^ mask) for i in range(count)])  5.37 us
    pallas_call x6, Pallas kernels, call(): pl.pallas_call(body, out_shape=[jax.ShapeDtypeStruct(shape, kind) for sha...  5.3 us
    ppermute x2, starting transfers between devices, by_frames(): pieces[mask] = lax.ppermute(own, ('row', 'frame'), pairs)  4.94 us
    ppermute x3, starting transfers between devices, by_frames(): lax.ppermute(windows[mask], 'row', [(i, i ^ mask) for i in range(count)])  4.52 us
    transpose x1, local copies, waits for them, and re-layouts, by_frames(): jnp.transpose(in_weight, (1, 0, 2)).reshape(-1, units)  1.39 us
    concatenate x1, other arithmetic, by_frames(): jnp.concatenate([qkv_weight.reshape(3 * share, width), out_weight, down_w...  1.33 us
  transfers between devices with their start and end apart: 25, of which 10 were waited for; matrix products, arithmetic and copies ran while one was open for 6% of the time, Pallas kernels for 1%

profile of v3, /device:TPU:0, one launch (start us, length us, event | category | flops | bytes accessed | tf_op | source)
XLA Modules:
  0.0 46.6 jit_solution(15686682563483797300)
XLA Ops:
  0.5 4.5 %collective-permute-start.2 = (bf16[32,512]{1,0:T(8,128)(2,1)}, bf16[32,512]{1,0:T(8,128)(2,1)S(1)}, u32[]{:S(2)}, u32[]{:S(2)}) collective-permute-start(bf16[32,512]{1,0:T(8,128)(2,1)} %bitcast.12), channel_id=1, source_target_pairs={{0,2},{1,6},{2,10},{3,14},{4,3},{5,7},{6,11},{7,15},{8,0},{9,4},{1... | collective-permute-start | bytes 98312 | tf_op jit(solution)/shard_map/ppermute | solution.py:414
  4.9 1.8 %collective-permute-start.8 = (bf16[128,512]{1,0:T(8,128)(2,1)}, bf16[128,512]{1,0:T(8,128)(2,1)S(1)}, u32[]{:S(2)}, u32[]{:S(2)}) collective-permute-start(bf16[128,512]{1,0:T(8,128)(2,1)} %param.12), channel_id=1, source_target_pairs={{0,3},{1,2},{2,1},{3,0},{4,7},{5,6},{6,5},{7,4},{8,11},{9,10},{10,... | collective-permute-start | bytes 393224 | tf_op jit(solution)/shard_map/ppermute | solution.py:159
  6.7 1.4 %copy.11 = bf16[2,512,512]{2,1,0:T(8,128)(2,1)S(1)} copy(bf16[2,512,512]{2,0,1:T(2,128)(2,1)} %bitcast.7) | data formatting | bytes 2097152 | tf_op jit(solution)/shard_map/transpose | solution.py:423
  8.1 0.6 %collective-permute-start.1 = (bf16[32,512]{1,0:T(8,128)(2,1)S(1)}, bf16[32,512]{1,0:T(8,128)(2,1)S(1)}, u32[]{:S(2)}, u32[]{:S(2)}) collective-permute-start(bf16[32,512]{1,0:T(8,128)(2,1)S(1)} %collective-permute-done.refs_1_), channel_id=1, source_target_pairs={{0,1},{1,0},{2,3},{3,2},{4,5},{5,4},{6,7},{7,6},{8,9},{9,8},{10,11... | collective-permute-start | bytes 98312 | tf_op jit(solution)/shard_map/ppermute | solution.py:159
  8.8 1.3 %pad_maximum_fusion.refs_4_.refs_8_ = bf16[2048,512]{1,0:T(8,128)(2,1)S(1)} fusion(bf16[1024,512]{1,0:T(8,128)(2,1)S(1)} %bitcast.6, bf16[512,512]{1,0:T(8,128)(2,1)} %param.16, bf16[128,512]{1,0:T(8,128)(2,1)} %param.12, bf16[384,512]{1,0:T(8,128)(2,1)} %bitcast.8), kind=kLoop, calls=%fused_computation | loop fusion | flops 8388608 | bytes 4194304 | tf_op jit(solution)/shard_map/concatenate | solution.py:418
  10.2 0.7 %shard_map.100 = (bf16[128,128]{1,0:T(8,128)(2,1)S(1)}, bf16[128,512]{1,0:T(8,128)(2,1)S(1)}) custom-call(bf16[32,512]{1,0:T(8,128)(2,1)S(1)} %collective-permute-done.1.refs_0_, bf16[32,512]{1,0:T(8,128)(2,1)S(1)} %collective-permute-done.refs_1_, bf16[32,512]{1,0:T(8,128)(2,1)S(1)} %collective-permute-done.2.refs_2_, ...), custom_call_target="tpu_custom_call" | custom-call | flops 50331648 | bytes 2228224 | tf_op jit(solution)/shard_map/pallas_call | solution.py:193
  10.8 1.4 %collective-permute-start.5 = (bf16[128,128]{1,0:T(8,128)(2,1)S(1)}, bf16[128,128]{1,0:T(8,128)(2,1)S(1)}, u32[]{:S(2)}, u32[]{:S(2)}) collective-permute-start(bf16[128,128]{1,0:T(8,128)(2,1)S(1)} %get-tuple-element.20.refs_0_), channel_id=1, source_target_pairs={{0,3},{1,2},{2,1},{3,0},{4,7},{5,6},{6,5},{7,4},{8,11},{9,10},{10,... | collective-permute-start | bytes 98312 | tf_op jit(solution)/shard_map/ppermute | solution.py:159
  12.9 1.3 %collective-permute-done.5.refs_3_ = bf16[128,128]{1,0:T(8,128)(2,1)S(1)} collective-permute-done((bf16[128,128]{1,0:T(8,128)(2,1)S(1)}, bf16[128,128]{1,0:T(8,128)(2,1)S(1)}, u32[]{:S(2)}, u32[]{:S(2)}) %collective-permute-start.5) | collective-permute-done | bytes 32800 | tf_op jit(solution)/shard_map/ppermute | solution.py:159
  14.7 0.8 %collective-permute-done.6.refs_2_ = bf16[128,128]{1,0:T(8,128)(2,1)S(1)} collective-permute-done((bf16[128,128]{1,0:T(8,128)(2,1)S(1)}, bf16[128,128]{1,0:T(8,128)(2,1)S(1)}, u32[]{:S(2)}, u32[]{:S(2)}) %collective-permute-start.6) | collective-permute-done | bytes 32800 | tf_op jit(solution)/shard_map/ppermute | solution.py:159
  15.6 1.2 %shard_map.101 = (f32[4,16,512]{2,1,0:T(8,128)S(1)}, f32[4,16,512]{2,1,0:T(8,128)S(1)}, bf16[4,16,512]{2,1,0:T(8,128)(2,1)S(1)}) custom-call(bf16[128,128]{1,0:T(8,128)(2,1)S(1)} %get-tuple-element.20.refs_0_, bf16[128,128]{1,0:T(8,128)(2,1)S(1)} %collective-permute-done.4.refs_1_, bf16[128,128]{1,0:T(8,128)(2,1)S(1)} %collective-permute-done.6.refs_2_, ...), custom_call_target="tpu_custom_call" | custom-call | flops 268435456 | bytes 2793472 | tf_op jit(solution)/shard_map/pallas_call | solution.py:193
  17.2 1.0 %collective-permute-done.10 = f32[4,16,512]{2,1,0:T(8,128)S(1)} collective-permute-done((f32[4,16,512]{2,1,0:T(8,128)S(1)}, f32[4,16,512]{2,1,0:T(8,128)S(1)}, u32[]{:S(2)}, u32[]{:S(2)}) %collective-permute-start.10) | collective-permute-done | bytes 131104 | tf_op jit(solution)/shard_map/ppermute | solution.py:159
  18.2 1.7 %collective-permute-start.11 = (bf16[4,16,512]{2,1,0:T(8,128)(2,1)S(1)}, bf16[4,16,512]{2,1,0:T(8,128)(2,1)S(1)}, u32[]{:S(2)}, u32[]{:S(2)}) collective-permute-start(bf16[4,16,512]{2,1,0:T(8,128)(2,1)S(1)} %get-tuple-element.35), channel_id=1, source_target_pairs={{0,3},{1,2},{2,1},{3,0},{4,7},{5,6},{6,5},{7,4},{8,11},{9,10},{10,... | collective-permute-start | bytes 196616 | tf_op jit(solution)/shard_map/ppermute | solution.py:159
  19.9 2.3 %collective-permute-done.11.refs_3_ = bf16[4,16,512]{2,1,0:T(8,128)(2,1)S(1)} collective-permute-done((bf16[4,16,512]{2,1,0:T(8,128)(2,1)S(1)}, bf16[4,16,512]{2,1,0:T(8,128)(2,1)S(1)}, u32[]{:S(2)}, u32[]{:S(2)}) %collective-permute-start.11) | collective-permute-done | bytes 65568 | tf_op jit(solution)/shard_map/ppermute | solution.py:159
  22.9 4.0 %collective-permute-start.13 = (bf16[3,16,512]{2,1,0:T(8,128)(2,1)S(1)}, bf16[3,16,512]{2,1,0:T(8,128)(2,1)S(1)}, u32[]{:S(2)}, u32[]{:S(2)}) collective-permute-start(bf16[3,16,512]{2,1,0:T(8,128)(2,1)S(1)} %get-tuple-element.27), channel_id=1, source_target_pairs={{0,8},{4,12},{8,0},{12,4},{1,9},{5,13},{9,1},{13,5},{2,10},{6,14},... | collective-permute-start | bytes 147464 | tf_op jit(solution)/shard_map/ppermute | solution.py:460
  27.4 2.7 %collective-permute-done.13.refs_2_ = bf16[3,16,512]{2,1,0:T(8,128)(2,1)S(1)} collective-permute-done((bf16[3,16,512]{2,1,0:T(8,128)(2,1)S(1)}, bf16[3,16,512]{2,1,0:T(8,128)(2,1)S(1)}, u32[]{:S(2)}, u32[]{:S(2)}) %collective-permute-start.13) | collective-permute-done | bytes 49184 | tf_op jit(solution)/shard_map/ppermute | solution.py:460
  30.1 2.7 %collective-permute-done.14.refs_3_ = bf16[3,16,512]{2,1,0:T(8,128)(2,1)S(1)} collective-permute-done((bf16[3,16,512]{2,1,0:T(8,128)(2,1)S(1)}, bf16[3,16,512]{2,1,0:T(8,128)(2,1)S(1)}, u32[]{:S(2)}, u32[]{:S(2)}) %collective-permute-start.14) | collective-permute-done | bytes 49184 | tf_op jit(solution)/shard_map/ppermute | solution.py:460
  32.8 1.2 %collective-permute-done.18.refs_7_ = bf16[3,16,512]{2,1,0:T(8,128)(2,1)S(1)} collective-permute-done((bf16[3,16,512]{2,1,0:T(8,128)(2,1)S(1)}, bf16[3,16,512]{2,1,0:T(8,128)(2,1)S(1)}, u32[]{:S(2)}, u32[]{:S(2)}) %collective-permute-start.18) | collective-permute-done | bytes 49184 | tf_op jit(solution)/shard_map/ppermute | solution.py:159
  34.0 1.4 %shard_map.103 = (bf16[4,4,16,128]{3,2,1,0:T(8,128)(2,1)S(1)}, bf16[4,2,16,128]{3,2,1,0:T(8,128)(2,1)S(1)}) custom-call(bf16[3,16,512]{2,1,0:T(8,128)(2,1)S(1)} %get-tuple-element.25.refs_0_, bf16[3,16,512]{2,1,0:T(8,128)(2,1)S(1)} %collective-permute-done.12.refs_1_, bf16[3,16,512]{2,1,0:T(8,128)(2,1)S(1)} %collective-permute-done.13.refs_2_, ...), custom_call_target="tpu_custom_call" | custom-call | flops 905969664 | bytes 3932160 | tf_op jit(solution)/shard_map/pallas_call | solution.py:193
  35.8 3.7 %collective-permute-done.20.refs_3_ = bf16[4,4,16,128]{3,2,1,0:T(8,128)(2,1)S(1)} collective-permute-done((bf16[4,4,16,128]{3,2,1,0:T(8,128)(2,1)S(1)}, bf16[4,4,16,128]{3,2,1,0:T(8,128)(2,1)S(1)}, u32[]{:S(2)}, u32[]{:S(2)}) %collective-permute-start.20) | collective-permute-done | bytes 65568 | tf_op jit(solution)/shard_map/ppermute | solution.py:159
  39.7 1.1 %collective-permute-done.21.refs_2_ = bf16[4,4,16,128]{3,2,1,0:T(8,128)(2,1)S(1)} collective-permute-done((bf16[4,4,16,128]{3,2,1,0:T(8,128)(2,1)S(1)}, bf16[4,4,16,128]{3,2,1,0:T(8,128)(2,1)S(1)}, u32[]{:S(2)}, u32[]{:S(2)}) %collective-permute-start.21) | collective-permute-done | bytes 65568 | tf_op jit(solution)/shard_map/ppermute | solution.py:159
  40.8 1.2 %shard_map.104 = (bf16[32,128]{1,0:T(8,128)(2,1)S(1)}, bf16[32,128]{1,0:T(8,128)(2,1)S(1)}, bf16[32,128]{1,0:T(8,128)(2,1)S(1)}, bf16[32,128]{1,0:T(8,128)(2,1)S(1)}) custom-call(bf16[4,4,16,128]{3,2,1,0:T(8,128)(2,1)S(1)} %get-tuple-element.29.refs_0_, bf16[4,4,16,128]{3,2,1,0:T(8,128)(2,1)S(1)} %collective-permute-done.19.refs_1_, ...), custom_call_target="tpu_custom_call" | custom-call | flops 452984832 | bytes 3833856 | tf_op jit(solution)/shard_map/pallas_call | solution.py:193
  42.5 1.5 %collective-permute-start.24 = (bf16[32,128]{1,0:T(8,128)(2,1)S(1)}, bf16[32,128]{1,0:T(8,128)(2,1)S(1)}, u32[]{:S(2)}, u32[]{:S(2)}) collective-permute-start(bf16[32,128]{1,0:T(8,128)(2,1)S(1)} %get-tuple-element.34), channel_id=1, source_target_pairs={{0,3},{1,2},{2,1},{3,0},{4,7},{5,6},{6,5},{7,4},{8,11},{9,10},{10,... | collective-permute-start | bytes 24584 | tf_op jit(solution)/shard_map/ppermute | solution.py:159
  44.0 2.0 %collective-permute-done.23.refs_2_ = bf16[32,128]{1,0:T(8,128)(2,1)S(1)} collective-permute-done((bf16[32,128]{1,0:T(8,128)(2,1)S(1)}, bf16[32,128]{1,0:T(8,128)(2,1)S(1)}, u32[]{:S(2)}, u32[]{:S(2)}) %collective-permute-start.23) | collective-permute-done | bytes 8224 | tf_op jit(solution)/shard_map/ppermute | solution.py:159
  45.9 0.6 %shard_map.105 = bf16[4,2,4,512]{3,2,1,0:T(4,128)(2,1)} custom-call(bf16[32,128]{1,0:T(8,128)(2,1)S(1)} %get-tuple-element.31.refs_0_, bf16[32,128]{1,0:T(8,128)(2,1)S(1)} %collective-permute-done.22.refs_1_, bf16[32,128]{1,0:T(8,128)(2,1)S(1)} %collective-permute-done.23.refs_2_, bf16[32,128]{1,0:T(8,128)(2,1)S(1)} %collective-permute-done.24.refs_3_), custom_call_target="tpu_custom_call" | custom-call | bytes 32768 | tf_op jit(solution)/shard_map/pallas_call | solution.py:193
  (48 shorter events, 4.3 us)
Async XLA Ops:
  0.0 8.1 %collective-permute-start = (bf16[32,512]{1,0:T(8,128)(2,1)}, bf16[32,512]{1,0:T(8,128)(2,1)S(1)}, u32[]{:S(2)}, u32[]{:S(2)}) collective-permute-start(bf16[32,512]{1,0:T(8,128)(2,1)} %bitcast.11), channel_id=1, source_target_pairs={{0,1},{1,5},{2,9},{3,13},{4,0},{5,4},{6,8},{7,12},{8,3},{9,7},{10,... | collective-permute-start | bytes 98312 | tf_op jit(solution)/shard_map/ppermute | solution.py:414
  0.5 8.3 %collective-permute-start.2 = (bf16[32,512]{1,0:T(8,128)(2,1)}, bf16[32,512]{1,0:T(8,128)(2,1)S(1)}, u32[]{:S(2)}, u32[]{:S(2)}) collective-permute-start(bf16[32,512]{1,0:T(8,128)(2,1)} %bitcast.12), channel_id=1, source_target_pairs={{0,2},{1,6},{2,10},{3,14},{4,3},{5,7},{6,11},{7,15},{8,0},{9,4},{1... | collective-permute-start | bytes 98312 | tf_op jit(solution)/shard_map/ppermute | solution.py:414
  4.9 7.3 %collective-permute-start.8 = (bf16[128,512]{1,0:T(8,128)(2,1)}, bf16[128,512]{1,0:T(8,128)(2,1)S(1)}, u32[]{:S(2)}, u32[]{:S(2)}) collective-permute-start(bf16[128,512]{1,0:T(8,128)(2,1)} %param.12), channel_id=1, source_target_pairs={{0,3},{1,2},{2,1},{3,0},{4,7},{5,6},{6,5},{7,4},{8,11},{9,10},{10,... | collective-permute-start | bytes 393224 | tf_op jit(solution)/shard_map/ppermute | solution.py:159
  6.7 8.8 %collective-permute-start.7 = (bf16[128,512]{1,0:T(8,128)(2,1)}, bf16[128,512]{1,0:T(8,128)(2,1)S(1)}, u32[]{:S(2)}, u32[]{:S(2)}) collective-permute-start(bf16[128,512]{1,0:T(8,128)(2,1)} %param.12), channel_id=1, source_target_pairs={{0,1},{1,0},{2,3},{3,2},{4,5},{5,4},{6,7},{7,6},{8,9},{9,8},{10,11... | collective-permute-start | bytes 393224 | tf_op jit(solution)/shard_map/ppermute | solution.py:159
  8.1 2.0 %collective-permute-start.1 = (bf16[32,512]{1,0:T(8,128)(2,1)S(1)}, bf16[32,512]{1,0:T(8,128)(2,1)S(1)}, u32[]{:S(2)}, u32[]{:S(2)}) collective-permute-start(bf16[32,512]{1,0:T(8,128)(2,1)S(1)} %collective-permute-done.refs_1_), channel_id=1, source_target_pairs={{0,1},{1,0},{2,3},{3,2},{4,5},{5,4},{6,7},{7,6},{8,9},{9,8},{10,11... | collective-permute-start | bytes 98312 | tf_op jit(solution)/shard_map/ppermute | solution.py:159
  8.7 1.4 %collective-permute-start.3 = (bf16[32,512]{1,0:T(8,128)(2,1)S(1)}, bf16[32,512]{1,0:T(8,128)(2,1)S(1)}, u32[]{:S(2)}, u32[]{:S(2)}) collective-permute-start(bf16[32,512]{1,0:T(8,128)(2,1)S(1)} %collective-permute-done.2.refs_2_), channel_id=1, source_target_pairs={{0,1},{1,0},{2,3},{3,2},{4,5},{5,4},{6,7},{7,6},{8,9},{9,8},{10,11... | collective-permute-start | bytes 98312 | tf_op jit(solution)/shard_map/ppermute | solution.py:159
  10.8 3.4 %collective-permute-start.5 = (bf16[128,128]{1,0:T(8,128)(2,1)S(1)}, bf16[128,128]{1,0:T(8,128)(2,1)S(1)}, u32[]{:S(2)}, u32[]{:S(2)}) collective-permute-start(bf16[128,128]{1,0:T(8,128)(2,1)S(1)} %get-tuple-element.20.refs_0_), channel_id=1, source_target_pairs={{0,3},{1,2},{2,1},{3,0},{4,7},{5,6},{6,5},{7,4},{8,11},{9,10},{10,... | collective-permute-start | bytes 98312 | tf_op jit(solution)/shard_map/ppermute | solution.py:159
  12.3 3.3 %collective-permute-start.9 = (bf16[128,512]{1,0:T(8,128)(2,1)S(1)}, bf16[128,512]{1,0:T(8,128)(2,1)S(1)}, u32[]{:S(2)}, u32[]{:S(2)}) collective-permute-start(bf16[128,512]{1,0:T(8,128)(2,1)S(1)} %collective-permute-done.8.refs_6_), channel_id=1, source_target_pairs={{0,1},{1,0},{2,3},{3,2},{4,5},{5,4},{6,7},{7,6},{8,9},{9,8},{10,11... | collective-permute-start | bytes 393224 | tf_op jit(solution)/shard_map/ppermute | solution.py:159
  12.8 1.9 %collective-permute-start.4 = (bf16[128,128]{1,0:T(8,128)(2,1)S(1)}, bf16[128,128]{1,0:T(8,128)(2,1)S(1)}, u32[]{:S(2)}, u32[]{:S(2)}) collective-permute-start(bf16[128,128]{1,0:T(8,128)(2,1)S(1)} %get-tuple-element.20.refs_0_), channel_id=1, source_target_pairs={{0,1},{1,0},{2,3},{3,2},{4,5},{5,4},{6,7},{7,6},{8,9},{9,8},{10,11... | collective-permute-start | bytes 98312 | tf_op jit(solution)/shard_map/ppermute | solution.py:159
  14.2 1.3 %collective-permute-start.6 = (bf16[128,128]{1,0:T(8,128)(2,1)S(1)}, bf16[128,128]{1,0:T(8,128)(2,1)S(1)}, u32[]{:S(2)}, u32[]{:S(2)}) collective-permute-start(bf16[128,128]{1,0:T(8,128)(2,1)S(1)} %collective-permute-done.5.refs_3_), channel_id=1, source_target_pairs={{0,1},{1,0},{2,3},{3,2},{4,5},{5,4},{6,7},{7,6},{8,9},{9,8},{10,11... | collective-permute-start | bytes 98312 | tf_op jit(solution)/shard_map/ppermute | solution.py:159
  16.8 1.4 %collective-permute-start.10 = (f32[4,16,512]{2,1,0:T(8,128)S(1)}, f32[4,16,512]{2,1,0:T(8,128)S(1)}, u32[]{:S(2)}, u32[]{:S(2)}) collective-permute-start(f32[4,16,512]{2,1,0:T(8,128)S(1)} %get-tuple-element.23), channel_id=1, source_target_pairs={{0,1},{1,0},{2,3},{3,2},{4,5},{5,4},{6,7},{7,6},{8,9},{9,8},{10,11... | collective-permute-start | bytes 393224 | tf_op jit(solution)/shard_map/ppermute | solution.py:159
  18.2 4.0 %collective-permute-start.11 = (bf16[4,16,512]{2,1,0:T(8,128)(2,1)S(1)}, bf16[4,16,512]{2,1,0:T(8,128)(2,1)S(1)}, u32[]{:S(2)}, u32[]{:S(2)}) collective-permute-start(bf16[4,16,512]{2,1,0:T(8,128)(2,1)S(1)} %get-tuple-element.35), channel_id=1, source_target_pairs={{0,3},{1,2},{2,1},{3,0},{4,7},{5,6},{6,5},{7,4},{8,11},{9,10},{10,... | collective-permute-start | bytes 196616 | tf_op jit(solution)/shard_map/ppermute | solution.py:159
  22.4 4.5 %collective-permute-start.12 = (bf16[3,16,512]{2,1,0:T(8,128)(2,1)S(1)}, bf16[3,16,512]{2,1,0:T(8,128)(2,1)S(1)}, u32[]{:S(2)}, u32[]{:S(2)}) collective-permute-start(bf16[3,16,512]{2,1,0:T(8,128)(2,1)S(1)} %get-tuple-element.26), channel_id=1, source_target_pairs={{0,4},{4,0},{8,12},{12,8},{1,5},{5,1},{9,13},{13,9},{2,6},{6,2},{1... | collective-permute-start | bytes 147464 | tf_op jit(solution)/shard_map/ppermute | solution.py:460
  22.9 7.1 %collective-permute-start.13 = (bf16[3,16,512]{2,1,0:T(8,128)(2,1)S(1)}, bf16[3,16,512]{2,1,0:T(8,128)(2,1)S(1)}, u32[]{:S(2)}, u32[]{:S(2)}) collective-permute-start(bf16[3,16,512]{2,1,0:T(8,128)(2,1)S(1)} %get-tuple-element.27), channel_id=1, source_target_pairs={{0,8},{4,12},{8,0},{12,4},{1,9},{5,13},{9,1},{13,5},{2,10},{6,14},... | collective-permute-start | bytes 147464 | tf_op jit(solution)/shard_map/ppermute | solution.py:460
  26.9 5.9 %collective-permute-start.14 = (bf16[3,16,512]{2,1,0:T(8,128)(2,1)S(1)}, bf16[3,16,512]{2,1,0:T(8,128)(2,1)S(1)}, u32[]{:S(2)}, u32[]{:S(2)}) collective-permute-start(bf16[3,16,512]{2,1,0:T(8,128)(2,1)S(1)} %get-tuple-element.28), channel_id=1, source_target_pairs={{0,12},{4,8},{8,4},{12,0},{1,13},{5,9},{9,5},{13,1},{2,14},{6,10},... | collective-permute-start | bytes 147464 | tf_op jit(solution)/shard_map/ppermute | solution.py:460
  26.9 5.9 %collective-permute-start.15 = (bf16[3,16,512]{2,1,0:T(8,128)(2,1)S(1)}, bf16[3,16,512]{2,1,0:T(8,128)(2,1)S(1)}, u32[]{:S(2)}, u32[]{:S(2)}) collective-permute-start(bf16[3,16,512]{2,1,0:T(8,128)(2,1)S(1)} %get-tuple-element.25.refs_0_), channel_id=1, source_target_pairs={{0,1},{1,0},{2,3},{3,2},{4,5},{5,4},{6,7},{7,6},{8,9},{9,8},{10,11... | collective-permute-start | bytes 147464 | tf_op jit(solution)/shard_map/ppermute | solution.py:159
  26.9 5.9 %collective-permute-start.16 = (bf16[3,16,512]{2,1,0:T(8,128)(2,1)S(1)}, bf16[3,16,512]{2,1,0:T(8,128)(2,1)S(1)}, u32[]{:S(2)}, u32[]{:S(2)}) collective-permute-start(bf16[3,16,512]{2,1,0:T(8,128)(2,1)S(1)} %collective-permute-done.12.refs_1_), channel_id=1, source_target_pairs={{0,1},{1,0},{2,3},{3,2},{4,5},{5,4},{6,7},{7,6},{8,9},{9,8},{10,11... | collective-permute-start | bytes 147464 | tf_op jit(solution)/shard_map/ppermute | solution.py:159
  30.1 2.7 %collective-permute-start.17 = (bf16[3,16,512]{2,1,0:T(8,128)(2,1)S(1)}, bf16[3,16,512]{2,1,0:T(8,128)(2,1)S(1)}, u32[]{:S(2)}, u32[]{:S(2)}) collective-permute-start(bf16[3,16,512]{2,1,0:T(8,128)(2,1)S(1)} %collective-permute-done.13.refs_2_), channel_id=1, source_target_pairs={{0,1},{1,0},{2,3},{3,2},{4,5},{5,4},{6,7},{7,6},{8,9},{9,8},{10,11... | collective-permute-start | bytes 147464 | tf_op jit(solution)/shard_map/ppermute | solution.py:159
  35.4 4.1 %collective-permute-start.20 = (bf16[4,4,16,128]{3,2,1,0:T(8,128)(2,1)S(1)}, bf16[4,4,16,128]{3,2,1,0:T(8,128)(2,1)S(1)}, u32[]{:S(2)}, u32[]{:S(2)}) collective-permute-start(bf16[4,4,16,128]{3,2,1,0:T(8,128)(2,1)S(1)} %get-tuple-element.29.refs_0_), channel_id=1, source_target_pairs={{0,3},{1,2},{2,1},{3,0},{4,7},{5,6},{6,5},{7,4},{8,11},{9,10},{10,... | collective-permute-start | bytes 196616 | tf_op jit(solution)/shard_map/ppermute | solution.py:159
  35.5 4.2 %collective-permute-start.19 = (bf16[4,4,16,128]{3,2,1,0:T(8,128)(2,1)S(1)}, bf16[4,4,16,128]{3,2,1,0:T(8,128)(2,1)S(1)}, u32[]{:S(2)}, u32[]{:S(2)}) collective-permute-start(bf16[4,4,16,128]{3,2,1,0:T(8,128)(2,1)S(1)} %get-tuple-element.29.refs_0_), channel_id=1, source_target_pairs={{0,1},{1,0},{2,3},{3,2},{4,5},{5,4},{6,7},{7,6},{8,9},{9,8},{10,11... | collective-permute-start | bytes 196616 | tf_op jit(solution)/shard_map/ppermute | solution.py:159
  39.6 1.3 %collective-permute-start.21 = (bf16[4,4,16,128]{3,2,1,0:T(8,128)(2,1)S(1)}, bf16[4,4,16,128]{3,2,1,0:T(8,128)(2,1)S(1)}, u32[]{:S(2)}, u32[]{:S(2)}) collective-permute-start(bf16[4,4,16,128]{3,2,1,0:T(8,128)(2,1)S(1)} %collective-permute-done.20.refs_3_), channel_id=1, source_target_pairs={{0,1},{1,0},{2,3},{3,2},{4,5},{5,4},{6,7},{7,6},{8,9},{9,8},{10,11... | collective-permute-start | bytes 196616 | tf_op jit(solution)/shard_map/ppermute | solution.py:159
  42.0 1.9 %collective-permute-start.22 = (bf16[32,128]{1,0:T(8,128)(2,1)S(1)}, bf16[32,128]{1,0:T(8,128)(2,1)S(1)}, u32[]{:S(2)}, u32[]{:S(2)}) collective-permute-start(bf16[32,128]{1,0:T(8,128)(2,1)S(1)} %get-tuple-element.32), channel_id=1, source_target_pairs={{0,1},{1,0},{2,3},{3,2},{4,5},{5,4},{6,7},{7,6},{8,9},{9,8},{10,11... | collective-permute-start | bytes 24584 | tf_op jit(solution)/shard_map/ppermute | solution.py:159
  42.3 3.7 %collective-permute-start.23 = (bf16[32,128]{1,0:T(8,128)(2,1)S(1)}, bf16[32,128]{1,0:T(8,128)(2,1)S(1)}, u32[]{:S(2)}, u32[]{:S(2)}) collective-permute-start(bf16[32,128]{1,0:T(8,128)(2,1)S(1)} %get-tuple-element.33), channel_id=1, source_target_pairs={{0,2},{1,3},{2,0},{3,1},{4,6},{5,7},{6,4},{7,5},{8,10},{9,11},{10,... | collective-permute-start | bytes 24584 | tf_op jit(solution)/shard_map/ppermute | solution.py:159
  42.5 3.4 %collective-permute-start.24 = (bf16[32,128]{1,0:T(8,128)(2,1)S(1)}, bf16[32,128]{1,0:T(8,128)(2,1)S(1)}, u32[]{:S(2)}, u32[]{:S(2)}) collective-permute-start(bf16[32,128]{1,0:T(8,128)(2,1)S(1)} %get-tuple-element.34), channel_id=1, source_target_pairs={{0,3},{1,2},{2,1},{3,0},{4,7},{5,6},{6,5},{7,4},{8,11},{9,10},{10,... | collective-permute-start | bytes 24584 | tf_op jit(solution)/shard_map/ppermute | solution.py:159
  (6 other events, 73.6 us)

commit v4 on v3

--- a/solution.py
+++ b/solution.py
@@ -233,13 +233,12 @@
 
 def mlp_body(count, columns, *refs):
     mixed, out_weight = refs[:count], refs[count : 2 * count - 1]
-    cells, weights, scales, kept_ref, sent_ref, first_ref, field = refs[2 * count - 1 :]
+    cells, weights, in_parts, scales, kept_ref, sent_ref, first_ref, field = refs[2 * count - 1 :]
     place = lax.axis_index("frame")
     tokens, width = cells.shape
     units = field.shape[1]
     share = mixed[0].shape[1]
-    starts = [3 * share, 4 * share, 4 * share + units, 4 * share + units + width]
-    own_out, down = weights[pl.ds(starts[0], share)], weights[pl.ds(starts[1], units)]
+    own_out, down = weights[pl.ds(3 * share, share)], weights[pl.ds(4 * share, units)]
     height = tokens // columns
     attn_out = sum(
         jnp.dot(a[...], b, preferred_element_type=jnp.float32)
@@ -250,7 +249,7 @@
     blank = jnp.zeros((columns, units), jnp.float32)
     spread = []
     for part in range(2):
-        inner = silu(jnp.dot(first, weights[pl.ds(starts[2 + part], width)], preferred_element_type=jnp.float32))
+        inner = silu(jnp.dot(first, in_parts[part], preferred_element_type=jnp.float32))
         field[pl.ds(0, columns)] = blank
         field[pl.ds(columns, tokens)] = inner.astype(jnp.bfloat16).astype(jnp.float32)
         field[pl.ds(columns + tokens, columns)] = blank
@@ -415,14 +414,8 @@
     for mask in masks:
         pieces[mask ^ 1] = swap(pieces[mask], 1)
     out_pieces = gathered_by_mask(out_weight)
-    weights = jnp.concatenate(
-        [
-            qkv_weight.reshape(3 * share, width),
-            out_weight,
-            down_weight,
-            jnp.transpose(in_weight, (1, 0, 2)).reshape(-1, units),
-        ]
-    )
+    weights = jnp.concatenate([qkv_weight.reshape(3 * share, width), out_weight, down_weight])
+    in_parts = jnp.transpose(in_weight, (1, 0, 2))
     taps = lax.dynamic_slice_in_dim(depth_weight, place * units, units, 3)
     scales = jnp.concatenate([taps.reshape(-1, units), attn_gain[None], mlp_gain[None]])
     mixed, cells = call(
@@ -438,6 +431,7 @@
             *out_pieces[1:],
             cells,
             weights,
+            in_parts,
             scales,
         ],
         [((half, columns, width), f32)] * 2 + [((half, columns, width), bf16)],
@@ -456,7 +450,7 @@
         flops=8 * total.size,
     )
     windows = list(windows)
-    for mask in range(1, count):
+    for mask in reversed(range(1, count)):
         windows[mask] = lax.ppermute(windows[mask], "row", [(i, i ^ mask) for i in range(count)])
     others = [swap(window, 1) for window in windows]
     hidden, own_part = call(

time: 46.7 us -> 47.2 us (1.011)
  starting transfers between devices: 19.4 us -> 23 us
  waiting for transfers between devices: 18.9 us -> 17.1 us
  local copies, waits for them, and re-layouts: 1.45 us -> 0.23 us
    ppermute x20, starting transfers between devices: 9.97 us -> 14.4 us  [swap(): return lax.ppermute(cells, 'frame', [(i, i ^ mask) for i in range(count)])]
    ppermute x3, waiting for transfers between devices: 5.37 us -> 2.94 us  [by_frames(): lax.ppermute(windows[mask], 'row', [(i, i ^ mask) for i in range(count)])]
    transpose x1 -> x0, local copies, waits for them, and re-layouts: 1.39 us -> none  [by_frames(): jnp.transpose(in_weight, (1, 0, 2)).reshape(-1, units)]
    ppermute x2, starting transfers between devices: 4.94 us -> 4.13 us  [by_frames(): pieces[mask] = lax.ppermute(own, ('row', 'frame'), pairs)]
    ppermute x2, waiting for transfers between devices: 0.01 us -> 0.78 us  [by_frames(): pieces[mask] = lax.ppermute(own, ('row', 'frame'), pairs)]
  transfers between devices with their start and end apart: 25 -> 25, of which waited for: 10 -> 15; matrix products, arithmetic and copies ran while one was open for 6% -> 3% of each run, Pallas kernels for 1% -> 1%
where the time goes in v4:
time: 47.2 us; the launch traced here: 47 us
  starting transfers between devices  23 us (49%)
  waiting for transfers between devices  17.1 us (36%)
  Pallas kernels  5.3 us (11%)
  other arithmetic  1.29 us (3%)
    ppermute x20, starting transfers between devices, swap(): return lax.ppermute(cells, 'frame', [(i, i ^ mask) for i in range(count)])  14.4 us
    ppermute x20, waiting for transfers between devices, swap(): return lax.ppermute(cells, 'frame', [(i, i ^ mask) for i in range(count)])  13.3 us
    pallas_call x6, Pallas kernels, call(): pl.pallas_call(body, out_shape=[jax.ShapeDtypeStruct(shape, kind) for sha...  5.3 us
    ppermute x3, starting transfers between devices, by_frames(): lax.ppermute(windows[mask], 'row', [(i, i ^ mask) for i in range(count)])  4.44 us
    ppermute x2, starting transfers between devices, by_frames(): pieces[mask] = lax.ppermute(own, ('row', 'frame'), pairs)  4.13 us
    ppermute x3, waiting for transfers between devices, by_frames(): lax.ppermute(windows[mask], 'row', [(i, i ^ mask) for i in range(count)])  2.94 us
    concatenate x1, other arithmetic, by_frames(): jnp.concatenate([qkv_weight.reshape(3 * share, width), out_weight, down_w...  1.26 us
  transfers between devices with their start and end apart: 25, of which 15 were waited for; matrix products, arithmetic and copies ran while one was open for 3% of the time, Pallas kernels for 1%

profile of v4, /device:TPU:0, one launch (start us, length us, event | category | flops | bytes accessed | tf_op | source)
XLA Modules:
  0.0 47.0 jit_solution(12424272167293690298)
XLA Ops:
  0.0 3.0 %collective-permute-start.2 = (bf16[32,512]{1,0:T(8,128)(2,1)}, bf16[32,512]{1,0:T(8,128)(2,1)S(1)}, u32[]{:S(2)}, u32[]{:S(2)}) collective-permute-start(bf16[32,512]{1,0:T(8,128)(2,1)} %bitcast.11), channel_id=1, source_target_pairs={{0,2},{1,6},{2,10},{3,14},{4,3},{5,7},{6,11},{7,15},{8,0},{9,4},{1... | collective-permute-start | bytes 98312 | tf_op jit(solution)/shard_map/ppermute | solution.py:413
  3.0 1.1 %collective-permute-start = (bf16[32,512]{1,0:T(8,128)(2,1)}, bf16[32,512]{1,0:T(8,128)(2,1)S(1)}, u32[]{:S(2)}, u32[]{:S(2)}) collective-permute-start(bf16[32,512]{1,0:T(8,128)(2,1)} %bitcast.12), channel_id=1, source_target_pairs={{0,1},{1,5},{2,9},{3,13},{4,0},{5,4},{6,8},{7,12},{8,3},{9,7},{10,... | collective-permute-start | bytes 98312 | tf_op jit(solution)/shard_map/ppermute | solution.py:413
  4.1 2.2 %collective-permute-start.8 = (bf16[128,512]{1,0:T(8,128)(2,1)}, bf16[128,512]{1,0:T(8,128)(2,1)S(1)}, u32[]{:S(2)}, u32[]{:S(2)}) collective-permute-start(bf16[128,512]{1,0:T(8,128)(2,1)} %param.12), channel_id=1, source_target_pairs={{0,3},{1,2},{2,1},{3,0},{4,7},{5,6},{6,5},{7,4},{8,11},{9,10},{10,... | collective-permute-start | bytes 393224 | tf_op jit(solution)/shard_map/ppermute | solution.py:159
  7.5 1.3 %pad_maximum_fusion.refs_4_.refs_8_ = bf16[1024,512]{1,0:T(8,128)(2,1)S(1)} fusion(bf16[512,512]{1,0:T(8,128)(2,1)} %param.16, bf16[128,512]{1,0:T(8,128)(2,1)} %param.12, bf16[384,512]{1,0:T(8,128)(2,1)} %bitcast.8), kind=kLoop, calls=%fused_computation | loop fusion | flops 3145728 | bytes 2097152 | tf_op jit(solution)/shard_map/concatenate | solution.py:417
  9.5 5.2 %collective-permute-start.5 = (bf16[128,128]{1,0:T(8,128)(2,1)S(1)}, bf16[128,128]{1,0:T(8,128)(2,1)S(1)}, u32[]{:S(2)}, u32[]{:S(2)}) collective-permute-start(bf16[128,128]{1,0:T(8,128)(2,1)S(1)} %get-tuple-element.20.refs_0_), channel_id=1, source_target_pairs={{0,3},{1,2},{2,1},{3,0},{4,7},{5,6},{6,5},{7,4},{8,11},{9,10},{10,... | collective-permute-start | bytes 98312 | tf_op jit(solution)/shard_map/ppermute | solution.py:159
  15.3 1.1 %collective-permute-done.5.refs_3_ = bf16[128,128]{1,0:T(8,128)(2,1)S(1)} collective-permute-done((bf16[128,128]{1,0:T(8,128)(2,1)S(1)}, bf16[128,128]{1,0:T(8,128)(2,1)S(1)}, u32[]{:S(2)}, u32[]{:S(2)}) %collective-permute-start.5) | collective-permute-done | bytes 32800 | tf_op jit(solution)/shard_map/ppermute | solution.py:159
  16.8 0.9 %collective-permute-done.6.refs_2_ = bf16[128,128]{1,0:T(8,128)(2,1)S(1)} collective-permute-done((bf16[128,128]{1,0:T(8,128)(2,1)S(1)}, bf16[128,128]{1,0:T(8,128)(2,1)S(1)}, u32[]{:S(2)}, u32[]{:S(2)}) %collective-permute-start.6) | collective-permute-done | bytes 32800 | tf_op jit(solution)/shard_map/ppermute | solution.py:159
  17.6 1.2 %shard_map.101 = (f32[4,16,512]{2,1,0:T(8,128)S(1)}, f32[4,16,512]{2,1,0:T(8,128)S(1)}, bf16[4,16,512]{2,1,0:T(8,128)(2,1)S(1)}) custom-call(bf16[128,128]{1,0:T(8,128)(2,1)S(1)} %get-tuple-element.20.refs_0_, bf16[128,128]{1,0:T(8,128)(2,1)S(1)} %collective-permute-done.4.refs_1_, bf16[128,128]{1,0:T(8,128)(2,1)S(1)} %collective-permute-done.6.refs_2_, ...), custom_call_target="tpu_custom_call" | custom-call | flops 268435456 | bytes 2793472 | tf_op jit(solution)/shard_map/pallas_call | solution.py:193
  19.1 1.2 %collective-permute-done.10 = f32[4,16,512]{2,1,0:T(8,128)S(1)} collective-permute-done((f32[4,16,512]{2,1,0:T(8,128)S(1)}, f32[4,16,512]{2,1,0:T(8,128)S(1)}, u32[]{:S(2)}, u32[]{:S(2)}) %collective-permute-start.10) | collective-permute-done | bytes 131104 | tf_op jit(solution)/shard_map/ppermute | solution.py:159
  20.3 1.7 %collective-permute-start.11 = (bf16[4,16,512]{2,1,0:T(8,128)(2,1)S(1)}, bf16[4,16,512]{2,1,0:T(8,128)(2,1)S(1)}, u32[]{:S(2)}, u32[]{:S(2)}) collective-permute-start(bf16[4,16,512]{2,1,0:T(8,128)(2,1)S(1)} %get-tuple-element.35), channel_id=1, source_target_pairs={{0,3},{1,2},{2,1},{3,0},{4,7},{5,6},{6,5},{7,4},{8,11},{9,10},{10,... | collective-permute-start | bytes 196616 | tf_op jit(solution)/shard_map/ppermute | solution.py:159
  22.0 2.5 %collective-permute-done.11.refs_3_ = bf16[4,16,512]{2,1,0:T(8,128)(2,1)S(1)} collective-permute-done((bf16[4,16,512]{2,1,0:T(8,128)(2,1)S(1)}, bf16[4,16,512]{2,1,0:T(8,128)(2,1)S(1)}, u32[]{:S(2)}, u32[]{:S(2)}) %collective-permute-start.11) | collective-permute-done | bytes 65568 | tf_op jit(solution)/shard_map/ppermute | solution.py:159
  24.7 1.6 %collective-permute-start.13 = (bf16[3,16,512]{2,1,0:T(8,128)(2,1)S(1)}, bf16[3,16,512]{2,1,0:T(8,128)(2,1)S(1)}, u32[]{:S(2)}, u32[]{:S(2)}) collective-permute-start(bf16[3,16,512]{2,1,0:T(8,128)(2,1)S(1)} %get-tuple-element.27), channel_id=1, source_target_pairs={{0,8},{4,12},{8,0},{12,4},{1,9},{5,13},{9,1},{13,5},{2,10},{6,14},... | collective-permute-start | bytes 147464 | tf_op jit(solution)/shard_map/ppermute | solution.py:454
  26.3 2.8 %collective-permute-start.14 = (bf16[3,16,512]{2,1,0:T(8,128)(2,1)S(1)}, bf16[3,16,512]{2,1,0:T(8,128)(2,1)S(1)}, u32[]{:S(2)}, u32[]{:S(2)}) collective-permute-start(bf16[3,16,512]{2,1,0:T(8,128)(2,1)S(1)} %get-tuple-element.28), channel_id=1, source_target_pairs={{0,12},{4,8},{8,4},{12,0},{1,13},{5,9},{9,5},{13,1},{2,14},{6,10},... | collective-permute-start | bytes 147464 | tf_op jit(solution)/shard_map/ppermute | solution.py:454
  29.6 1.9 %collective-permute-done.13.refs_2_ = bf16[3,16,512]{2,1,0:T(8,128)(2,1)S(1)} collective-permute-done((bf16[3,16,512]{2,1,0:T(8,128)(2,1)S(1)}, bf16[3,16,512]{2,1,0:T(8,128)(2,1)S(1)}, u32[]{:S(2)}, u32[]{:S(2)}) %collective-permute-start.13) | collective-permute-done | bytes 49184 | tf_op jit(solution)/shard_map/ppermute | solution.py:454
  31.5 0.7 %collective-permute-done.14.refs_3_ = bf16[3,16,512]{2,1,0:T(8,128)(2,1)S(1)} collective-permute-done((bf16[3,16,512]{2,1,0:T(8,128)(2,1)S(1)}, bf16[3,16,512]{2,1,0:T(8,128)(2,1)S(1)}, u32[]{:S(2)}, u32[]{:S(2)}) %collective-permute-start.14) | collective-permute-done | bytes 49184 | tf_op jit(solution)/shard_map/ppermute | solution.py:454
  32.8 0.7 %collective-permute-done.18.refs_7_ = bf16[3,16,512]{2,1,0:T(8,128)(2,1)S(1)} collective-permute-done((bf16[3,16,512]{2,1,0:T(8,128)(2,1)S(1)}, bf16[3,16,512]{2,1,0:T(8,128)(2,1)S(1)}, u32[]{:S(2)}, u32[]{:S(2)}) %collective-permute-start.18) | collective-permute-done | bytes 49184 | tf_op jit(solution)/shard_map/ppermute | solution.py:159
  33.5 1.4 %shard_map.103 = (bf16[4,4,16,128]{3,2,1,0:T(8,128)(2,1)S(1)}, bf16[4,2,16,128]{3,2,1,0:T(8,128)(2,1)S(1)}) custom-call(bf16[3,16,512]{2,1,0:T(8,128)(2,1)S(1)} %get-tuple-element.25.refs_0_, bf16[3,16,512]{2,1,0:T(8,128)(2,1)S(1)} %collective-permute-done.12.refs_1_, bf16[3,16,512]{2,1,0:T(8,128)(2,1)S(1)} %collective-permute-done.13.refs_2_, ...), custom_call_target="tpu_custom_call" | custom-call | flops 905969664 | bytes 3932160 | tf_op jit(solution)/shard_map/pallas_call | solution.py:193
  34.9 1.6 %collective-permute-start.20 = (bf16[4,4,16,128]{3,2,1,0:T(8,128)(2,1)S(1)}, bf16[4,4,16,128]{3,2,1,0:T(8,128)(2,1)S(1)}, u32[]{:S(2)}, u32[]{:S(2)}) collective-permute-start(bf16[4,4,16,128]{3,2,1,0:T(8,128)(2,1)S(1)} %get-tuple-element.29.refs_0_), channel_id=1, source_target_pairs={{0,3},{1,2},{2,1},{3,0},{4,7},{5,6},{6,5},{7,4},{8,11},{9,10},{10,... | collective-permute-start | bytes 196616 | tf_op jit(solution)/shard_map/ppermute | solution.py:159
  36.7 2.3 %collective-permute-done.20.refs_3_ = bf16[4,4,16,128]{3,2,1,0:T(8,128)(2,1)S(1)} collective-permute-done((bf16[4,4,16,128]{3,2,1,0:T(8,128)(2,1)S(1)}, bf16[4,4,16,128]{3,2,1,0:T(8,128)(2,1)S(1)}, u32[]{:S(2)}, u32[]{:S(2)}) %collective-permute-start.20) | collective-permute-done | bytes 65568 | tf_op jit(solution)/shard_map/ppermute | solution.py:159
  39.2 1.1 %collective-permute-done.21.refs_2_ = bf16[4,4,16,128]{3,2,1,0:T(8,128)(2,1)S(1)} collective-permute-done((bf16[4,4,16,128]{3,2,1,0:T(8,128)(2,1)S(1)}, bf16[4,4,16,128]{3,2,1,0:T(8,128)(2,1)S(1)}, u32[]{:S(2)}, u32[]{:S(2)}) %collective-permute-start.21) | collective-permute-done | bytes 65568 | tf_op jit(solution)/shard_map/ppermute | solution.py:159
  40.3 1.2 %shard_map.104 = (bf16[32,128]{1,0:T(8,128)(2,1)S(1)}, bf16[32,128]{1,0:T(8,128)(2,1)S(1)}, bf16[32,128]{1,0:T(8,128)(2,1)S(1)}, bf16[32,128]{1,0:T(8,128)(2,1)S(1)}) custom-call(bf16[4,4,16,128]{3,2,1,0:T(8,128)(2,1)S(1)} %get-tuple-element.29.refs_0_, bf16[4,4,16,128]{3,2,1,0:T(8,128)(2,1)S(1)} %collective-permute-done.19.refs_1_, ...), custom_call_target="tpu_custom_call" | custom-call | flops 452984832 | bytes 3833856 | tf_op jit(solution)/shard_map/pallas_call | solution.py:193
  41.7 1.6 %collective-permute-start.23 = (bf16[32,128]{1,0:T(8,128)(2,1)S(1)}, bf16[32,128]{1,0:T(8,128)(2,1)S(1)}, u32[]{:S(2)}, u32[]{:S(2)}) collective-permute-start(bf16[32,128]{1,0:T(8,128)(2,1)S(1)} %get-tuple-element.33), channel_id=1, source_target_pairs={{0,2},{1,3},{2,0},{3,1},{4,6},{5,7},{6,4},{7,5},{8,10},{9,11},{10,... | collective-permute-start | bytes 24584 | tf_op jit(solution)/shard_map/ppermute | solution.py:159
  43.4 2.0 %collective-permute-done.23.refs_2_ = bf16[32,128]{1,0:T(8,128)(2,1)S(1)} collective-permute-done((bf16[32,128]{1,0:T(8,128)(2,1)S(1)}, bf16[32,128]{1,0:T(8,128)(2,1)S(1)}, u32[]{:S(2)}, u32[]{:S(2)}) %collective-permute-start.23) | collective-permute-done | bytes 8224 | tf_op jit(solution)/shard_map/ppermute | solution.py:159
  45.4 1.0 %collective-permute-done.24.refs_3_ = bf16[32,128]{1,0:T(8,128)(2,1)S(1)} collective-permute-done((bf16[32,128]{1,0:T(8,128)(2,1)S(1)}, bf16[32,128]{1,0:T(8,128)(2,1)S(1)}, u32[]{:S(2)}, u32[]{:S(2)}) %collective-permute-start.24) | collective-permute-done | bytes 8224 | tf_op jit(solution)/shard_map/ppermute | solution.py:159
  (50 shorter events, 5.6 us)
Async XLA Ops:
  0.0 6.8 %collective-permute-start.2 = (bf16[32,512]{1,0:T(8,128)(2,1)}, bf16[32,512]{1,0:T(8,128)(2,1)S(1)}, u32[]{:S(2)}, u32[]{:S(2)}) collective-permute-start(bf16[32,512]{1,0:T(8,128)(2,1)} %bitcast.11), channel_id=1, source_target_pairs={{0,2},{1,6},{2,10},{3,14},{4,3},{5,7},{6,11},{7,15},{8,0},{9,4},{1... | collective-permute-start | bytes 98312 | tf_op jit(solution)/shard_map/ppermute | solution.py:413
  3.0 4.5 %collective-permute-start = (bf16[32,512]{1,0:T(8,128)(2,1)}, bf16[32,512]{1,0:T(8,128)(2,1)S(1)}, u32[]{:S(2)}, u32[]{:S(2)}) collective-permute-start(bf16[32,512]{1,0:T(8,128)(2,1)} %bitcast.12), channel_id=1, source_target_pairs={{0,1},{1,5},{2,9},{3,13},{4,0},{5,4},{6,8},{7,12},{8,3},{9,7},{10,... | collective-permute-start | bytes 98312 | tf_op jit(solution)/shard_map/ppermute | solution.py:413
  4.1 10.5 %collective-permute-start.8 = (bf16[128,512]{1,0:T(8,128)(2,1)}, bf16[128,512]{1,0:T(8,128)(2,1)S(1)}, u32[]{:S(2)}, u32[]{:S(2)}) collective-permute-start(bf16[128,512]{1,0:T(8,128)(2,1)} %param.12), channel_id=1, source_target_pairs={{0,3},{1,2},{2,1},{3,0},{4,7},{5,6},{6,5},{7,4},{8,11},{9,10},{10,... | collective-permute-start | bytes 393224 | tf_op jit(solution)/shard_map/ppermute | solution.py:159
  6.3 10.4 %collective-permute-start.7 = (bf16[128,512]{1,0:T(8,128)(2,1)}, bf16[128,512]{1,0:T(8,128)(2,1)S(1)}, u32[]{:S(2)}, u32[]{:S(2)}) collective-permute-start(bf16[128,512]{1,0:T(8,128)(2,1)} %param.12), channel_id=1, source_target_pairs={{0,1},{1,0},{2,3},{3,2},{4,5},{5,4},{6,7},{7,6},{8,9},{9,8},{10,11... | collective-permute-start | bytes 393224 | tf_op jit(solution)/shard_map/ppermute | solution.py:159
  6.8 2.0 %collective-permute-start.3 = (bf16[32,512]{1,0:T(8,128)(2,1)S(1)}, bf16[32,512]{1,0:T(8,128)(2,1)S(1)}, u32[]{:S(2)}, u32[]{:S(2)}) collective-permute-start(bf16[32,512]{1,0:T(8,128)(2,1)S(1)} %collective-permute-done.2.refs_2_), channel_id=1, source_target_pairs={{0,1},{1,0},{2,3},{3,2},{4,5},{5,4},{6,7},{7,6},{8,9},{9,8},{10,11... | collective-permute-start | bytes 98312 | tf_op jit(solution)/shard_map/ppermute | solution.py:159
  7.5 1.3 %collective-permute-start.1 = (bf16[32,512]{1,0:T(8,128)(2,1)S(1)}, bf16[32,512]{1,0:T(8,128)(2,1)S(1)}, u32[]{:S(2)}, u32[]{:S(2)}) collective-permute-start(bf16[32,512]{1,0:T(8,128)(2,1)S(1)} %collective-permute-done.refs_1_), channel_id=1, source_target_pairs={{0,1},{1,0},{2,3},{3,2},{4,5},{5,4},{6,7},{7,6},{8,9},{9,8},{10,11... | collective-permute-start | bytes 98312 | tf_op jit(solution)/shard_map/ppermute | solution.py:159
  9.5 7.0 %collective-permute-start.5 = (bf16[128,128]{1,0:T(8,128)(2,1)S(1)}, bf16[128,128]{1,0:T(8,128)(2,1)S(1)}, u32[]{:S(2)}, u32[]{:S(2)}) collective-permute-start(bf16[128,128]{1,0:T(8,128)(2,1)S(1)} %get-tuple-element.20.refs_0_), channel_id=1, source_target_pairs={{0,3},{1,2},{2,1},{3,0},{4,7},{5,6},{6,5},{7,4},{8,11},{9,10},{10,... | collective-permute-start | bytes 98312 | tf_op jit(solution)/shard_map/ppermute | solution.py:159
  14.7 3.0 %collective-permute-start.9 = (bf16[128,512]{1,0:T(8,128)(2,1)S(1)}, bf16[128,512]{1,0:T(8,128)(2,1)S(1)}, u32[]{:S(2)}, u32[]{:S(2)}) collective-permute-start(bf16[128,512]{1,0:T(8,128)(2,1)S(1)} %collective-permute-done.8.refs_6_), channel_id=1, source_target_pairs={{0,1},{1,0},{2,3},{3,2},{4,5},{5,4},{6,7},{7,6},{8,9},{9,8},{10,11... | collective-permute-start | bytes 393224 | tf_op jit(solution)/shard_map/ppermute | solution.py:159
  14.7 2.0 %collective-permute-start.4 = (bf16[128,128]{1,0:T(8,128)(2,1)S(1)}, bf16[128,128]{1,0:T(8,128)(2,1)S(1)}, u32[]{:S(2)}, u32[]{:S(2)}) collective-permute-start(bf16[128,128]{1,0:T(8,128)(2,1)S(1)} %get-tuple-element.20.refs_0_), channel_id=1, source_target_pairs={{0,1},{1,0},{2,3},{3,2},{4,5},{5,4},{6,7},{7,6},{8,9},{9,8},{10,11... | collective-permute-start | bytes 98312 | tf_op jit(solution)/shard_map/ppermute | solution.py:159
  18.9 1.4 %collective-permute-start.10 = (f32[4,16,512]{2,1,0:T(8,128)S(1)}, f32[4,16,512]{2,1,0:T(8,128)S(1)}, u32[]{:S(2)}, u32[]{:S(2)}) collective-permute-start(f32[4,16,512]{2,1,0:T(8,128)S(1)} %get-tuple-element.23), channel_id=1, source_target_pairs={{0,1},{1,0},{2,3},{3,2},{4,5},{5,4},{6,7},{7,6},{8,9},{9,8},{10,11... | collective-permute-start | bytes 393224 | tf_op jit(solution)/shard_map/ppermute | solution.py:159
  20.3 4.2 %collective-permute-start.11 = (bf16[4,16,512]{2,1,0:T(8,128)(2,1)S(1)}, bf16[4,16,512]{2,1,0:T(8,128)(2,1)S(1)}, u32[]{:S(2)}, u32[]{:S(2)}) collective-permute-start(bf16[4,16,512]{2,1,0:T(8,128)(2,1)S(1)} %get-tuple-element.35), channel_id=1, source_target_pairs={{0,3},{1,2},{2,1},{3,0},{4,7},{5,6},{6,5},{7,4},{8,11},{9,10},{10,... | collective-permute-start | bytes 196616 | tf_op jit(solution)/shard_map/ppermute | solution.py:159
  24.6 4.8 %collective-permute-start.12 = (bf16[3,16,512]{2,1,0:T(8,128)(2,1)S(1)}, bf16[3,16,512]{2,1,0:T(8,128)(2,1)S(1)}, u32[]{:S(2)}, u32[]{:S(2)}) collective-permute-start(bf16[3,16,512]{2,1,0:T(8,128)(2,1)S(1)} %get-tuple-element.26), channel_id=1, source_target_pairs={{0,4},{4,0},{8,12},{12,8},{1,5},{5,1},{9,13},{13,9},{2,6},{6,2},{1... | collective-permute-start | bytes 147464 | tf_op jit(solution)/shard_map/ppermute | solution.py:454
  24.7 6.8 %collective-permute-start.13 = (bf16[3,16,512]{2,1,0:T(8,128)(2,1)S(1)}, bf16[3,16,512]{2,1,0:T(8,128)(2,1)S(1)}, u32[]{:S(2)}, u32[]{:S(2)}) collective-permute-start(bf16[3,16,512]{2,1,0:T(8,128)(2,1)S(1)} %get-tuple-element.27), channel_id=1, source_target_pairs={{0,8},{4,12},{8,0},{12,4},{1,9},{5,13},{9,1},{13,5},{2,10},{6,14},... | collective-permute-start | bytes 147464 | tf_op jit(solution)/shard_map/ppermute | solution.py:454
  26.3 5.9 %collective-permute-start.14 = (bf16[3,16,512]{2,1,0:T(8,128)(2,1)S(1)}, bf16[3,16,512]{2,1,0:T(8,128)(2,1)S(1)}, u32[]{:S(2)}, u32[]{:S(2)}) collective-permute-start(bf16[3,16,512]{2,1,0:T(8,128)(2,1)S(1)} %get-tuple-element.28), channel_id=1, source_target_pairs={{0,12},{4,8},{8,4},{12,0},{1,13},{5,9},{9,5},{13,1},{2,14},{6,10},... | collective-permute-start | bytes 147464 | tf_op jit(solution)/shard_map/ppermute | solution.py:454
  29.1 3.1 %collective-permute-start.15 = (bf16[3,16,512]{2,1,0:T(8,128)(2,1)S(1)}, bf16[3,16,512]{2,1,0:T(8,128)(2,1)S(1)}, u32[]{:S(2)}, u32[]{:S(2)}) collective-permute-start(bf16[3,16,512]{2,1,0:T(8,128)(2,1)S(1)} %get-tuple-element.25.refs_0_), channel_id=1, source_target_pairs={{0,1},{1,0},{2,3},{3,2},{4,5},{5,4},{6,7},{7,6},{8,9},{9,8},{10,11... | collective-permute-start | bytes 147464 | tf_op jit(solution)/shard_map/ppermute | solution.py:159
  29.4 2.8 %collective-permute-start.16 = (bf16[3,16,512]{2,1,0:T(8,128)(2,1)S(1)}, bf16[3,16,512]{2,1,0:T(8,128)(2,1)S(1)}, u32[]{:S(2)}, u32[]{:S(2)}) collective-permute-start(bf16[3,16,512]{2,1,0:T(8,128)(2,1)S(1)} %collective-permute-done.12.refs_1_), channel_id=1, source_target_pairs={{0,1},{1,0},{2,3},{3,2},{4,5},{5,4},{6,7},{7,6},{8,9},{9,8},{10,11... | collective-permute-start | bytes 147464 | tf_op jit(solution)/shard_map/ppermute | solution.py:159
  31.5 1.2 %collective-permute-start.17 = (bf16[3,16,512]{2,1,0:T(8,128)(2,1)S(1)}, bf16[3,16,512]{2,1,0:T(8,128)(2,1)S(1)}, u32[]{:S(2)}, u32[]{:S(2)}) collective-permute-start(bf16[3,16,512]{2,1,0:T(8,128)(2,1)S(1)} %collective-permute-done.13.refs_2_), channel_id=1, source_target_pairs={{0,1},{1,0},{2,3},{3,2},{4,5},{5,4},{6,7},{7,6},{8,9},{9,8},{10,11... | collective-permute-start | bytes 147464 | tf_op jit(solution)/shard_map/ppermute | solution.py:159
  32.2 1.2 %collective-permute-start.18 = (bf16[3,16,512]{2,1,0:T(8,128)(2,1)S(1)}, bf16[3,16,512]{2,1,0:T(8,128)(2,1)S(1)}, u32[]{:S(2)}, u32[]{:S(2)}) collective-permute-start(bf16[3,16,512]{2,1,0:T(8,128)(2,1)S(1)} %collective-permute-done.14.refs_3_), channel_id=1, source_target_pairs={{0,1},{1,0},{2,3},{3,2},{4,5},{5,4},{6,7},{7,6},{8,9},{9,8},{10,11... | collective-permute-start | bytes 147464 | tf_op jit(solution)/shard_map/ppermute | solution.py:159
  34.9 4.1 %collective-permute-start.20 = (bf16[4,4,16,128]{3,2,1,0:T(8,128)(2,1)S(1)}, bf16[4,4,16,128]{3,2,1,0:T(8,128)(2,1)S(1)}, u32[]{:S(2)}, u32[]{:S(2)}) collective-permute-start(bf16[4,4,16,128]{3,2,1,0:T(8,128)(2,1)S(1)} %get-tuple-element.29.refs_0_), channel_id=1, source_target_pairs={{0,3},{1,2},{2,1},{3,0},{4,7},{5,6},{6,5},{7,4},{8,11},{9,10},{10,... | collective-permute-start | bytes 196616 | tf_op jit(solution)/shard_map/ppermute | solution.py:159
  36.5 2.6 %collective-permute-start.19 = (bf16[4,4,16,128]{3,2,1,0:T(8,128)(2,1)S(1)}, bf16[4,4,16,128]{3,2,1,0:T(8,128)(2,1)S(1)}, u32[]{:S(2)}, u32[]{:S(2)}) collective-permute-start(bf16[4,4,16,128]{3,2,1,0:T(8,128)(2,1)S(1)} %get-tuple-element.29.refs_0_), channel_id=1, source_target_pairs={{0,1},{1,0},{2,3},{3,2},{4,5},{5,4},{6,7},{7,6},{8,9},{9,8},{10,11... | collective-permute-start | bytes 196616 | tf_op jit(solution)/shard_map/ppermute | solution.py:159
  39.0 1.3 %collective-permute-start.21 = (bf16[4,4,16,128]{3,2,1,0:T(8,128)(2,1)S(1)}, bf16[4,4,16,128]{3,2,1,0:T(8,128)(2,1)S(1)}, u32[]{:S(2)}, u32[]{:S(2)}) collective-permute-start(bf16[4,4,16,128]{3,2,1,0:T(8,128)(2,1)S(1)} %collective-permute-done.20.refs_3_), channel_id=1, source_target_pairs={{0,1},{1,0},{2,3},{3,2},{4,5},{5,4},{6,7},{7,6},{8,9},{9,8},{10,11... | collective-permute-start | bytes 196616 | tf_op jit(solution)/shard_map/ppermute | solution.py:159
  41.5 1.9 %collective-permute-start.22 = (bf16[32,128]{1,0:T(8,128)(2,1)S(1)}, bf16[32,128]{1,0:T(8,128)(2,1)S(1)}, u32[]{:S(2)}, u32[]{:S(2)}) collective-permute-start(bf16[32,128]{1,0:T(8,128)(2,1)S(1)} %get-tuple-element.32), channel_id=1, source_target_pairs={{0,1},{1,0},{2,3},{3,2},{4,5},{5,4},{6,7},{7,6},{8,9},{9,8},{10,11... | collective-permute-start | bytes 24584 | tf_op jit(solution)/shard_map/ppermute | solution.py:159
  41.7 3.7 %collective-permute-start.23 = (bf16[32,128]{1,0:T(8,128)(2,1)S(1)}, bf16[32,128]{1,0:T(8,128)(2,1)S(1)}, u32[]{:S(2)}, u32[]{:S(2)}) collective-permute-start(bf16[32,128]{1,0:T(8,128)(2,1)S(1)} %get-tuple-element.33), channel_id=1, source_target_pairs={{0,2},{1,3},{2,0},{3,1},{4,6},{5,7},{6,4},{7,5},{8,10},{9,11},{10,... | collective-permute-start | bytes 24584 | tf_op jit(solution)/shard_map/ppermute | solution.py:159
  43.3 3.1 %collective-permute-start.24 = (bf16[32,128]{1,0:T(8,128)(2,1)S(1)}, bf16[32,128]{1,0:T(8,128)(2,1)S(1)}, u32[]{:S(2)}, u32[]{:S(2)}) collective-permute-start(bf16[32,128]{1,0:T(8,128)(2,1)S(1)} %get-tuple-element.34), channel_id=1, source_target_pairs={{0,3},{1,2},{2,1},{3,0},{4,7},{5,6},{6,5},{7,4},{8,11},{9,10},{10,... | collective-permute-start | bytes 24584 | tf_op jit(solution)/shard_map/ppermute | solution.py:159
  (7 other events, 98.0 us)

commit v5 on v4

--- a/solution.py
+++ b/solution.py
@@ -291,7 +291,7 @@
     framed[rows + 1] = blank
     framed[1 : rows + 1] = second.astype(jnp.bfloat16)
     for mask, out in enumerate(outs):
-        out[...] = framed[pl.ds((level ^ mask) * step, step + 2)]
+        out[...] = framed[pl.ds(lax.rem(level + mask, len(outs)) * step, step + 2)]
 
 
 def conv_rows(field, kernel):
@@ -329,7 +329,7 @@
     level, place = lax.axis_index("row"), lax.axis_index("frame")
     clear_ends(field)
     for index, piece in enumerate(pieces):
-        frame = (level ^ (index % count)) + 1
+        frame = lax.rem(level + count - index % count, count) + 1
         parity = half_of(place) ^ (index // count)
         for row in range(piece.shape[0]):
             field[frame, 2 * row + parity] = piece[row]
@@ -358,7 +358,7 @@
     lines = final.shape[0] * final.shape[1]
     strip = outs[0].shape[0] // lines
     for mask, out in enumerate(outs):
-        at = pl.multiple_of((place ^ mask) * strip, strip)
+        at = pl.multiple_of(lax.rem(place + mask, len(outs)) * strip, strip)
         out[...] = jnp.concatenate(
             [
                 final[line // final.shape[1], line % final.shape[1], pl.ds(at, strip)]
@@ -374,7 +374,7 @@
     share = pieces[0].shape[1]
     frames, rows, strip = out_ref.shape[:3]
     for mask, piece in enumerate(pieces):
-        at = pl.multiple_of((place ^ mask) * share, share)
+        at = pl.multiple_of(lax.rem(place + len(pieces) - mask, len(pieces)) * share, share)
         cells = piece[...].astype(jnp.float32)
         for line in range(frames * rows):
             out_ref[line // rows, line % rows, :, pl.ds(at, share)] = cells[
@@ -405,17 +405,18 @@
     bf16, f32 = jnp.bfloat16, jnp.float32
     own = latent.reshape(rows * columns, width)
     pieces = [None] * count
-    masks = [1] + list(range(2, count, 2))
+    masks = [*range(3, count, 2), 1]
     for mask in masks:
         pairs = [
             (z * count + f, f * count + (z ^ mask)) for z in range(count) for f in range(count)
         ]
         pieces[mask] = lax.ppermute(own, ("row", "frame"), pairs)
-    for mask in masks:
-        pieces[mask ^ 1] = swap(pieces[mask], 1)
-    out_pieces = gathered_by_mask(out_weight)
     weights = jnp.concatenate([qkv_weight.reshape(3 * share, width), out_weight, down_weight])
     in_parts = jnp.transpose(in_weight, (1, 0, 2))
+    *arrived, weights = lax.optimization_barrier((*[pieces[mask] for mask in masks], weights))
+    for mask, piece in zip(masks, arrived):
+        pieces[mask], pieces[mask ^ 1] = piece, swap(piece, 1)
+    out_pieces = gathered_by_mask(out_weight)
     taps = lax.dynamic_slice_in_dim(depth_weight, place * units, units, 3)
     scales = jnp.concatenate([taps.reshape(-1, units), attn_gain[None], mlp_gain[None]])
     mixed, cells = call(
@@ -450,8 +451,9 @@
         flops=8 * total.size,
     )
     windows = list(windows)
-    for mask in reversed(range(1, count)):
-        windows[mask] = lax.ppermute(windows[mask], "row", [(i, i ^ mask) for i in range(count)])
+    for mask in (1, 2, 3):
+        pairs = [(i, (i + mask) % count) for i in range(count)]
+        windows[mask] = lax.ppermute(windows[mask], "row", pairs)
     others = [swap(window, 1) for window in windows]
     hidden, own_part = call(
         functools.partial(first_conv_body, height),
@@ -473,7 +475,10 @@
         flops=2 * count * rows * columns * 27 * width * share,
         room=8,
     )
-    outs = [strips[0]] + [swap(strips[mask], mask) for mask in range(1, count)]
+    outs = list(strips)
+    for mask in (2, 1, 3):
+        pairs = [(i, (i + mask) % count) for i in range(count)]
+        outs[mask] = lax.ppermute(strips[mask], "frame", pairs)
     (decoded,) = call(join_body, outs, [((count, rows, strip, width), bf16)])
     return decoded
 

time: 47.2 us -> 45.1 us (0.956)
  starting transfers between devices: 23 us -> 21.1 us
    ppermute x20 -> x17, starting transfers between devices: 14.4 us -> 8.22 us  [swap(): return lax.ppermute(cells, 'frame', [(i, i ^ mask) for i in range(count)])]
    ppermute x20 -> x17, waiting for transfers between devices: 13.3 us -> 10.1 us  [swap(): return lax.ppermute(cells, 'frame', [(i, i ^ mask) for i in range(count)])]
    ppermute x3 -> x6, starting transfers between devices: 4.44 us -> 7.1 us  [the longest x3 4.01 us: by_frames(): windows[mask] = lax.ppermute(windows[mask], 'row', pairs)]
    ppermute x3 -> x6, waiting for transfers between devices: 2.94 us -> 5.44 us  [the longest x3 4.08 us: by_frames(): windows[mask] = lax.ppermute(windows[mask], 'row', pairs)]
    ppermute x2, starting transfers between devices: 4.13 us -> 5.74 us  [by_frames(): pieces[mask] = lax.ppermute(own, ('row', 'frame'), pairs)]
    ppermute x2, waiting for transfers between devices: 0.78 us -> 1.35 us  [by_frames(): pieces[mask] = lax.ppermute(own, ('row', 'frame'), pairs)]
  transfers between devices with their start and end apart: 25 -> 25, of which waited for: 15 -> 16; matrix products, arithmetic and copies ran while one was open for 3% -> 3% of each run, Pallas kernels for 1% -> 1%
where the time goes in v5:
time: 45.1 us; the launch traced here: 44.9 us
  starting transfers between devices  21.1 us (47%)
  waiting for transfers between devices  16.9 us (37%)
  Pallas kernels  5.3 us (12%)
  other arithmetic  1.29 us (3%)
    ppermute x17, waiting for transfers between devices, swap(): return lax.ppermute(cells, 'frame', [(i, i ^ mask) for i in range(count)])  10.1 us
    ppermute x17, starting transfers between devices, swap(): return lax.ppermute(cells, 'frame', [(i, i ^ mask) for i in range(count)])  8.22 us
    ppermute x2, starting transfers between devices, by_frames(): pieces[mask] = lax.ppermute(own, ('row', 'frame'), pairs)  5.74 us
    pallas_call x6, Pallas kernels, call(): pl.pallas_call(body, out_shape=[jax.ShapeDtypeStruct(shape, kind) for sha...  5.3 us
    ppermute x3, waiting for transfers between devices, by_frames(): windows[mask] = lax.ppermute(windows[mask], 'row', pairs)  4.08 us
    ppermute x3, starting transfers between devices, by_frames(): windows[mask] = lax.ppermute(windows[mask], 'row', pairs)  4.01 us
    ppermute x3, starting transfers between devices, by_frames(): outs[mask] = lax.ppermute(strips[mask], 'frame', pairs)  3.1 us
    ppermute x3, waiting for transfers between devices, by_frames(): outs[mask] = lax.ppermute(strips[mask], 'frame', pairs)  1.37 us
  transfers between devices with their start and end apart: 25, of which 16 were waited for; matrix products, arithmetic and copies ran while one was open for 3% of the time, Pallas kernels for 1%

profile of v5, /device:TPU:0, one launch (start us, length us, event | category | flops | bytes accessed | tf_op | source)
XLA Modules:
  0.0 44.9 jit_solution(5128506789800249628)
XLA Ops:
  0.5 5.2 %collective-permute-start = (bf16[32,512]{1,0:T(8,128)(2,1)}, bf16[32,512]{1,0:T(8,128)(2,1)S(1)}, u32[]{:S(2)}, u32[]{:S(2)}) collective-permute-start(bf16[32,512]{1,0:T(8,128)(2,1)} %bitcast.12), channel_id=1, source_target_pairs={{0,3},{1,7},{2,11},{3,15},{4,2},{5,6},{6,10},{7,14},{8,1},{9,5},{1... | collective-permute-start | bytes 98312 | tf_op jit(solution)/shard_map/ppermute | solution.py:413
  5.8 0.7 %collective-permute-start.8 = (bf16[128,512]{1,0:T(8,128)(2,1)}, bf16[128,512]{1,0:T(8,128)(2,1)S(1)}, u32[]{:S(2)}, u32[]{:S(2)}) collective-permute-start(bf16[128,512]{1,0:T(8,128)(2,1)} %param.12), channel_id=1, source_target_pairs={{0,3},{1,2},{2,1},{3,0},{4,7},{5,6},{6,5},{7,4},{8,11},{9,10},{10,... | collective-permute-start | bytes 393224 | tf_op jit(solution)/shard_map/ppermute | solution.py:159
  6.5 1.3 %pad_maximum_fusion.refs_4_.refs_8_ = bf16[1024,512]{1,0:T(8,128)(2,1)S(1)} fusion(bf16[512,512]{1,0:T(8,128)(2,1)} %param.16, bf16[128,512]{1,0:T(8,128)(2,1)} %param.12, bf16[384,512]{1,0:T(8,128)(2,1)} %bitcast.8), kind=kLoop, calls=%fused_computation | loop fusion | flops 3145728 | bytes 2097152 | tf_op jit(solution)/shard_map/concatenate | solution.py:414
  7.7 1.3 %collective-permute-done.refs_3_ = bf16[32,512]{1,0:T(8,128)(2,1)S(1)} collective-permute-done((bf16[32,512]{1,0:T(8,128)(2,1)}, bf16[32,512]{1,0:T(8,128)(2,1)S(1)}, u32[]{:S(2)}, u32[]{:S(2)}) %collective-permute-start) | collective-permute-done | bytes 32800 | tf_op jit(solution)/shard_map/ppermute | solution.py:413
  9.6 0.7 %collective-permute-done.2.refs_0_ = bf16[32,512]{1,0:T(8,128)(2,1)S(1)} collective-permute-done((bf16[32,512]{1,0:T(8,128)(2,1)S(1)}, bf16[32,512]{1,0:T(8,128)(2,1)S(1)}, u32[]{:S(2)}, u32[]{:S(2)}) %collective-permute-start.2) | collective-permute-done | bytes 32800 | tf_op jit(solution)/shard_map/ppermute | solution.py:159
  10.5 0.7 %shard_map.100 = (bf16[128,128]{1,0:T(8,128)(2,1)S(1)}, bf16[128,512]{1,0:T(8,128)(2,1)S(1)}) custom-call(bf16[32,512]{1,0:T(8,128)(2,1)S(1)} %collective-permute-done.2.refs_0_, bf16[32,512]{1,0:T(8,128)(2,1)S(1)} %collective-permute-done.1.refs_1_, bf16[32,512]{1,0:T(8,128)(2,1)S(1)} %collective-permute-done.3.refs_2_, ...), custom_call_target="tpu_custom_call" | custom-call | flops 50331648 | bytes 1179648 | tf_op jit(solution)/shard_map/pallas_call | solution.py:193
  11.1 1.6 %collective-permute-start.5 = (bf16[128,128]{1,0:T(8,128)(2,1)S(1)}, bf16[128,128]{1,0:T(8,128)(2,1)S(1)}, u32[]{:S(2)}, u32[]{:S(2)}) collective-permute-start(bf16[128,128]{1,0:T(8,128)(2,1)S(1)} %get-tuple-element.26.refs_0_), channel_id=1, source_target_pairs={{0,3},{1,2},{2,1},{3,0},{4,7},{5,6},{6,5},{7,4},{8,11},{9,10},{10,... | collective-permute-start | bytes 98312 | tf_op jit(solution)/shard_map/ppermute | solution.py:159
  13.4 1.2 %collective-permute-done.5.refs_3_ = bf16[128,128]{1,0:T(8,128)(2,1)S(1)} collective-permute-done((bf16[128,128]{1,0:T(8,128)(2,1)S(1)}, bf16[128,128]{1,0:T(8,128)(2,1)S(1)}, u32[]{:S(2)}, u32[]{:S(2)}) %collective-permute-start.5) | collective-permute-done | bytes 32800 | tf_op jit(solution)/shard_map/ppermute | solution.py:159
  15.8 1.2 %shard_map.101 = (f32[4,16,512]{2,1,0:T(8,128)S(1)}, f32[4,16,512]{2,1,0:T(8,128)S(1)}, bf16[4,16,512]{2,1,0:T(8,128)(2,1)S(1)}) custom-call(bf16[128,128]{1,0:T(8,128)(2,1)S(1)} %get-tuple-element.26.refs_0_, bf16[128,128]{1,0:T(8,128)(2,1)S(1)} %collective-permute-done.4.refs_1_, bf16[128,128]{1,0:T(8,128)(2,1)S(1)} %collective-permute-done.6.refs_2_, ...), custom_call_target="tpu_custom_call" | custom-call | flops 268435456 | bytes 2793472 | tf_op jit(solution)/shard_map/pallas_call | solution.py:193
  17.4 1.0 %collective-permute-done.10 = f32[4,16,512]{2,1,0:T(8,128)S(1)} collective-permute-done((f32[4,16,512]{2,1,0:T(8,128)S(1)}, f32[4,16,512]{2,1,0:T(8,128)S(1)}, u32[]{:S(2)}, u32[]{:S(2)}) %collective-permute-start.10) | collective-permute-done | bytes 131104 | tf_op jit(solution)/shard_map/ppermute | solution.py:159
  18.4 1.6 %collective-permute-start.11 = (bf16[4,16,512]{2,1,0:T(8,128)(2,1)S(1)}, bf16[4,16,512]{2,1,0:T(8,128)(2,1)S(1)}, u32[]{:S(2)}, u32[]{:S(2)}) collective-permute-start(bf16[4,16,512]{2,1,0:T(8,128)(2,1)S(1)} %get-tuple-element.41), channel_id=1, source_target_pairs={{0,3},{1,2},{2,1},{3,0},{4,7},{5,6},{6,5},{7,4},{8,11},{9,10},{10,... | collective-permute-start | bytes 196616 | tf_op jit(solution)/shard_map/ppermute | solution.py:159
  20.0 2.4 %collective-permute-done.11.refs_3_ = bf16[4,16,512]{2,1,0:T(8,128)(2,1)S(1)} collective-permute-done((bf16[4,16,512]{2,1,0:T(8,128)(2,1)S(1)}, bf16[4,16,512]{2,1,0:T(8,128)(2,1)S(1)}, u32[]{:S(2)}, u32[]{:S(2)}) %collective-permute-start.11) | collective-permute-done | bytes 65568 | tf_op jit(solution)/shard_map/ppermute | solution.py:159
  22.7 3.6 %collective-permute-start.13 = (bf16[3,16,512]{2,1,0:T(8,128)(2,1)S(1)}, bf16[3,16,512]{2,1,0:T(8,128)(2,1)S(1)}, u32[]{:S(2)}, u32[]{:S(2)}) collective-permute-start(bf16[3,16,512]{2,1,0:T(8,128)(2,1)S(1)} %get-tuple-element.33), channel_id=1, source_target_pairs={{0,8},{4,12},{8,0},{12,4},{1,9},{5,13},{9,1},{13,5},{2,10},{6,14},... | collective-permute-start | bytes 147464 | tf_op jit(solution)/shard_map/ppermute | solution.py:456
  26.6 2.6 %collective-permute-done.12.refs_1_ = bf16[3,16,512]{2,1,0:T(8,128)(2,1)S(1)} collective-permute-done((bf16[3,16,512]{2,1,0:T(8,128)(2,1)S(1)}, bf16[3,16,512]{2,1,0:T(8,128)(2,1)S(1)}, u32[]{:S(2)}, u32[]{:S(2)}) %collective-permute-start.12) | collective-permute-done | bytes 49184 | tf_op jit(solution)/shard_map/ppermute | solution.py:456
  29.1 1.4 %collective-permute-done.13.refs_2_ = bf16[3,16,512]{2,1,0:T(8,128)(2,1)S(1)} collective-permute-done((bf16[3,16,512]{2,1,0:T(8,128)(2,1)S(1)}, bf16[3,16,512]{2,1,0:T(8,128)(2,1)S(1)}, u32[]{:S(2)}, u32[]{:S(2)}) %collective-permute-start.13) | collective-permute-done | bytes 49184 | tf_op jit(solution)/shard_map/ppermute | solution.py:456
  31.1 0.7 %collective-permute-done.17.refs_6_ = bf16[3,16,512]{2,1,0:T(8,128)(2,1)S(1)} collective-permute-done((bf16[3,16,512]{2,1,0:T(8,128)(2,1)S(1)}, bf16[3,16,512]{2,1,0:T(8,128)(2,1)S(1)}, u32[]{:S(2)}, u32[]{:S(2)}) %collective-permute-start.17) | collective-permute-done | bytes 49184 | tf_op jit(solution)/shard_map/ppermute | solution.py:159
  31.9 1.4 %shard_map.103 = (bf16[4,4,16,128]{3,2,1,0:T(8,128)(2,1)S(1)}, bf16[4,2,16,128]{3,2,1,0:T(8,128)(2,1)S(1)}) custom-call(bf16[3,16,512]{2,1,0:T(8,128)(2,1)S(1)} %get-tuple-element.31.refs_0_, bf16[3,16,512]{2,1,0:T(8,128)(2,1)S(1)} %collective-permute-done.12.refs_1_, bf16[3,16,512]{2,1,0:T(8,128)(2,1)S(1)} %collective-permute-done.13.refs_2_, ...), custom_call_target="tpu_custom_call" | custom-call | flops 905969664 | bytes 3932160 | tf_op jit(solution)/shard_map/pallas_call | solution.py:193
  33.4 1.6 %collective-permute-start.20 = (bf16[4,4,16,128]{3,2,1,0:T(8,128)(2,1)S(1)}, bf16[4,4,16,128]{3,2,1,0:T(8,128)(2,1)S(1)}, u32[]{:S(2)}, u32[]{:S(2)}) collective-permute-start(bf16[4,4,16,128]{3,2,1,0:T(8,128)(2,1)S(1)} %get-tuple-element.35.refs_0_), channel_id=1, source_target_pairs={{0,3},{1,2},{2,1},{3,0},{4,7},{5,6},{6,5},{7,4},{8,11},{9,10},{10,... | collective-permute-start | bytes 196616 | tf_op jit(solution)/shard_map/ppermute | solution.py:159
  35.1 2.2 %collective-permute-done.20.refs_3_ = bf16[4,4,16,128]{3,2,1,0:T(8,128)(2,1)S(1)} collective-permute-done((bf16[4,4,16,128]{3,2,1,0:T(8,128)(2,1)S(1)}, bf16[4,4,16,128]{3,2,1,0:T(8,128)(2,1)S(1)}, u32[]{:S(2)}, u32[]{:S(2)}) %collective-permute-start.20) | collective-permute-done | bytes 65568 | tf_op jit(solution)/shard_map/ppermute | solution.py:159
  37.7 1.0 %collective-permute-done.21.refs_2_ = bf16[4,4,16,128]{3,2,1,0:T(8,128)(2,1)S(1)} collective-permute-done((bf16[4,4,16,128]{3,2,1,0:T(8,128)(2,1)S(1)}, bf16[4,4,16,128]{3,2,1,0:T(8,128)(2,1)S(1)}, u32[]{:S(2)}, u32[]{:S(2)}) %collective-permute-start.21) | collective-permute-done | bytes 65568 | tf_op jit(solution)/shard_map/ppermute | solution.py:159
  38.6 1.2 %shard_map.104 = (bf16[32,128]{1,0:T(8,128)(2,1)S(1)}, bf16[32,128]{1,0:T(8,128)(2,1)S(1)}, bf16[32,128]{1,0:T(8,128)(2,1)S(1)}, bf16[32,128]{1,0:T(8,128)(2,1)S(1)}) custom-call(bf16[4,4,16,128]{3,2,1,0:T(8,128)(2,1)S(1)} %get-tuple-element.35.refs_0_, bf16[4,4,16,128]{3,2,1,0:T(8,128)(2,1)S(1)} %collective-permute-done.19.refs_1_, ...), custom_call_target="tpu_custom_call" | custom-call | flops 452984832 | bytes 3833856 | tf_op jit(solution)/shard_map/pallas_call | solution.py:193
  40.2 1.6 %collective-permute-start.23 = (bf16[32,128]{1,0:T(8,128)(2,1)S(1)}, bf16[32,128]{1,0:T(8,128)(2,1)S(1)}, u32[]{:S(2)}, u32[]{:S(2)}) collective-permute-start(bf16[32,128]{1,0:T(8,128)(2,1)S(1)} %get-tuple-element.39), channel_id=1, source_target_pairs={{0,2},{1,3},{2,0},{3,1},{4,6},{5,7},{6,4},{7,5},{8,10},{9,11},{10,... | collective-permute-start | bytes 24584 | tf_op jit(solution)/shard_map/ppermute | solution.py:481
  41.7 1.2 %collective-permute-start.24 = (bf16[32,128]{1,0:T(8,128)(2,1)S(1)}, bf16[32,128]{1,0:T(8,128)(2,1)S(1)}, u32[]{:S(2)}, u32[]{:S(2)}) collective-permute-start(bf16[32,128]{1,0:T(8,128)(2,1)S(1)} %get-tuple-element.40), channel_id=1, source_target_pairs={{0,3},{1,0},{2,1},{3,2},{4,7},{5,4},{6,5},{7,6},{8,11},{9,8},{10,9... | collective-permute-start | bytes 24584 | tf_op jit(solution)/shard_map/ppermute | solution.py:481
  43.0 0.9 %collective-permute-done.23.refs_2_ = bf16[32,128]{1,0:T(8,128)(2,1)S(1)} collective-permute-done((bf16[32,128]{1,0:T(8,128)(2,1)S(1)}, bf16[32,128]{1,0:T(8,128)(2,1)S(1)}, u32[]{:S(2)}, u32[]{:S(2)}) %collective-permute-start.23) | collective-permute-done | bytes 8224 | tf_op jit(solution)/shard_map/ppermute | solution.py:481
  (52 shorter events, 6.6 us)
Async XLA Ops:
  0.0 7.7 %collective-permute-start.1 = (bf16[32,512]{1,0:T(8,128)(2,1)}, bf16[32,512]{1,0:T(8,128)(2,1)S(1)}, u32[]{:S(2)}, u32[]{:S(2)}) collective-permute-start(bf16[32,512]{1,0:T(8,128)(2,1)} %bitcast.11), channel_id=1, source_target_pairs={{0,1},{1,5},{2,9},{3,13},{4,0},{5,4},{6,8},{7,12},{8,3},{9,7},{10,... | collective-permute-start | bytes 98312 | tf_op jit(solution)/shard_map/ppermute | solution.py:413
  0.5 8.5 %collective-permute-start = (bf16[32,512]{1,0:T(8,128)(2,1)}, bf16[32,512]{1,0:T(8,128)(2,1)S(1)}, u32[]{:S(2)}, u32[]{:S(2)}) collective-permute-start(bf16[32,512]{1,0:T(8,128)(2,1)} %bitcast.12), channel_id=1, source_target_pairs={{0,3},{1,7},{2,11},{3,15},{4,2},{5,6},{6,10},{7,14},{8,1},{9,5},{1... | collective-permute-start | bytes 98312 | tf_op jit(solution)/shard_map/ppermute | solution.py:413
  5.8 7.0 %collective-permute-start.8 = (bf16[128,512]{1,0:T(8,128)(2,1)}, bf16[128,512]{1,0:T(8,128)(2,1)S(1)}, u32[]{:S(2)}, u32[]{:S(2)}) collective-permute-start(bf16[128,512]{1,0:T(8,128)(2,1)} %param.12), channel_id=1, source_target_pairs={{0,3},{1,2},{2,1},{3,0},{4,7},{5,6},{6,5},{7,4},{8,11},{9,10},{10,... | collective-permute-start | bytes 393224 | tf_op jit(solution)/shard_map/ppermute | solution.py:159
  9.1 1.4 %collective-permute-start.3 = (bf16[32,512]{1,0:T(8,128)(2,1)S(1)}, bf16[32,512]{1,0:T(8,128)(2,1)S(1)}, u32[]{:S(2)}, u32[]{:S(2)}) collective-permute-start(bf16[32,512]{1,0:T(8,128)(2,1)S(1)} %collective-permute-done.refs_3_), channel_id=1, source_target_pairs={{0,1},{1,0},{2,3},{3,2},{4,5},{5,4},{6,7},{7,6},{8,9},{9,8},{10,11... | collective-permute-start | bytes 98312 | tf_op jit(solution)/shard_map/ppermute | solution.py:159
  9.6 5.5 %collective-permute-start.7 = (bf16[128,512]{1,0:T(8,128)(2,1)S(1)}, bf16[128,512]{1,0:T(8,128)(2,1)S(1)}, u32[]{:S(2)}, u32[]{:S(2)}) collective-permute-start(bf16[128,512]{1,0:T(8,128)(2,1)S(1)} %copy-done.4), channel_id=1, source_target_pairs={{0,1},{1,0},{2,3},{3,2},{4,5},{5,4},{6,7},{7,6},{8,9},{9,8},{10,11... | collective-permute-start | bytes 393224 | tf_op jit(solution)/shard_map/ppermute | solution.py:159
  11.1 3.4 %collective-permute-start.5 = (bf16[128,128]{1,0:T(8,128)(2,1)S(1)}, bf16[128,128]{1,0:T(8,128)(2,1)S(1)}, u32[]{:S(2)}, u32[]{:S(2)}) collective-permute-start(bf16[128,128]{1,0:T(8,128)(2,1)S(1)} %get-tuple-element.26.refs_0_), channel_id=1, source_target_pairs={{0,3},{1,2},{2,1},{3,0},{4,7},{5,6},{6,5},{7,4},{8,11},{9,10},{10,... | collective-permute-start | bytes 98312 | tf_op jit(solution)/shard_map/ppermute | solution.py:159
  12.7 3.0 %collective-permute-start.9 = (bf16[128,512]{1,0:T(8,128)(2,1)S(1)}, bf16[128,512]{1,0:T(8,128)(2,1)S(1)}, u32[]{:S(2)}, u32[]{:S(2)}) collective-permute-start(bf16[128,512]{1,0:T(8,128)(2,1)S(1)} %collective-permute-done.8.refs_6_), channel_id=1, source_target_pairs={{0,1},{1,0},{2,3},{3,2},{4,5},{5,4},{6,7},{7,6},{8,9},{9,8},{10,11... | collective-permute-start | bytes 393224 | tf_op jit(solution)/shard_map/ppermute | solution.py:159
  13.1 2.0 %collective-permute-start.4 = (bf16[128,128]{1,0:T(8,128)(2,1)S(1)}, bf16[128,128]{1,0:T(8,128)(2,1)S(1)}, u32[]{:S(2)}, u32[]{:S(2)}) collective-permute-start(bf16[128,128]{1,0:T(8,128)(2,1)S(1)} %get-tuple-element.26.refs_0_), channel_id=1, source_target_pairs={{0,1},{1,0},{2,3},{3,2},{4,5},{5,4},{6,7},{7,6},{8,9},{9,8},{10,11... | collective-permute-start | bytes 98312 | tf_op jit(solution)/shard_map/ppermute | solution.py:159
  14.5 1.2 %collective-permute-start.6 = (bf16[128,128]{1,0:T(8,128)(2,1)S(1)}, bf16[128,128]{1,0:T(8,128)(2,1)S(1)}, u32[]{:S(2)}, u32[]{:S(2)}) collective-permute-start(bf16[128,128]{1,0:T(8,128)(2,1)S(1)} %collective-permute-done.5.refs_3_), channel_id=1, source_target_pairs={{0,1},{1,0},{2,3},{3,2},{4,5},{5,4},{6,7},{7,6},{8,9},{9,8},{10,11... | collective-permute-start | bytes 98312 | tf_op jit(solution)/shard_map/ppermute | solution.py:159
  17.0 1.4 %collective-permute-start.10 = (f32[4,16,512]{2,1,0:T(8,128)S(1)}, f32[4,16,512]{2,1,0:T(8,128)S(1)}, u32[]{:S(2)}, u32[]{:S(2)}) collective-permute-start(f32[4,16,512]{2,1,0:T(8,128)S(1)} %get-tuple-element.29), channel_id=1, source_target_pairs={{0,1},{1,0},{2,3},{3,2},{4,5},{5,4},{6,7},{7,6},{8,9},{9,8},{10,11... | collective-permute-start | bytes 393224 | tf_op jit(solution)/shard_map/ppermute | solution.py:159
  18.4 4.0 %collective-permute-start.11 = (bf16[4,16,512]{2,1,0:T(8,128)(2,1)S(1)}, bf16[4,16,512]{2,1,0:T(8,128)(2,1)S(1)}, u32[]{:S(2)}, u32[]{:S(2)}) collective-permute-start(bf16[4,16,512]{2,1,0:T(8,128)(2,1)S(1)} %get-tuple-element.41), channel_id=1, source_target_pairs={{0,3},{1,2},{2,1},{3,0},{4,7},{5,6},{6,5},{7,4},{8,11},{9,10},{10,... | collective-permute-start | bytes 196616 | tf_op jit(solution)/shard_map/ppermute | solution.py:159
  22.5 6.6 %collective-permute-start.12 = (bf16[3,16,512]{2,1,0:T(8,128)(2,1)S(1)}, bf16[3,16,512]{2,1,0:T(8,128)(2,1)S(1)}, u32[]{:S(2)}, u32[]{:S(2)}) collective-permute-start(bf16[3,16,512]{2,1,0:T(8,128)(2,1)S(1)} %get-tuple-element.32), channel_id=1, source_target_pairs={{0,4},{4,8},{8,12},{12,0},{1,5},{5,9},{9,13},{13,1},{2,6},{6,10},{... | collective-permute-start | bytes 147464 | tf_op jit(solution)/shard_map/ppermute | solution.py:456
  22.7 7.9 %collective-permute-start.13 = (bf16[3,16,512]{2,1,0:T(8,128)(2,1)S(1)}, bf16[3,16,512]{2,1,0:T(8,128)(2,1)S(1)}, u32[]{:S(2)}, u32[]{:S(2)}) collective-permute-start(bf16[3,16,512]{2,1,0:T(8,128)(2,1)S(1)} %get-tuple-element.33), channel_id=1, source_target_pairs={{0,8},{4,12},{8,0},{12,4},{1,9},{5,13},{9,1},{13,5},{2,10},{6,14},... | collective-permute-start | bytes 147464 | tf_op jit(solution)/shard_map/ppermute | solution.py:456
  26.2 4.4 %collective-permute-start.14 = (bf16[3,16,512]{2,1,0:T(8,128)(2,1)S(1)}, bf16[3,16,512]{2,1,0:T(8,128)(2,1)S(1)}, u32[]{:S(2)}, u32[]{:S(2)}) collective-permute-start(bf16[3,16,512]{2,1,0:T(8,128)(2,1)S(1)} %get-tuple-element.34), channel_id=1, source_target_pairs={{0,12},{4,0},{8,4},{12,8},{1,13},{5,1},{9,5},{13,9},{2,14},{6,2},{... | collective-permute-start | bytes 147464 | tf_op jit(solution)/shard_map/ppermute | solution.py:456
  26.6 4.5 %collective-permute-start.15 = (bf16[3,16,512]{2,1,0:T(8,128)(2,1)S(1)}, bf16[3,16,512]{2,1,0:T(8,128)(2,1)S(1)}, u32[]{:S(2)}, u32[]{:S(2)}) collective-permute-start(bf16[3,16,512]{2,1,0:T(8,128)(2,1)S(1)} %get-tuple-element.31.refs_0_), channel_id=1, source_target_pairs={{0,1},{1,0},{2,3},{3,2},{4,5},{5,4},{6,7},{7,6},{8,9},{9,8},{10,11... | collective-permute-start | bytes 147464 | tf_op jit(solution)/shard_map/ppermute | solution.py:159
  29.1 1.9 %collective-permute-start.16 = (bf16[3,16,512]{2,1,0:T(8,128)(2,1)S(1)}, bf16[3,16,512]{2,1,0:T(8,128)(2,1)S(1)}, u32[]{:S(2)}, u32[]{:S(2)}) collective-permute-start(bf16[3,16,512]{2,1,0:T(8,128)(2,1)S(1)} %collective-permute-done.12.refs_1_), channel_id=1, source_target_pairs={{0,1},{1,0},{2,3},{3,2},{4,5},{5,4},{6,7},{7,6},{8,9},{9,8},{10,11... | collective-permute-start | bytes 147464 | tf_op jit(solution)/shard_map/ppermute | solution.py:159
  30.5 1.2 %collective-permute-start.17 = (bf16[3,16,512]{2,1,0:T(8,128)(2,1)S(1)}, bf16[3,16,512]{2,1,0:T(8,128)(2,1)S(1)}, u32[]{:S(2)}, u32[]{:S(2)}) collective-permute-start(bf16[3,16,512]{2,1,0:T(8,128)(2,1)S(1)} %collective-permute-done.13.refs_2_), channel_id=1, source_target_pairs={{0,1},{1,0},{2,3},{3,2},{4,5},{5,4},{6,7},{7,6},{8,9},{9,8},{10,11... | collective-permute-start | bytes 147464 | tf_op jit(solution)/shard_map/ppermute | solution.py:159
  30.6 1.3 %collective-permute-start.18 = (bf16[3,16,512]{2,1,0:T(8,128)(2,1)S(1)}, bf16[3,16,512]{2,1,0:T(8,128)(2,1)S(1)}, u32[]{:S(2)}, u32[]{:S(2)}) collective-permute-start(bf16[3,16,512]{2,1,0:T(8,128)(2,1)S(1)} %collective-permute-done.14.refs_3_), channel_id=1, source_target_pairs={{0,1},{1,0},{2,3},{3,2},{4,5},{5,4},{6,7},{7,6},{8,9},{9,8},{10,11... | collective-permute-start | bytes 147464 | tf_op jit(solution)/shard_map/ppermute | solution.py:159
  33.4 4.0 %collective-permute-start.20 = (bf16[4,4,16,128]{3,2,1,0:T(8,128)(2,1)S(1)}, bf16[4,4,16,128]{3,2,1,0:T(8,128)(2,1)S(1)}, u32[]{:S(2)}, u32[]{:S(2)}) collective-permute-start(bf16[4,4,16,128]{3,2,1,0:T(8,128)(2,1)S(1)} %get-tuple-element.35.refs_0_), channel_id=1, source_target_pairs={{0,3},{1,2},{2,1},{3,0},{4,7},{5,6},{6,5},{7,4},{8,11},{9,10},{10,... | collective-permute-start | bytes 196616 | tf_op jit(solution)/shard_map/ppermute | solution.py:159
  35.0 2.7 %collective-permute-start.19 = (bf16[4,4,16,128]{3,2,1,0:T(8,128)(2,1)S(1)}, bf16[4,4,16,128]{3,2,1,0:T(8,128)(2,1)S(1)}, u32[]{:S(2)}, u32[]{:S(2)}) collective-permute-start(bf16[4,4,16,128]{3,2,1,0:T(8,128)(2,1)S(1)} %get-tuple-element.35.refs_0_), channel_id=1, source_target_pairs={{0,1},{1,0},{2,3},{3,2},{4,5},{5,4},{6,7},{7,6},{8,9},{9,8},{10,11... | collective-permute-start | bytes 196616 | tf_op jit(solution)/shard_map/ppermute | solution.py:159
  37.4 1.3 %collective-permute-start.21 = (bf16[4,4,16,128]{3,2,1,0:T(8,128)(2,1)S(1)}, bf16[4,4,16,128]{3,2,1,0:T(8,128)(2,1)S(1)}, u32[]{:S(2)}, u32[]{:S(2)}) collective-permute-start(bf16[4,4,16,128]{3,2,1,0:T(8,128)(2,1)S(1)} %collective-permute-done.20.refs_3_), channel_id=1, source_target_pairs={{0,1},{1,0},{2,3},{3,2},{4,5},{5,4},{6,7},{7,6},{8,9},{9,8},{10,11... | collective-permute-start | bytes 196616 | tf_op jit(solution)/shard_map/ppermute | solution.py:159
  39.8 3.1 %collective-permute-start.22 = (bf16[32,128]{1,0:T(8,128)(2,1)S(1)}, bf16[32,128]{1,0:T(8,128)(2,1)S(1)}, u32[]{:S(2)}, u32[]{:S(2)}) collective-permute-start(bf16[32,128]{1,0:T(8,128)(2,1)S(1)} %get-tuple-element.38), channel_id=1, source_target_pairs={{0,1},{1,2},{2,3},{3,0},{4,5},{5,6},{6,7},{7,4},{8,9},{9,10},{10,1... | collective-permute-start | bytes 24584 | tf_op jit(solution)/shard_map/ppermute | solution.py:481
  40.2 3.7 %collective-permute-start.23 = (bf16[32,128]{1,0:T(8,128)(2,1)S(1)}, bf16[32,128]{1,0:T(8,128)(2,1)S(1)}, u32[]{:S(2)}, u32[]{:S(2)}) collective-permute-start(bf16[32,128]{1,0:T(8,128)(2,1)S(1)} %get-tuple-element.39), channel_id=1, source_target_pairs={{0,2},{1,3},{2,0},{3,1},{4,6},{5,7},{6,4},{7,5},{8,10},{9,11},{10,... | collective-permute-start | bytes 24584 | tf_op jit(solution)/shard_map/ppermute | solution.py:481
  41.7 2.6 %collective-permute-start.24 = (bf16[32,128]{1,0:T(8,128)(2,1)S(1)}, bf16[32,128]{1,0:T(8,128)(2,1)S(1)}, u32[]{:S(2)}, u32[]{:S(2)}) collective-permute-start(bf16[32,128]{1,0:T(8,128)(2,1)S(1)} %get-tuple-element.40), channel_id=1, source_target_pairs={{0,3},{1,0},{2,1},{3,2},{4,7},{5,4},{6,5},{7,6},{8,11},{9,8},{10,9... | collective-permute-start | bytes 24584 | tf_op jit(solution)/shard_map/ppermute | solution.py:481
  (8 other events, 101.6 us)

commit v6 on v5

--- a/solution.py
+++ b/solution.py
@@ -294,26 +294,29 @@
         out[...] = framed[pl.ds(lax.rem(level + mask, len(outs)) * step, step + 2)]
 
 
-def conv_rows(field, kernel):
+def conv_taps(field, kernel, lane=0, total=0.0):
     frames, rows = field.shape[0] - 2, field.shape[1] - 2
     columns, width = field.shape[2:]
     share = kernel.shape[3]
     tokens = frames * rows * columns
-    total = None
     for shift_time in range(3):
         for shift_row in range(3):
             slab = field[shift_time : shift_time + frames, shift_row : shift_row + rows]
-            term = lax.dot_general(
+            total = total + lax.dot_general(
                 slab.reshape(tokens, width),
-                kernel[shift_time, shift_row].reshape(3 * share, width),
+                kernel[shift_time, shift_row, :, :, pl.ds(lane, width)].reshape(3 * share, width),
                 (((1,), (1,)), ((), ())),
                 preferred_element_type=jnp.float32,
             )
-            total = term if total is None else total + term
+    return total
+
+
+def conv_join(total, columns):
+    tokens, share = total.shape[0], total.shape[1] // 3
     column = lax.rem(lax.broadcasted_iota(jnp.int32, (tokens, share), 0), columns)
     before = jnp.where(column > 0, pltpu.roll(total[:, :share], 1, 0), 0.0)
     after = jnp.where(column < columns - 1, pltpu.roll(total[:, 2 * share :], tokens - 1, 0), 0.0)
-    return (before + total[:, share : 2 * share] + after).reshape(frames, rows, columns, share)
+    return before + total[:, share : 2 * share] + after
 
 
 def clear_ends(field):
@@ -333,9 +336,9 @@
         parity = half_of(place) ^ (index // count)
         for row in range(piece.shape[0]):
             field[frame, 2 * row + parity] = piece[row]
-    activated = silu(conv_rows(field, kernel))
     frames, band, columns, share = hidden_ref.shape
     rows = band - 2
+    activated = silu(conv_join(conv_taps(field, kernel), columns).reshape(hidden_ref.shape))
     global_row = level * rows - 1 + lax.broadcasted_iota(jnp.int32, activated.shape, 1)
     inside = (global_row >= 0) & (global_row < height)
     hidden_ref[...] = jnp.where(inside, activated, 0.0).astype(jnp.bfloat16)
@@ -343,18 +346,31 @@
     part_ref[...] = field[1 : frames + 1, 2 : 2 + rows, :, pl.ds(at, share)]
 
 
-def second_conv_body(*refs):
-    pieces = refs[: (len(refs) - 4) // 2]
-    part, kernel = refs[len(pieces) : len(pieces) + 2]
-    outs, field, final = refs[len(pieces) + 2 : -2], refs[-2], refs[-1]
+def chip_taps(pieces, chip, kernel, field, total=0.0):
+    share = pieces[0].shape[3]
+    core = lax.axis_index("frame") % 2
+    clear_ends(field)
+    for other, piece in enumerate(pieces):
+        at = pl.multiple_of((core ^ other) * share, share)
+        field[1 : 1 + piece.shape[0], :, :, pl.ds(at, share)] = piece[...]
+    return conv_taps(field, kernel, pl.multiple_of(chip * 2 * share, 2 * share), total)
+
+
+def near_conv_body(own, other, kernel, total_ref, field):
+    total_ref[...] = chip_taps([own, other], lax.axis_index("frame") // 2, kernel, field)
+
+
+def second_conv_body(far, *refs):
+    pieces = refs[:far]
+    total, part, kernel = refs[far : far + 3]
+    outs, field, final = refs[far + 3 : -2], refs[-2], refs[-1]
     place = lax.axis_index("frame")
-    clear_ends(field)
-    share = part.shape[3]
-    frames = part.shape[0]
-    for mask, piece in enumerate(pieces):
-        at = pl.multiple_of((place ^ mask) * share, share)
-        field[1 : frames + 1, :, :, pl.ds(at, share)] = piece[...]
-    final[...] = part[...].astype(jnp.float32) + conv_rows(field, kernel)
+    result = total[...]
+    for index in range(0, far, 2):
+        pair = [pieces[index], pieces[index + 1]]
+        result = chip_taps(pair, (place // 2) ^ (index // 2 + 1), kernel, field, result)
+    result = conv_join(result, part.shape[2]).reshape(part.shape)
+    final[...] = part[...].astype(jnp.float32) + result
     lines = final.shape[0] * final.shape[1]
     strip = outs[0].shape[0] // lines
     for mask, out in enumerate(outs):
@@ -464,15 +480,24 @@
         room=8,
     )
     strip = columns // count
+    pieces = gathered_by_mask(hidden)
+    taps_shape = (count * rows * columns, 3 * share)
+    field = ((count + 2, rows + 2, columns, 2 * share), bf16)
+    flops = 2 * count * rows * columns * 27 * 2 * share * share
+    (total,) = call(
+        near_conv_body,
+        [*pieces[:2], conv_second],
+        [(taps_shape, f32)],
+        scratch=[field],
+        flops=flops,
+        room=8,
+    )
     strips = call(
-        second_conv_body,
-        [*gathered_by_mask(hidden), own_part, conv_second],
+        functools.partial(second_conv_body, count - 2),
+        [*pieces[2:], total, own_part, conv_second],
         [((count * rows * strip, share), bf16)] * count,
-        scratch=[
-            ((count + 2, rows + 2, columns, width), bf16),
-            ((count, rows, columns, share), f32),
-        ],
-        flops=2 * count * rows * columns * 27 * width * share,
+        scratch=[field, ((count, rows, columns, share), f32)],
+        flops=flops * (count // 2 - 1),
         room=8,
     )
     outs = list(strips)

time: 45.1 us -> 44.6 us (0.989)
  waiting for transfers between devices: 16.9 us -> 16.2 us
    ppermute x17, waiting for transfers between devices: 10.1 us -> 9.46 us  [swap(): return lax.ppermute(cells, 'frame', [(i, i ^ mask) for i in range(count)])]
    pallas_call x6 -> x7, Pallas kernels: 5.3 us -> 5.42 us  [call(): pl.pallas_call(body, out_shape=[jax.ShapeDtypeStruct(shape, kind) for sha...]
  transfers between devices with their start and end apart: 25 -> 25, of which waited for: 16 -> 16; matrix products, arithmetic and copies ran while one was open for 3% -> 3% of each run, Pallas kernels for 1% -> 3%
where the time goes in v6:
time: 44.6 us; the launch traced here: 44.4 us
  starting transfers between devices  21.1 us (47%)
  waiting for transfers between devices  16.2 us (36%)
  Pallas kernels  5.42 us (12%)
  other arithmetic  1.29 us (3%)
    ppermute x17, waiting for transfers between devices, swap(): return lax.ppermute(cells, 'frame', [(i, i ^ mask) for i in range(count)])  9.46 us
    ppermute x17, starting transfers between devices, swap(): return lax.ppermute(cells, 'frame', [(i, i ^ mask) for i in range(count)])  8.22 us
    ppermute x2, starting transfers between devices, by_frames(): pieces[mask] = lax.ppermute(own, ('row', 'frame'), pairs)  5.74 us
    pallas_call x7, Pallas kernels, call(): pl.pallas_call(body, out_shape=[jax.ShapeDtypeStruct(shape, kind) for sha...  5.42 us
    ppermute x3, waiting for transfers between devices, by_frames(): windows[mask] = lax.ppermute(windows[mask], 'row', pairs)  4.08 us
    ppermute x3, starting transfers between devices, by_frames(): windows[mask] = lax.ppermute(windows[mask], 'row', pairs)  4.01 us
    ppermute x3, starting transfers between devices, by_frames(): outs[mask] = lax.ppermute(strips[mask], 'frame', pairs)  3.1 us
    ppermute x3, waiting for transfers between devices, by_frames(): outs[mask] = lax.ppermute(strips[mask], 'frame', pairs)  1.37 us
  transfers between devices with their start and end apart: 25, of which 16 were waited for; matrix products, arithmetic and copies ran while one was open for 3% of the time, Pallas kernels for 3%

profile of v6, /device:TPU:0, one launch (start us, length us, event | category | flops | bytes accessed | tf_op | source)
XLA Modules:
  0.0 44.4 jit_solution(9629341144660027500)
XLA Ops:
  0.5 5.2 %collective-permute-start = (bf16[32,512]{1,0:T(8,128)(2,1)}, bf16[32,512]{1,0:T(8,128)(2,1)S(1)}, u32[]{:S(2)}, u32[]{:S(2)}) collective-permute-start(bf16[32,512]{1,0:T(8,128)(2,1)} %bitcast.12), channel_id=1, source_target_pairs={{0,3},{1,7},{2,11},{3,15},{4,2},{5,6},{6,10},{7,14},{8,1},{9,5},{1... | collective-permute-start | bytes 98312 | tf_op jit(solution)/shard_map/ppermute | solution.py:429
  5.8 0.7 %collective-permute-start.8 = (bf16[128,512]{1,0:T(8,128)(2,1)}, bf16[128,512]{1,0:T(8,128)(2,1)S(1)}, u32[]{:S(2)}, u32[]{:S(2)}) collective-permute-start(bf16[128,512]{1,0:T(8,128)(2,1)} %param.12), channel_id=1, source_target_pairs={{0,3},{1,2},{2,1},{3,0},{4,7},{5,6},{6,5},{7,4},{8,11},{9,10},{10,... | collective-permute-start | bytes 393224 | tf_op jit(solution)/shard_map/ppermute | solution.py:159
  6.5 1.3 %pad_maximum_fusion.refs_4_.refs_8_ = bf16[1024,512]{1,0:T(8,128)(2,1)S(1)} fusion(bf16[512,512]{1,0:T(8,128)(2,1)} %param.16, bf16[128,512]{1,0:T(8,128)(2,1)} %param.12, bf16[384,512]{1,0:T(8,128)(2,1)} %bitcast.8), kind=kLoop, calls=%fused_computation | loop fusion | flops 3145728 | bytes 2097152 | tf_op jit(solution)/shard_map/concatenate | solution.py:430
  7.7 1.3 %collective-permute-done.refs_3_ = bf16[32,512]{1,0:T(8,128)(2,1)S(1)} collective-permute-done((bf16[32,512]{1,0:T(8,128)(2,1)}, bf16[32,512]{1,0:T(8,128)(2,1)S(1)}, u32[]{:S(2)}, u32[]{:S(2)}) %collective-permute-start) | collective-permute-done | bytes 32800 | tf_op jit(solution)/shard_map/ppermute | solution.py:429
  9.6 0.7 %collective-permute-done.2.refs_0_ = bf16[32,512]{1,0:T(8,128)(2,1)S(1)} collective-permute-done((bf16[32,512]{1,0:T(8,128)(2,1)S(1)}, bf16[32,512]{1,0:T(8,128)(2,1)S(1)}, u32[]{:S(2)}, u32[]{:S(2)}) %collective-permute-start.2) | collective-permute-done | bytes 32800 | tf_op jit(solution)/shard_map/ppermute | solution.py:159
  10.5 0.7 %shard_map.100 = (bf16[128,128]{1,0:T(8,128)(2,1)S(1)}, bf16[128,512]{1,0:T(8,128)(2,1)S(1)}) custom-call(bf16[32,512]{1,0:T(8,128)(2,1)S(1)} %collective-permute-done.2.refs_0_, bf16[32,512]{1,0:T(8,128)(2,1)S(1)} %collective-permute-done.1.refs_1_, bf16[32,512]{1,0:T(8,128)(2,1)S(1)} %collective-permute-done.3.refs_2_, ...), custom_call_target="tpu_custom_call" | custom-call | flops 50331648 | bytes 1179648 | tf_op jit(solution)/shard_map/pallas_call | solution.py:193
  11.1 1.6 %collective-permute-start.5 = (bf16[128,128]{1,0:T(8,128)(2,1)S(1)}, bf16[128,128]{1,0:T(8,128)(2,1)S(1)}, u32[]{:S(2)}, u32[]{:S(2)}) collective-permute-start(bf16[128,128]{1,0:T(8,128)(2,1)S(1)} %get-tuple-element.26.refs_0_), channel_id=1, source_target_pairs={{0,3},{1,2},{2,1},{3,0},{4,7},{5,6},{6,5},{7,4},{8,11},{9,10},{10,... | collective-permute-start | bytes 98312 | tf_op jit(solution)/shard_map/ppermute | solution.py:159
  13.4 1.2 %collective-permute-done.5.refs_3_ = bf16[128,128]{1,0:T(8,128)(2,1)S(1)} collective-permute-done((bf16[128,128]{1,0:T(8,128)(2,1)S(1)}, bf16[128,128]{1,0:T(8,128)(2,1)S(1)}, u32[]{:S(2)}, u32[]{:S(2)}) %collective-permute-start.5) | collective-permute-done | bytes 32800 | tf_op jit(solution)/shard_map/ppermute | solution.py:159
  15.8 1.2 %shard_map.101 = (f32[4,16,512]{2,1,0:T(8,128)S(1)}, f32[4,16,512]{2,1,0:T(8,128)S(1)}, bf16[4,16,512]{2,1,0:T(8,128)(2,1)S(1)}) custom-call(bf16[128,128]{1,0:T(8,128)(2,1)S(1)} %get-tuple-element.26.refs_0_, bf16[128,128]{1,0:T(8,128)(2,1)S(1)} %collective-permute-done.4.refs_1_, bf16[128,128]{1,0:T(8,128)(2,1)S(1)} %collective-permute-done.6.refs_2_, ...), custom_call_target="tpu_custom_call" | custom-call | flops 268435456 | bytes 2793472 | tf_op jit(solution)/shard_map/pallas_call | solution.py:193
  17.4 1.0 %collective-permute-done.10 = f32[4,16,512]{2,1,0:T(8,128)S(1)} collective-permute-done((f32[4,16,512]{2,1,0:T(8,128)S(1)}, f32[4,16,512]{2,1,0:T(8,128)S(1)}, u32[]{:S(2)}, u32[]{:S(2)}) %collective-permute-start.10) | collective-permute-done | bytes 131104 | tf_op jit(solution)/shard_map/ppermute | solution.py:159
  18.4 1.6 %collective-permute-start.11 = (bf16[4,16,512]{2,1,0:T(8,128)(2,1)S(1)}, bf16[4,16,512]{2,1,0:T(8,128)(2,1)S(1)}, u32[]{:S(2)}, u32[]{:S(2)}) collective-permute-start(bf16[4,16,512]{2,1,0:T(8,128)(2,1)S(1)} %get-tuple-element.41), channel_id=1, source_target_pairs={{0,3},{1,2},{2,1},{3,0},{4,7},{5,6},{6,5},{7,4},{8,11},{9,10},{10,... | collective-permute-start | bytes 196616 | tf_op jit(solution)/shard_map/ppermute | solution.py:159
  20.0 2.4 %collective-permute-done.11.refs_3_ = bf16[4,16,512]{2,1,0:T(8,128)(2,1)S(1)} collective-permute-done((bf16[4,16,512]{2,1,0:T(8,128)(2,1)S(1)}, bf16[4,16,512]{2,1,0:T(8,128)(2,1)S(1)}, u32[]{:S(2)}, u32[]{:S(2)}) %collective-permute-start.11) | collective-permute-done | bytes 65568 | tf_op jit(solution)/shard_map/ppermute | solution.py:159
  22.7 3.6 %collective-permute-start.13 = (bf16[3,16,512]{2,1,0:T(8,128)(2,1)S(1)}, bf16[3,16,512]{2,1,0:T(8,128)(2,1)S(1)}, u32[]{:S(2)}, u32[]{:S(2)}) collective-permute-start(bf16[3,16,512]{2,1,0:T(8,128)(2,1)S(1)} %get-tuple-element.33), channel_id=1, source_target_pairs={{0,8},{4,12},{8,0},{12,4},{1,9},{5,13},{9,1},{13,5},{2,10},{6,14},... | collective-permute-start | bytes 147464 | tf_op jit(solution)/shard_map/ppermute | solution.py:472
  26.6 2.6 %collective-permute-done.12.refs_1_ = bf16[3,16,512]{2,1,0:T(8,128)(2,1)S(1)} collective-permute-done((bf16[3,16,512]{2,1,0:T(8,128)(2,1)S(1)}, bf16[3,16,512]{2,1,0:T(8,128)(2,1)S(1)}, u32[]{:S(2)}, u32[]{:S(2)}) %collective-permute-start.12) | collective-permute-done | bytes 49184 | tf_op jit(solution)/shard_map/ppermute | solution.py:472
  29.1 1.4 %collective-permute-done.13.refs_2_ = bf16[3,16,512]{2,1,0:T(8,128)(2,1)S(1)} collective-permute-done((bf16[3,16,512]{2,1,0:T(8,128)(2,1)S(1)}, bf16[3,16,512]{2,1,0:T(8,128)(2,1)S(1)}, u32[]{:S(2)}, u32[]{:S(2)}) %collective-permute-start.13) | collective-permute-done | bytes 49184 | tf_op jit(solution)/shard_map/ppermute | solution.py:472
  31.1 0.7 %collective-permute-done.17.refs_6_ = bf16[3,16,512]{2,1,0:T(8,128)(2,1)S(1)} collective-permute-done((bf16[3,16,512]{2,1,0:T(8,128)(2,1)S(1)}, bf16[3,16,512]{2,1,0:T(8,128)(2,1)S(1)}, u32[]{:S(2)}, u32[]{:S(2)}) %collective-permute-start.17) | collective-permute-done | bytes 49184 | tf_op jit(solution)/shard_map/ppermute | solution.py:159
  31.9 1.4 %shard_map.103 = (bf16[4,4,16,128]{3,2,1,0:T(8,128)(2,1)S(1)}, bf16[4,2,16,128]{3,2,1,0:T(8,128)(2,1)S(1)}) custom-call(bf16[3,16,512]{2,1,0:T(8,128)(2,1)S(1)} %get-tuple-element.31.refs_0_, bf16[3,16,512]{2,1,0:T(8,128)(2,1)S(1)} %collective-permute-done.12.refs_1_, bf16[3,16,512]{2,1,0:T(8,128)(2,1)S(1)} %collective-permute-done.13.refs_2_, ...), custom_call_target="tpu_custom_call" | custom-call | flops 905969664 | bytes 3932160 | tf_op jit(solution)/shard_map/pallas_call | solution.py:193
  33.4 1.6 %collective-permute-start.19 = (bf16[4,4,16,128]{3,2,1,0:T(8,128)(2,1)S(1)}, bf16[4,4,16,128]{3,2,1,0:T(8,128)(2,1)S(1)}, u32[]{:S(2)}, u32[]{:S(2)}) collective-permute-start(bf16[4,4,16,128]{3,2,1,0:T(8,128)(2,1)S(1)} %get-tuple-element.35.own), channel_id=1, source_target_pairs={{0,3},{1,2},{2,1},{3,0},{4,7},{5,6},{6,5},{7,4},{8,11},{9,10},{10,... | collective-permute-start | bytes 196616 | tf_op jit(solution)/shard_map/ppermute | solution.py:159
  35.1 2.2 %collective-permute-done.19.refs_1_ = bf16[4,4,16,128]{3,2,1,0:T(8,128)(2,1)S(1)} collective-permute-done((bf16[4,4,16,128]{3,2,1,0:T(8,128)(2,1)S(1)}, bf16[4,4,16,128]{3,2,1,0:T(8,128)(2,1)S(1)}, u32[]{:S(2)}, u32[]{:S(2)}) %collective-permute-start.19) | collective-permute-done | bytes 65568 | tf_op jit(solution)/shard_map/ppermute | solution.py:159
  37.7 0.7 %shard_map.104.refs_2_ = f32[128,384]{1,0:T(8,128)S(1)} custom-call(bf16[4,4,16,128]{3,2,1,0:T(8,128)(2,1)S(1)} %get-tuple-element.35.own, bf16[4,4,16,128]{3,2,1,0:T(8,128)(2,1)S(1)} %collective-permute-done.21.other, bf16[3,3,3,128,512]{4,3,2,1,0:T(8,128)(2,1)S(1)} %copy-done.1), custom_call_target="tpu_custom_call" | custom-call | flops 226492416 | bytes 3670016 | tf_op jit(solution)/shard_map/pallas_call | solution.py:193
  38.6 0.7 %shard_map.105 = (bf16[32,128]{1,0:T(8,128)(2,1)S(1)}, bf16[32,128]{1,0:T(8,128)(2,1)S(1)}, bf16[32,128]{1,0:T(8,128)(2,1)S(1)}, bf16[32,128]{1,0:T(8,128)(2,1)S(1)}) custom-call(bf16[4,4,16,128]{3,2,1,0:T(8,128)(2,1)S(1)} %collective-permute-done.20.refs_0_, bf16[4,4,16,128]{3,2,1,0:T(8,128)(2,1)S(1)} %collective-permute-done.19.refs_1_, ...), custom_call_target="tpu_custom_call" | custom-call | flops 226492416 | bytes 3899392 | tf_op jit(solution)/shard_map/pallas_call | solution.py:193
  39.6 1.6 %collective-permute-start.23 = (bf16[32,128]{1,0:T(8,128)(2,1)S(1)}, bf16[32,128]{1,0:T(8,128)(2,1)S(1)}, u32[]{:S(2)}, u32[]{:S(2)}) collective-permute-start(bf16[32,128]{1,0:T(8,128)(2,1)S(1)} %get-tuple-element.39), channel_id=1, source_target_pairs={{0,2},{1,3},{2,0},{3,1},{4,6},{5,7},{6,4},{7,5},{8,10},{9,11},{10,... | collective-permute-start | bytes 24584 | tf_op jit(solution)/shard_map/ppermute | solution.py:506
  41.2 1.2 %collective-permute-start.24 = (bf16[32,128]{1,0:T(8,128)(2,1)S(1)}, bf16[32,128]{1,0:T(8,128)(2,1)S(1)}, u32[]{:S(2)}, u32[]{:S(2)}) collective-permute-start(bf16[32,128]{1,0:T(8,128)(2,1)S(1)} %get-tuple-element.40), channel_id=1, source_target_pairs={{0,3},{1,0},{2,1},{3,2},{4,7},{5,4},{6,5},{7,6},{8,11},{9,8},{10,9... | collective-permute-start | bytes 24584 | tf_op jit(solution)/shard_map/ppermute | solution.py:506
  42.4 0.9 %collective-permute-done.23.refs_2_ = bf16[32,128]{1,0:T(8,128)(2,1)S(1)} collective-permute-done((bf16[32,128]{1,0:T(8,128)(2,1)S(1)}, bf16[32,128]{1,0:T(8,128)(2,1)S(1)}, u32[]{:S(2)}, u32[]{:S(2)}) %collective-permute-start.23) | collective-permute-done | bytes 8224 | tf_op jit(solution)/shard_map/ppermute | solution.py:506
  (53 shorter events, 6.9 us)
Async XLA Ops:
  0.0 7.7 %collective-permute-start.1 = (bf16[32,512]{1,0:T(8,128)(2,1)}, bf16[32,512]{1,0:T(8,128)(2,1)S(1)}, u32[]{:S(2)}, u32[]{:S(2)}) collective-permute-start(bf16[32,512]{1,0:T(8,128)(2,1)} %bitcast.11), channel_id=1, source_target_pairs={{0,1},{1,5},{2,9},{3,13},{4,0},{5,4},{6,8},{7,12},{8,3},{9,7},{10,... | collective-permute-start | bytes 98312 | tf_op jit(solution)/shard_map/ppermute | solution.py:429
  0.5 8.5 %collective-permute-start = (bf16[32,512]{1,0:T(8,128)(2,1)}, bf16[32,512]{1,0:T(8,128)(2,1)S(1)}, u32[]{:S(2)}, u32[]{:S(2)}) collective-permute-start(bf16[32,512]{1,0:T(8,128)(2,1)} %bitcast.12), channel_id=1, source_target_pairs={{0,3},{1,7},{2,11},{3,15},{4,2},{5,6},{6,10},{7,14},{8,1},{9,5},{1... | collective-permute-start | bytes 98312 | tf_op jit(solution)/shard_map/ppermute | solution.py:429
  5.8 7.0 %collective-permute-start.8 = (bf16[128,512]{1,0:T(8,128)(2,1)}, bf16[128,512]{1,0:T(8,128)(2,1)S(1)}, u32[]{:S(2)}, u32[]{:S(2)}) collective-permute-start(bf16[128,512]{1,0:T(8,128)(2,1)} %param.12), channel_id=1, source_target_pairs={{0,3},{1,2},{2,1},{3,0},{4,7},{5,6},{6,5},{7,4},{8,11},{9,10},{10,... | collective-permute-start | bytes 393224 | tf_op jit(solution)/shard_map/ppermute | solution.py:159
  9.1 1.4 %collective-permute-start.3 = (bf16[32,512]{1,0:T(8,128)(2,1)S(1)}, bf16[32,512]{1,0:T(8,128)(2,1)S(1)}, u32[]{:S(2)}, u32[]{:S(2)}) collective-permute-start(bf16[32,512]{1,0:T(8,128)(2,1)S(1)} %collective-permute-done.refs_3_), channel_id=1, source_target_pairs={{0,1},{1,0},{2,3},{3,2},{4,5},{5,4},{6,7},{7,6},{8,9},{9,8},{10,11... | collective-permute-start | bytes 98312 | tf_op jit(solution)/shard_map/ppermute | solution.py:159
  9.6 5.5 %collective-permute-start.7 = (bf16[128,512]{1,0:T(8,128)(2,1)S(1)}, bf16[128,512]{1,0:T(8,128)(2,1)S(1)}, u32[]{:S(2)}, u32[]{:S(2)}) collective-permute-start(bf16[128,512]{1,0:T(8,128)(2,1)S(1)} %copy-done.4), channel_id=1, source_target_pairs={{0,1},{1,0},{2,3},{3,2},{4,5},{5,4},{6,7},{7,6},{8,9},{9,8},{10,11... | collective-permute-start | bytes 393224 | tf_op jit(solution)/shard_map/ppermute | solution.py:159
  11.1 3.4 %collective-permute-start.5 = (bf16[128,128]{1,0:T(8,128)(2,1)S(1)}, bf16[128,128]{1,0:T(8,128)(2,1)S(1)}, u32[]{:S(2)}, u32[]{:S(2)}) collective-permute-start(bf16[128,128]{1,0:T(8,128)(2,1)S(1)} %get-tuple-element.26.refs_0_), channel_id=1, source_target_pairs={{0,3},{1,2},{2,1},{3,0},{4,7},{5,6},{6,5},{7,4},{8,11},{9,10},{10,... | collective-permute-start | bytes 98312 | tf_op jit(solution)/shard_map/ppermute | solution.py:159
  12.7 3.0 %collective-permute-start.9 = (bf16[128,512]{1,0:T(8,128)(2,1)S(1)}, bf16[128,512]{1,0:T(8,128)(2,1)S(1)}, u32[]{:S(2)}, u32[]{:S(2)}) collective-permute-start(bf16[128,512]{1,0:T(8,128)(2,1)S(1)} %collective-permute-done.8.refs_6_), channel_id=1, source_target_pairs={{0,1},{1,0},{2,3},{3,2},{4,5},{5,4},{6,7},{7,6},{8,9},{9,8},{10,11... | collective-permute-start | bytes 393224 | tf_op jit(solution)/shard_map/ppermute | solution.py:159
  13.1 2.0 %collective-permute-start.4 = (bf16[128,128]{1,0:T(8,128)(2,1)S(1)}, bf16[128,128]{1,0:T(8,128)(2,1)S(1)}, u32[]{:S(2)}, u32[]{:S(2)}) collective-permute-start(bf16[128,128]{1,0:T(8,128)(2,1)S(1)} %get-tuple-element.26.refs_0_), channel_id=1, source_target_pairs={{0,1},{1,0},{2,3},{3,2},{4,5},{5,4},{6,7},{7,6},{8,9},{9,8},{10,11... | collective-permute-start | bytes 98312 | tf_op jit(solution)/shard_map/ppermute | solution.py:159
  14.5 1.2 %collective-permute-start.6 = (bf16[128,128]{1,0:T(8,128)(2,1)S(1)}, bf16[128,128]{1,0:T(8,128)(2,1)S(1)}, u32[]{:S(2)}, u32[]{:S(2)}) collective-permute-start(bf16[128,128]{1,0:T(8,128)(2,1)S(1)} %collective-permute-done.5.refs_3_), channel_id=1, source_target_pairs={{0,1},{1,0},{2,3},{3,2},{4,5},{5,4},{6,7},{7,6},{8,9},{9,8},{10,11... | collective-permute-start | bytes 98312 | tf_op jit(solution)/shard_map/ppermute | solution.py:159
  17.0 1.4 %collective-permute-start.10 = (f32[4,16,512]{2,1,0:T(8,128)S(1)}, f32[4,16,512]{2,1,0:T(8,128)S(1)}, u32[]{:S(2)}, u32[]{:S(2)}) collective-permute-start(f32[4,16,512]{2,1,0:T(8,128)S(1)} %get-tuple-element.29), channel_id=1, source_target_pairs={{0,1},{1,0},{2,3},{3,2},{4,5},{5,4},{6,7},{7,6},{8,9},{9,8},{10,11... | collective-permute-start | bytes 393224 | tf_op jit(solution)/shard_map/ppermute | solution.py:159
  18.4 4.0 %collective-permute-start.11 = (bf16[4,16,512]{2,1,0:T(8,128)(2,1)S(1)}, bf16[4,16,512]{2,1,0:T(8,128)(2,1)S(1)}, u32[]{:S(2)}, u32[]{:S(2)}) collective-permute-start(bf16[4,16,512]{2,1,0:T(8,128)(2,1)S(1)} %get-tuple-element.41), channel_id=1, source_target_pairs={{0,3},{1,2},{2,1},{3,0},{4,7},{5,6},{6,5},{7,4},{8,11},{9,10},{10,... | collective-permute-start | bytes 196616 | tf_op jit(solution)/shard_map/ppermute | solution.py:159
  22.5 6.6 %collective-permute-start.12 = (bf16[3,16,512]{2,1,0:T(8,128)(2,1)S(1)}, bf16[3,16,512]{2,1,0:T(8,128)(2,1)S(1)}, u32[]{:S(2)}, u32[]{:S(2)}) collective-permute-start(bf16[3,16,512]{2,1,0:T(8,128)(2,1)S(1)} %get-tuple-element.32), channel_id=1, source_target_pairs={{0,4},{4,8},{8,12},{12,0},{1,5},{5,9},{9,13},{13,1},{2,6},{6,10},{... | collective-permute-start | bytes 147464 | tf_op jit(solution)/shard_map/ppermute | solution.py:472
  22.7 7.9 %collective-permute-start.13 = (bf16[3,16,512]{2,1,0:T(8,128)(2,1)S(1)}, bf16[3,16,512]{2,1,0:T(8,128)(2,1)S(1)}, u32[]{:S(2)}, u32[]{:S(2)}) collective-permute-start(bf16[3,16,512]{2,1,0:T(8,128)(2,1)S(1)} %get-tuple-element.33), channel_id=1, source_target_pairs={{0,8},{4,12},{8,0},{12,4},{1,9},{5,13},{9,1},{13,5},{2,10},{6,14},... | collective-permute-start | bytes 147464 | tf_op jit(solution)/shard_map/ppermute | solution.py:472
  26.2 4.4 %collective-permute-start.14 = (bf16[3,16,512]{2,1,0:T(8,128)(2,1)S(1)}, bf16[3,16,512]{2,1,0:T(8,128)(2,1)S(1)}, u32[]{:S(2)}, u32[]{:S(2)}) collective-permute-start(bf16[3,16,512]{2,1,0:T(8,128)(2,1)S(1)} %get-tuple-element.34), channel_id=1, source_target_pairs={{0,12},{4,0},{8,4},{12,8},{1,13},{5,1},{9,5},{13,9},{2,14},{6,2},{... | collective-permute-start | bytes 147464 | tf_op jit(solution)/shard_map/ppermute | solution.py:472
  26.6 4.5 %collective-permute-start.15 = (bf16[3,16,512]{2,1,0:T(8,128)(2,1)S(1)}, bf16[3,16,512]{2,1,0:T(8,128)(2,1)S(1)}, u32[]{:S(2)}, u32[]{:S(2)}) collective-permute-start(bf16[3,16,512]{2,1,0:T(8,128)(2,1)S(1)} %get-tuple-element.31.refs_0_), channel_id=1, source_target_pairs={{0,1},{1,0},{2,3},{3,2},{4,5},{5,4},{6,7},{7,6},{8,9},{9,8},{10,11... | collective-permute-start | bytes 147464 | tf_op jit(solution)/shard_map/ppermute | solution.py:159
  29.1 1.9 %collective-permute-start.16 = (bf16[3,16,512]{2,1,0:T(8,128)(2,1)S(1)}, bf16[3,16,512]{2,1,0:T(8,128)(2,1)S(1)}, u32[]{:S(2)}, u32[]{:S(2)}) collective-permute-start(bf16[3,16,512]{2,1,0:T(8,128)(2,1)S(1)} %collective-permute-done.12.refs_1_), channel_id=1, source_target_pairs={{0,1},{1,0},{2,3},{3,2},{4,5},{5,4},{6,7},{7,6},{8,9},{9,8},{10,11... | collective-permute-start | bytes 147464 | tf_op jit(solution)/shard_map/ppermute | solution.py:159
  30.5 1.2 %collective-permute-start.17 = (bf16[3,16,512]{2,1,0:T(8,128)(2,1)S(1)}, bf16[3,16,512]{2,1,0:T(8,128)(2,1)S(1)}, u32[]{:S(2)}, u32[]{:S(2)}) collective-permute-start(bf16[3,16,512]{2,1,0:T(8,128)(2,1)S(1)} %collective-permute-done.13.refs_2_), channel_id=1, source_target_pairs={{0,1},{1,0},{2,3},{3,2},{4,5},{5,4},{6,7},{7,6},{8,9},{9,8},{10,11... | collective-permute-start | bytes 147464 | tf_op jit(solution)/shard_map/ppermute | solution.py:159
  30.6 1.3 %collective-permute-start.18 = (bf16[3,16,512]{2,1,0:T(8,128)(2,1)S(1)}, bf16[3,16,512]{2,1,0:T(8,128)(2,1)S(1)}, u32[]{:S(2)}, u32[]{:S(2)}) collective-permute-start(bf16[3,16,512]{2,1,0:T(8,128)(2,1)S(1)} %collective-permute-done.14.refs_3_), channel_id=1, source_target_pairs={{0,1},{1,0},{2,3},{3,2},{4,5},{5,4},{6,7},{7,6},{8,9},{9,8},{10,11... | collective-permute-start | bytes 147464 | tf_op jit(solution)/shard_map/ppermute | solution.py:159
  33.4 4.0 %collective-permute-start.19 = (bf16[4,4,16,128]{3,2,1,0:T(8,128)(2,1)S(1)}, bf16[4,4,16,128]{3,2,1,0:T(8,128)(2,1)S(1)}, u32[]{:S(2)}, u32[]{:S(2)}) collective-permute-start(bf16[4,4,16,128]{3,2,1,0:T(8,128)(2,1)S(1)} %get-tuple-element.35.own), channel_id=1, source_target_pairs={{0,3},{1,2},{2,1},{3,0},{4,7},{5,6},{6,5},{7,4},{8,11},{9,10},{10,... | collective-permute-start | bytes 196616 | tf_op jit(solution)/shard_map/ppermute | solution.py:159
  35.0 2.7 %collective-permute-start.21 = (bf16[4,4,16,128]{3,2,1,0:T(8,128)(2,1)S(1)}, bf16[4,4,16,128]{3,2,1,0:T(8,128)(2,1)S(1)}, u32[]{:S(2)}, u32[]{:S(2)}) collective-permute-start(bf16[4,4,16,128]{3,2,1,0:T(8,128)(2,1)S(1)} %get-tuple-element.35.own), channel_id=1, source_target_pairs={{0,1},{1,0},{2,3},{3,2},{4,5},{5,4},{6,7},{7,6},{8,9},{9,8},{10,11... | collective-permute-start | bytes 196616 | tf_op jit(solution)/shard_map/ppermute | solution.py:159
  37.4 1.3 %collective-permute-start.20 = (bf16[4,4,16,128]{3,2,1,0:T(8,128)(2,1)S(1)}, bf16[4,4,16,128]{3,2,1,0:T(8,128)(2,1)S(1)}, u32[]{:S(2)}, u32[]{:S(2)}) collective-permute-start(bf16[4,4,16,128]{3,2,1,0:T(8,128)(2,1)S(1)} %collective-permute-done.19.refs_1_), channel_id=1, source_target_pairs={{0,1},{1,0},{2,3},{3,2},{4,5},{5,4},{6,7},{7,6},{8,9},{9,8},{10,11... | collective-permute-start | bytes 196616 | tf_op jit(solution)/shard_map/ppermute | solution.py:159
  39.3 3.1 %collective-permute-start.22 = (bf16[32,128]{1,0:T(8,128)(2,1)S(1)}, bf16[32,128]{1,0:T(8,128)(2,1)S(1)}, u32[]{:S(2)}, u32[]{:S(2)}) collective-permute-start(bf16[32,128]{1,0:T(8,128)(2,1)S(1)} %get-tuple-element.38), channel_id=1, source_target_pairs={{0,1},{1,2},{2,3},{3,0},{4,5},{5,6},{6,7},{7,4},{8,9},{9,10},{10,1... | collective-permute-start | bytes 24584 | tf_op jit(solution)/shard_map/ppermute | solution.py:506
  39.6 3.7 %collective-permute-start.23 = (bf16[32,128]{1,0:T(8,128)(2,1)S(1)}, bf16[32,128]{1,0:T(8,128)(2,1)S(1)}, u32[]{:S(2)}, u32[]{:S(2)}) collective-permute-start(bf16[32,128]{1,0:T(8,128)(2,1)S(1)} %get-tuple-element.39), channel_id=1, source_target_pairs={{0,2},{1,3},{2,0},{3,1},{4,6},{5,7},{6,4},{7,5},{8,10},{9,11},{10,... | collective-permute-start | bytes 24584 | tf_op jit(solution)/shard_map/ppermute | solution.py:506
  41.2 2.5 %collective-permute-start.24 = (bf16[32,128]{1,0:T(8,128)(2,1)S(1)}, bf16[32,128]{1,0:T(8,128)(2,1)S(1)}, u32[]{:S(2)}, u32[]{:S(2)}) collective-permute-start(bf16[32,128]{1,0:T(8,128)(2,1)S(1)} %get-tuple-element.40), channel_id=1, source_target_pairs={{0,3},{1,0},{2,1},{3,2},{4,7},{5,4},{6,5},{7,6},{8,11},{9,8},{10,9... | collective-permute-start | bytes 24584 | tf_op jit(solution)/shard_map/ppermute | solution.py:506
  (8 other events, 100.7 us)

commit v7 on v6

--- a/solution.py
+++ b/solution.py
@@ -225,8 +225,10 @@
     table = jnp.where(head_in == head_out, table, 0.0)
     high = table.astype(jnp.bfloat16)
     low = (table - high.astype(jnp.float32)).astype(jnp.bfloat16)
-    both = jnp.dot(query, high, preferred_element_type=jnp.float32) + jnp.dot(
-        query, low, preferred_element_type=jnp.float32
+    both = jnp.dot(
+        jnp.concatenate([query, query], axis=1),
+        jnp.concatenate([high, low], axis=0),
+        preferred_element_type=jnp.float32,
     )
     mixed_ref[...] = (both[:, :share] / jnp.maximum(both[:, share:], 1.0)).astype(jnp.bfloat16)
 
@@ -240,9 +242,10 @@
     share = mixed[0].shape[1]
     own_out, down = weights[pl.ds(3 * share, share)], weights[pl.ds(4 * share, units)]
     height = tokens // columns
-    attn_out = sum(
-        jnp.dot(a[...], b, preferred_element_type=jnp.float32)
-        for a, b in zip(mixed, [own_out] + [piece[...] for piece in out_weight])
+    attn_out = jnp.dot(
+        jnp.concatenate([piece[...] for piece in mixed], axis=1),
+        jnp.concatenate([own_out] + [piece[...] for piece in out_weight], axis=0),
+        preferred_element_type=jnp.float32,
     )
     first = (cells[...].astype(jnp.float32) + norm_rows(attn_out, scales[18:19])).astype(jnp.bfloat16)
     column = lax.rem(lax.broadcasted_iota(jnp.int32, (tokens, units), 0), columns)
@@ -294,29 +297,32 @@
         out[...] = framed[pl.ds(lax.rem(level + mask, len(outs)) * step, step + 2)]
 
 
-def conv_taps(field, kernel, lane=0, total=0.0):
+def conv_taps(field, kernel, lane=0, total=0.0, upright=True):
     frames, rows = field.shape[0] - 2, field.shape[1] - 2
     columns, width = field.shape[2:]
     share = kernel.shape[3]
-    tokens = frames * rows * columns
     for shift_time in range(3):
         for shift_row in range(3):
             slab = field[shift_time : shift_time + frames, shift_row : shift_row + rows]
+            slab = slab.reshape(frames * rows * columns, width)
+            taps = kernel[shift_time, shift_row, :, :, pl.ds(lane, width)].reshape(-1, width)
             total = total + lax.dot_general(
-                slab.reshape(tokens, width),
-                kernel[shift_time, shift_row, :, :, pl.ds(lane, width)].reshape(3 * share, width),
+                *((slab, taps) if upright else (taps, slab)),
                 (((1,), (1,)), ((), ())),
                 preferred_element_type=jnp.float32,
             )
     return total
 
 
-def conv_join(total, columns):
-    tokens, share = total.shape[0], total.shape[1] // 3
-    column = lax.rem(lax.broadcasted_iota(jnp.int32, (tokens, share), 0), columns)
-    before = jnp.where(column > 0, pltpu.roll(total[:, :share], 1, 0), 0.0)
-    after = jnp.where(column < columns - 1, pltpu.roll(total[:, 2 * share :], tokens - 1, 0), 0.0)
-    return before + total[:, share : 2 * share] + after
+def conv_join(total, columns, upright=True):
+    axis = 0 if upright else 1
+    left, middle, right = jnp.split(total, 3, axis=1 - axis)
+    tokens = left.shape[axis]
+    column = lax.rem(lax.broadcasted_iota(jnp.int32, left.shape, axis), columns)
+    before = jnp.where(column > 0, pltpu.roll(left, 1, axis), 0.0)
+    after = jnp.where(column < columns - 1, pltpu.roll(right, tokens - 1, axis), 0.0)
+    result = before + middle + after
+    return result if upright else result.T
 
 
 def clear_ends(field):
@@ -338,7 +344,8 @@
             field[frame, 2 * row + parity] = piece[row]
     frames, band, columns, share = hidden_ref.shape
     rows = band - 2
-    activated = silu(conv_join(conv_taps(field, kernel), columns).reshape(hidden_ref.shape))
+    total = conv_taps(field, kernel, upright=False)
+    activated = silu(conv_join(total, columns, upright=False).reshape(hidden_ref.shape))
     global_row = level * rows - 1 + lax.broadcasted_iota(jnp.int32, activated.shape, 1)
     inside = (global_row >= 0) & (global_row < height)
     hidden_ref[...] = jnp.where(inside, activated, 0.0).astype(jnp.bfloat16)
@@ -421,7 +428,7 @@
     bf16, f32 = jnp.bfloat16, jnp.float32
     own = latent.reshape(rows * columns, width)
     pieces = [None] * count
-    masks = [*range(3, count, 2), 1]
+    masks = [*range(2, count, 2), 1]
     for mask in masks:
         pairs = [
             (z * count + f, f * count + (z ^ mask)) for z in range(count) for f in range(count)
@@ -467,7 +474,7 @@
         flops=8 * total.size,
     )
     windows = list(windows)
-    for mask in (1, 2, 3):
+    for mask in range(1, count):
         pairs = [(i, (i + mask) % count) for i in range(count)]
         windows[mask] = lax.ppermute(windows[mask], "row", pairs)
     others = [swap(window, 1) for window in windows]
@@ -501,7 +508,7 @@
         room=8,
     )
     outs = list(strips)
-    for mask in (2, 1, 3):
+    for mask in range(1, count):
         pairs = [(i, (i + mask) % count) for i in range(count)]
         outs[mask] = lax.ppermute(strips[mask], "frame", pairs)
     (decoded,) = call(join_body, outs, [((count, rows, strip, width), bf16)])
@@ -509,7 +516,9 @@
 
 
 def solution(mesh):
-    body = by_frames if mesh.shape["row"] == mesh.shape["frame"] else local
+    count = mesh.shape["frame"]
+    square = mesh.shape["row"] == count > 1 and count & (count - 1) == 0
+    body = by_frames if square else local
     in_specs = (
         P(("parts", "frame"), "row", None, None),
         P(None, "frame", None),

time: 44.6 us -> 44.4 us (level)
  waiting for transfers between devices: 16.2 us -> 15.5 us
    ppermute x2, waiting for transfers between devices: 1.35 us -> 0.01 us  [by_frames(): pieces[mask] = lax.ppermute(own, ('row', 'frame'), pairs)]
    ppermute x17, starting transfers between devices: 8.22 us -> 9.32 us  [swap(): return lax.ppermute(cells, 'frame', [(i, i ^ mask) for i in range(count)])]
    ppermute x2, starting transfers between devices: 5.74 us -> 5.01 us  [by_frames(): pieces[mask] = lax.ppermute(own, ('row', 'frame'), pairs)]
    ppermute x17, waiting for transfers between devices: 9.46 us -> 10.2 us  [swap(): return lax.ppermute(cells, 'frame', [(i, i ^ mask) for i in range(count)])]
where the time goes in v7:
time: 44.4 us; the launch traced here: 43.9 us
  starting transfers between devices  21.5 us (48%)
  waiting for transfers between devices  15.5 us (35%)
  Pallas kernels  5.23 us (12%)
  other arithmetic  1.29 us (3%)
    ppermute x17, waiting for transfers between devices, swap(): return lax.ppermute(cells, 'frame', [(i, i ^ mask) for i in range(count)])  10.2 us
    ppermute x17, starting transfers between devices, swap(): return lax.ppermute(cells, 'frame', [(i, i ^ mask) for i in range(count)])  9.32 us
    pallas_call x7, Pallas kernels, call(): pl.pallas_call(body, out_shape=[jax.ShapeDtypeStruct(shape, kind) for sha...  5.23 us
    ppermute x2, starting transfers between devices, by_frames(): pieces[mask] = lax.ppermute(own, ('row', 'frame'), pairs)  5.01 us
    ppermute x3, starting transfers between devices, by_frames(): windows[mask] = lax.ppermute(windows[mask], 'row', pairs)  4.29 us
    ppermute x3, waiting for transfers between devices, by_frames(): windows[mask] = lax.ppermute(windows[mask], 'row', pairs)  3.99 us
    ppermute x3, starting transfers between devices, by_frames(): outs[mask] = lax.ppermute(strips[mask], 'frame', pairs)  2.84 us
    ppermute x3, waiting for transfers between devices, by_frames(): outs[mask] = lax.ppermute(strips[mask], 'frame', pairs)  1.37 us
  transfers between devices with their start and end apart: 25, of which 16 were waited for; matrix products, arithmetic and copies ran while one was open for 3% of the time, Pallas kernels for 3%

profile of v7, /device:TPU:0, one launch (start us, length us, event | category | flops | bytes accessed | tf_op | source)
XLA Modules:
  0.0 43.9 jit_solution(15531522276454563709)
XLA Ops:
  0.5 4.5 %collective-permute-start = (bf16[32,512]{1,0:T(8,128)(2,1)}, bf16[32,512]{1,0:T(8,128)(2,1)S(1)}, u32[]{:S(2)}, u32[]{:S(2)}) collective-permute-start(bf16[32,512]{1,0:T(8,128)(2,1)} %bitcast.12), channel_id=1, source_target_pairs={{0,2},{1,6},{2,10},{3,14},{4,3},{5,7},{6,11},{7,15},{8,0},{9,4},{1... | collective-permute-start | bytes 98312 | tf_op jit(solution)/shard_map/ppermute | solution.py:436
  5.0 1.8 %collective-permute-start.8 = (bf16[128,512]{1,0:T(8,128)(2,1)}, bf16[128,512]{1,0:T(8,128)(2,1)S(1)}, u32[]{:S(2)}, u32[]{:S(2)}) collective-permute-start(bf16[128,512]{1,0:T(8,128)(2,1)} %param.12), channel_id=1, source_target_pairs={{0,3},{1,2},{2,1},{3,0},{4,7},{5,6},{6,5},{7,4},{8,11},{9,10},{10,... | collective-permute-start | bytes 393224 | tf_op jit(solution)/shard_map/ppermute | solution.py:159
  6.8 1.3 %pad_maximum_fusion.refs_4_.refs_8_ = bf16[1024,512]{1,0:T(8,128)(2,1)S(1)} fusion(bf16[512,512]{1,0:T(8,128)(2,1)} %param.16, bf16[128,512]{1,0:T(8,128)(2,1)} %param.12, bf16[384,512]{1,0:T(8,128)(2,1)} %bitcast.8), kind=kLoop, calls=%fused_computation | loop fusion | flops 3145728 | bytes 2097152 | tf_op jit(solution)/shard_map/concatenate | solution.py:437
  8.1 0.7 %collective-permute-start.2 = (bf16[32,512]{1,0:T(8,128)(2,1)S(1)}, bf16[32,512]{1,0:T(8,128)(2,1)S(1)}, u32[]{:S(2)}, u32[]{:S(2)}) collective-permute-start(bf16[32,512]{1,0:T(8,128)(2,1)S(1)} %collective-permute-done.1.refs_1_), channel_id=1, source_target_pairs={{0,1},{1,0},{2,3},{3,2},{4,5},{5,4},{6,7},{7,6},{8,9},{9,8},{10,11... | collective-permute-start | bytes 98312 | tf_op jit(solution)/shard_map/ppermute | solution.py:159
  10.0 0.7 %shard_map.100 = (bf16[128,128]{1,0:T(8,128)(2,1)S(1)}, bf16[128,512]{1,0:T(8,128)(2,1)S(1)}) custom-call(bf16[32,512]{1,0:T(8,128)(2,1)S(1)} %collective-permute-done.2.refs_0_, bf16[32,512]{1,0:T(8,128)(2,1)S(1)} %collective-permute-done.1.refs_1_, bf16[32,512]{1,0:T(8,128)(2,1)S(1)} %collective-permute-done.refs_2_, ...), custom_call_target="tpu_custom_call" | custom-call | flops 50331648 | bytes 1179648 | tf_op jit(solution)/shard_map/pallas_call | solution.py:193
  10.7 1.7 %collective-permute-start.5 = (bf16[128,128]{1,0:T(8,128)(2,1)S(1)}, bf16[128,128]{1,0:T(8,128)(2,1)S(1)}, u32[]{:S(2)}, u32[]{:S(2)}) collective-permute-start(bf16[128,128]{1,0:T(8,128)(2,1)S(1)} %get-tuple-element.26.refs_0_), channel_id=1, source_target_pairs={{0,3},{1,2},{2,1},{3,0},{4,7},{5,6},{6,5},{7,4},{8,11},{9,10},{10,... | collective-permute-start | bytes 98312 | tf_op jit(solution)/shard_map/ppermute | solution.py:159
  13.0 1.1 %collective-permute-done.5.refs_3_ = bf16[128,128]{1,0:T(8,128)(2,1)S(1)} collective-permute-done((bf16[128,128]{1,0:T(8,128)(2,1)S(1)}, bf16[128,128]{1,0:T(8,128)(2,1)S(1)}, u32[]{:S(2)}, u32[]{:S(2)}) %collective-permute-start.5) | collective-permute-done | bytes 32800 | tf_op jit(solution)/shard_map/ppermute | solution.py:159
  14.5 0.7 %collective-permute-done.6.refs_2_ = bf16[128,128]{1,0:T(8,128)(2,1)S(1)} collective-permute-done((bf16[128,128]{1,0:T(8,128)(2,1)S(1)}, bf16[128,128]{1,0:T(8,128)(2,1)S(1)}, u32[]{:S(2)}, u32[]{:S(2)}) %collective-permute-start.6) | collective-permute-done | bytes 32800 | tf_op jit(solution)/shard_map/ppermute | solution.py:159
  15.3 1.2 %shard_map.101 = (f32[4,16,512]{2,1,0:T(8,128)S(1)}, f32[4,16,512]{2,1,0:T(8,128)S(1)}, bf16[4,16,512]{2,1,0:T(8,128)(2,1)S(1)}) custom-call(bf16[128,128]{1,0:T(8,128)(2,1)S(1)} %get-tuple-element.26.refs_0_, bf16[128,128]{1,0:T(8,128)(2,1)S(1)} %collective-permute-done.4.refs_1_, bf16[128,128]{1,0:T(8,128)(2,1)S(1)} %collective-permute-done.6.refs_2_, ...), custom_call_target="tpu_custom_call" | custom-call | flops 268435456 | bytes 2793472 | tf_op jit(solution)/shard_map/pallas_call | solution.py:193
  16.8 1.1 %collective-permute-done.10 = f32[4,16,512]{2,1,0:T(8,128)S(1)} collective-permute-done((f32[4,16,512]{2,1,0:T(8,128)S(1)}, f32[4,16,512]{2,1,0:T(8,128)S(1)}, u32[]{:S(2)}, u32[]{:S(2)}) %collective-permute-start.10) | collective-permute-done | bytes 131104 | tf_op jit(solution)/shard_map/ppermute | solution.py:159
  17.9 1.7 %collective-permute-start.11 = (bf16[4,16,512]{2,1,0:T(8,128)(2,1)S(1)}, bf16[4,16,512]{2,1,0:T(8,128)(2,1)S(1)}, u32[]{:S(2)}, u32[]{:S(2)}) collective-permute-start(bf16[4,16,512]{2,1,0:T(8,128)(2,1)S(1)} %get-tuple-element.41), channel_id=1, source_target_pairs={{0,3},{1,2},{2,1},{3,0},{4,7},{5,6},{6,5},{7,4},{8,11},{9,10},{10,... | collective-permute-start | bytes 196616 | tf_op jit(solution)/shard_map/ppermute | solution.py:159
  19.6 2.4 %collective-permute-done.11.refs_3_ = bf16[4,16,512]{2,1,0:T(8,128)(2,1)S(1)} collective-permute-done((bf16[4,16,512]{2,1,0:T(8,128)(2,1)S(1)}, bf16[4,16,512]{2,1,0:T(8,128)(2,1)S(1)}, u32[]{:S(2)}, u32[]{:S(2)}) %collective-permute-start.11) | collective-permute-done | bytes 65568 | tf_op jit(solution)/shard_map/ppermute | solution.py:159
  22.6 3.5 %collective-permute-start.13 = (bf16[3,16,512]{2,1,0:T(8,128)(2,1)S(1)}, bf16[3,16,512]{2,1,0:T(8,128)(2,1)S(1)}, u32[]{:S(2)}, u32[]{:S(2)}) collective-permute-start(bf16[3,16,512]{2,1,0:T(8,128)(2,1)S(1)} %get-tuple-element.33), channel_id=1, source_target_pairs={{0,8},{4,12},{8,0},{12,4},{1,9},{5,13},{9,1},{13,5},{2,10},{6,14},... | collective-permute-start | bytes 147464 | tf_op jit(solution)/shard_map/ppermute | solution.py:479
  26.4 2.1 %collective-permute-done.12.refs_1_ = bf16[3,16,512]{2,1,0:T(8,128)(2,1)S(1)} collective-permute-done((bf16[3,16,512]{2,1,0:T(8,128)(2,1)S(1)}, bf16[3,16,512]{2,1,0:T(8,128)(2,1)S(1)}, u32[]{:S(2)}, u32[]{:S(2)}) %collective-permute-start.12) | collective-permute-done | bytes 49184 | tf_op jit(solution)/shard_map/ppermute | solution.py:479
  28.5 1.4 %collective-permute-done.13.refs_2_ = bf16[3,16,512]{2,1,0:T(8,128)(2,1)S(1)} collective-permute-done((bf16[3,16,512]{2,1,0:T(8,128)(2,1)S(1)}, bf16[3,16,512]{2,1,0:T(8,128)(2,1)S(1)}, u32[]{:S(2)}, u32[]{:S(2)}) %collective-permute-start.13) | collective-permute-done | bytes 49184 | tf_op jit(solution)/shard_map/ppermute | solution.py:479
  30.5 0.7 %collective-permute-done.17.refs_6_ = bf16[3,16,512]{2,1,0:T(8,128)(2,1)S(1)} collective-permute-done((bf16[3,16,512]{2,1,0:T(8,128)(2,1)S(1)}, bf16[3,16,512]{2,1,0:T(8,128)(2,1)S(1)}, u32[]{:S(2)}, u32[]{:S(2)}) %collective-permute-start.17) | collective-permute-done | bytes 49184 | tf_op jit(solution)/shard_map/ppermute | solution.py:159
  31.7 1.3 %shard_map.103 = (bf16[4,4,16,128]{3,2,1,0:T(8,128)(2,1)S(1)}, bf16[4,2,16,128]{3,2,1,0:T(8,128)(2,1)S(1)}) custom-call(bf16[3,16,512]{2,1,0:T(8,128)(2,1)S(1)} %get-tuple-element.31.refs_0_, bf16[3,16,512]{2,1,0:T(8,128)(2,1)S(1)} %collective-permute-done.12.refs_1_, bf16[3,16,512]{2,1,0:T(8,128)(2,1)S(1)} %collective-permute-done.13.refs_2_, ...), custom_call_target="tpu_custom_call" | custom-call | flops 905969664 | bytes 3932160 | tf_op jit(solution)/shard_map/pallas_call | solution.py:193
  33.0 1.5 %collective-permute-start.19 = (bf16[4,4,16,128]{3,2,1,0:T(8,128)(2,1)S(1)}, bf16[4,4,16,128]{3,2,1,0:T(8,128)(2,1)S(1)}, u32[]{:S(2)}, u32[]{:S(2)}) collective-permute-start(bf16[4,4,16,128]{3,2,1,0:T(8,128)(2,1)S(1)} %get-tuple-element.35.own), channel_id=1, source_target_pairs={{0,3},{1,2},{2,1},{3,0},{4,7},{5,6},{6,5},{7,4},{8,11},{9,10},{10,... | collective-permute-start | bytes 196616 | tf_op jit(solution)/shard_map/ppermute | solution.py:159
  34.6 2.5 %collective-permute-done.19.refs_1_ = bf16[4,4,16,128]{3,2,1,0:T(8,128)(2,1)S(1)} collective-permute-done((bf16[4,4,16,128]{3,2,1,0:T(8,128)(2,1)S(1)}, bf16[4,4,16,128]{3,2,1,0:T(8,128)(2,1)S(1)}, u32[]{:S(2)}, u32[]{:S(2)}) %collective-permute-start.19) | collective-permute-done | bytes 65568 | tf_op jit(solution)/shard_map/ppermute | solution.py:159
  37.3 0.7 %shard_map.104.refs_2_ = f32[128,384]{1,0:T(8,128)S(1)} custom-call(bf16[4,4,16,128]{3,2,1,0:T(8,128)(2,1)S(1)} %get-tuple-element.35.own, bf16[4,4,16,128]{3,2,1,0:T(8,128)(2,1)S(1)} %collective-permute-done.21.other, bf16[3,3,3,128,512]{4,3,2,1,0:T(8,128)(2,1)S(1)} %copy-done.1), custom_call_target="tpu_custom_call" | custom-call | flops 226492416 | bytes 3670016 | tf_op jit(solution)/shard_map/pallas_call | solution.py:193
  38.4 0.7 %shard_map.105 = (bf16[32,128]{1,0:T(8,128)(2,1)S(1)}, bf16[32,128]{1,0:T(8,128)(2,1)S(1)}, bf16[32,128]{1,0:T(8,128)(2,1)S(1)}, bf16[32,128]{1,0:T(8,128)(2,1)S(1)}) custom-call(bf16[4,4,16,128]{3,2,1,0:T(8,128)(2,1)S(1)} %collective-permute-done.20.refs_0_, bf16[4,4,16,128]{3,2,1,0:T(8,128)(2,1)S(1)} %collective-permute-done.19.refs_1_, ...), custom_call_target="tpu_custom_call" | custom-call | flops 226492416 | bytes 3899392 | tf_op jit(solution)/shard_map/pallas_call | solution.py:193
  39.3 1.4 %collective-permute-start.23 = (bf16[32,128]{1,0:T(8,128)(2,1)S(1)}, bf16[32,128]{1,0:T(8,128)(2,1)S(1)}, u32[]{:S(2)}, u32[]{:S(2)}) collective-permute-start(bf16[32,128]{1,0:T(8,128)(2,1)S(1)} %get-tuple-element.39), channel_id=1, source_target_pairs={{0,2},{1,3},{2,0},{3,1},{4,6},{5,7},{6,4},{7,5},{8,10},{9,11},{10,... | collective-permute-start | bytes 24584 | tf_op jit(solution)/shard_map/ppermute | solution.py:513
  40.7 1.2 %collective-permute-start.24 = (bf16[32,128]{1,0:T(8,128)(2,1)S(1)}, bf16[32,128]{1,0:T(8,128)(2,1)S(1)}, u32[]{:S(2)}, u32[]{:S(2)}) collective-permute-start(bf16[32,128]{1,0:T(8,128)(2,1)S(1)} %get-tuple-element.40), channel_id=1, source_target_pairs={{0,3},{1,0},{2,1},{3,2},{4,7},{5,4},{6,5},{7,6},{8,11},{9,8},{10,9... | collective-permute-start | bytes 24584 | tf_op jit(solution)/shard_map/ppermute | solution.py:513
  42.2 0.7 %collective-permute-done.23.refs_2_ = bf16[32,128]{1,0:T(8,128)(2,1)S(1)} collective-permute-done((bf16[32,128]{1,0:T(8,128)(2,1)S(1)}, bf16[32,128]{1,0:T(8,128)(2,1)S(1)}, u32[]{:S(2)}, u32[]{:S(2)}) %collective-permute-start.23) | collective-permute-done | bytes 8224 | tf_op jit(solution)/shard_map/ppermute | solution.py:513
  (53 shorter events, 7.2 us)
Async XLA Ops:
  0.0 8.0 %collective-permute-start.1 = (bf16[32,512]{1,0:T(8,128)(2,1)}, bf16[32,512]{1,0:T(8,128)(2,1)S(1)}, u32[]{:S(2)}, u32[]{:S(2)}) collective-permute-start(bf16[32,512]{1,0:T(8,128)(2,1)} %bitcast.11), channel_id=1, source_target_pairs={{0,1},{1,5},{2,9},{3,13},{4,0},{5,4},{6,8},{7,12},{8,3},{9,7},{10,... | collective-permute-start | bytes 98312 | tf_op jit(solution)/shard_map/ppermute | solution.py:436
  0.5 7.5 %collective-permute-start = (bf16[32,512]{1,0:T(8,128)(2,1)}, bf16[32,512]{1,0:T(8,128)(2,1)S(1)}, u32[]{:S(2)}, u32[]{:S(2)}) collective-permute-start(bf16[32,512]{1,0:T(8,128)(2,1)} %bitcast.12), channel_id=1, source_target_pairs={{0,2},{1,6},{2,10},{3,14},{4,3},{5,7},{6,11},{7,15},{8,0},{9,4},{1... | collective-permute-start | bytes 98312 | tf_op jit(solution)/shard_map/ppermute | solution.py:436
  5.0 7.3 %collective-permute-start.8 = (bf16[128,512]{1,0:T(8,128)(2,1)}, bf16[128,512]{1,0:T(8,128)(2,1)S(1)}, u32[]{:S(2)}, u32[]{:S(2)}) collective-permute-start(bf16[128,512]{1,0:T(8,128)(2,1)} %param.12), channel_id=1, source_target_pairs={{0,3},{1,2},{2,1},{3,0},{4,7},{5,6},{6,5},{7,4},{8,11},{9,10},{10,... | collective-permute-start | bytes 393224 | tf_op jit(solution)/shard_map/ppermute | solution.py:159
  8.1 1.6 %collective-permute-start.2 = (bf16[32,512]{1,0:T(8,128)(2,1)S(1)}, bf16[32,512]{1,0:T(8,128)(2,1)S(1)}, u32[]{:S(2)}, u32[]{:S(2)}) collective-permute-start(bf16[32,512]{1,0:T(8,128)(2,1)S(1)} %collective-permute-done.1.refs_1_), channel_id=1, source_target_pairs={{0,1},{1,0},{2,3},{3,2},{4,5},{5,4},{6,7},{7,6},{8,9},{9,8},{10,11... | collective-permute-start | bytes 98312 | tf_op jit(solution)/shard_map/ppermute | solution.py:159
  8.8 1.2 %collective-permute-start.3 = (bf16[32,512]{1,0:T(8,128)(2,1)S(1)}, bf16[32,512]{1,0:T(8,128)(2,1)S(1)}, u32[]{:S(2)}, u32[]{:S(2)}) collective-permute-start(bf16[32,512]{1,0:T(8,128)(2,1)S(1)} %collective-permute-done.refs_2_), channel_id=1, source_target_pairs={{0,1},{1,0},{2,3},{3,2},{4,5},{5,4},{6,7},{7,6},{8,9},{9,8},{10,11... | collective-permute-start | bytes 98312 | tf_op jit(solution)/shard_map/ppermute | solution.py:159
  8.8 5.7 %collective-permute-start.7 = (bf16[128,512]{1,0:T(8,128)(2,1)S(1)}, bf16[128,512]{1,0:T(8,128)(2,1)S(1)}, u32[]{:S(2)}, u32[]{:S(2)}) collective-permute-start(bf16[128,512]{1,0:T(8,128)(2,1)S(1)} %copy-done.4), channel_id=1, source_target_pairs={{0,1},{1,0},{2,3},{3,2},{4,5},{5,4},{6,7},{7,6},{8,9},{9,8},{10,11... | collective-permute-start | bytes 393224 | tf_op jit(solution)/shard_map/ppermute | solution.py:159
  10.7 3.4 %collective-permute-start.5 = (bf16[128,128]{1,0:T(8,128)(2,1)S(1)}, bf16[128,128]{1,0:T(8,128)(2,1)S(1)}, u32[]{:S(2)}, u32[]{:S(2)}) collective-permute-start(bf16[128,128]{1,0:T(8,128)(2,1)S(1)} %get-tuple-element.26.refs_0_), channel_id=1, source_target_pairs={{0,3},{1,2},{2,1},{3,0},{4,7},{5,6},{6,5},{7,4},{8,11},{9,10},{10,... | collective-permute-start | bytes 98312 | tf_op jit(solution)/shard_map/ppermute | solution.py:159
  12.4 2.9 %collective-permute-start.9 = (bf16[128,512]{1,0:T(8,128)(2,1)S(1)}, bf16[128,512]{1,0:T(8,128)(2,1)S(1)}, u32[]{:S(2)}, u32[]{:S(2)}) collective-permute-start(bf16[128,512]{1,0:T(8,128)(2,1)S(1)} %collective-permute-done.8.refs_6_), channel_id=1, source_target_pairs={{0,1},{1,0},{2,3},{3,2},{4,5},{5,4},{6,7},{7,6},{8,9},{9,8},{10,11... | collective-permute-start | bytes 393224 | tf_op jit(solution)/shard_map/ppermute | solution.py:159
  12.8 1.8 %collective-permute-start.4 = (bf16[128,128]{1,0:T(8,128)(2,1)S(1)}, bf16[128,128]{1,0:T(8,128)(2,1)S(1)}, u32[]{:S(2)}, u32[]{:S(2)}) collective-permute-start(bf16[128,128]{1,0:T(8,128)(2,1)S(1)} %get-tuple-element.26.refs_0_), channel_id=1, source_target_pairs={{0,1},{1,0},{2,3},{3,2},{4,5},{5,4},{6,7},{7,6},{8,9},{9,8},{10,11... | collective-permute-start | bytes 98312 | tf_op jit(solution)/shard_map/ppermute | solution.py:159
  16.5 1.4 %collective-permute-start.10 = (f32[4,16,512]{2,1,0:T(8,128)S(1)}, f32[4,16,512]{2,1,0:T(8,128)S(1)}, u32[]{:S(2)}, u32[]{:S(2)}) collective-permute-start(f32[4,16,512]{2,1,0:T(8,128)S(1)} %get-tuple-element.29), channel_id=1, source_target_pairs={{0,1},{1,0},{2,3},{3,2},{4,5},{5,4},{6,7},{7,6},{8,9},{9,8},{10,11... | collective-permute-start | bytes 393224 | tf_op jit(solution)/shard_map/ppermute | solution.py:159
  17.9 4.1 %collective-permute-start.11 = (bf16[4,16,512]{2,1,0:T(8,128)(2,1)S(1)}, bf16[4,16,512]{2,1,0:T(8,128)(2,1)S(1)}, u32[]{:S(2)}, u32[]{:S(2)}) collective-permute-start(bf16[4,16,512]{2,1,0:T(8,128)(2,1)S(1)} %get-tuple-element.41), channel_id=1, source_target_pairs={{0,3},{1,2},{2,1},{3,0},{4,7},{5,6},{6,5},{7,4},{8,11},{9,10},{10,... | collective-permute-start | bytes 196616 | tf_op jit(solution)/shard_map/ppermute | solution.py:159
  22.1 6.4 %collective-permute-start.12 = (bf16[3,16,512]{2,1,0:T(8,128)(2,1)S(1)}, bf16[3,16,512]{2,1,0:T(8,128)(2,1)S(1)}, u32[]{:S(2)}, u32[]{:S(2)}) collective-permute-start(bf16[3,16,512]{2,1,0:T(8,128)(2,1)S(1)} %get-tuple-element.32), channel_id=1, source_target_pairs={{0,4},{4,8},{8,12},{12,0},{1,5},{5,9},{9,13},{13,1},{2,6},{6,10},{... | collective-permute-start | bytes 147464 | tf_op jit(solution)/shard_map/ppermute | solution.py:479
  22.6 7.4 %collective-permute-start.13 = (bf16[3,16,512]{2,1,0:T(8,128)(2,1)S(1)}, bf16[3,16,512]{2,1,0:T(8,128)(2,1)S(1)}, u32[]{:S(2)}, u32[]{:S(2)}) collective-permute-start(bf16[3,16,512]{2,1,0:T(8,128)(2,1)S(1)} %get-tuple-element.33), channel_id=1, source_target_pairs={{0,8},{4,12},{8,0},{12,4},{1,9},{5,13},{9,1},{13,5},{2,10},{6,14},... | collective-permute-start | bytes 147464 | tf_op jit(solution)/shard_map/ppermute | solution.py:479
  26.1 4.3 %collective-permute-start.14 = (bf16[3,16,512]{2,1,0:T(8,128)(2,1)S(1)}, bf16[3,16,512]{2,1,0:T(8,128)(2,1)S(1)}, u32[]{:S(2)}, u32[]{:S(2)}) collective-permute-start(bf16[3,16,512]{2,1,0:T(8,128)(2,1)S(1)} %get-tuple-element.34), channel_id=1, source_target_pairs={{0,12},{4,0},{8,4},{12,8},{1,13},{5,1},{9,5},{13,9},{2,14},{6,2},{... | collective-permute-start | bytes 147464 | tf_op jit(solution)/shard_map/ppermute | solution.py:479
  26.4 4.1 %collective-permute-start.15 = (bf16[3,16,512]{2,1,0:T(8,128)(2,1)S(1)}, bf16[3,16,512]{2,1,0:T(8,128)(2,1)S(1)}, u32[]{:S(2)}, u32[]{:S(2)}) collective-permute-start(bf16[3,16,512]{2,1,0:T(8,128)(2,1)S(1)} %get-tuple-element.31.refs_0_), channel_id=1, source_target_pairs={{0,1},{1,0},{2,3},{3,2},{4,5},{5,4},{6,7},{7,6},{8,9},{9,8},{10,11... | collective-permute-start | bytes 147464 | tf_op jit(solution)/shard_map/ppermute | solution.py:159
  28.5 2.0 %collective-permute-start.16 = (bf16[3,16,512]{2,1,0:T(8,128)(2,1)S(1)}, bf16[3,16,512]{2,1,0:T(8,128)(2,1)S(1)}, u32[]{:S(2)}, u32[]{:S(2)}) collective-permute-start(bf16[3,16,512]{2,1,0:T(8,128)(2,1)S(1)} %collective-permute-done.12.refs_1_), channel_id=1, source_target_pairs={{0,1},{1,0},{2,3},{3,2},{4,5},{5,4},{6,7},{7,6},{8,9},{9,8},{10,11... | collective-permute-start | bytes 147464 | tf_op jit(solution)/shard_map/ppermute | solution.py:159
  30.0 1.2 %collective-permute-start.17 = (bf16[3,16,512]{2,1,0:T(8,128)(2,1)S(1)}, bf16[3,16,512]{2,1,0:T(8,128)(2,1)S(1)}, u32[]{:S(2)}, u32[]{:S(2)}) collective-permute-start(bf16[3,16,512]{2,1,0:T(8,128)(2,1)S(1)} %collective-permute-done.13.refs_2_), channel_id=1, source_target_pairs={{0,1},{1,0},{2,3},{3,2},{4,5},{5,4},{6,7},{7,6},{8,9},{9,8},{10,11... | collective-permute-start | bytes 147464 | tf_op jit(solution)/shard_map/ppermute | solution.py:159
  30.4 1.2 %collective-permute-start.18 = (bf16[3,16,512]{2,1,0:T(8,128)(2,1)S(1)}, bf16[3,16,512]{2,1,0:T(8,128)(2,1)S(1)}, u32[]{:S(2)}, u32[]{:S(2)}) collective-permute-start(bf16[3,16,512]{2,1,0:T(8,128)(2,1)S(1)} %collective-permute-done.14.refs_3_), channel_id=1, source_target_pairs={{0,1},{1,0},{2,3},{3,2},{4,5},{5,4},{6,7},{7,6},{8,9},{9,8},{10,11... | collective-permute-start | bytes 147464 | tf_op jit(solution)/shard_map/ppermute | solution.py:159
  33.0 4.1 %collective-permute-start.19 = (bf16[4,4,16,128]{3,2,1,0:T(8,128)(2,1)S(1)}, bf16[4,4,16,128]{3,2,1,0:T(8,128)(2,1)S(1)}, u32[]{:S(2)}, u32[]{:S(2)}) collective-permute-start(bf16[4,4,16,128]{3,2,1,0:T(8,128)(2,1)S(1)} %get-tuple-element.35.own), channel_id=1, source_target_pairs={{0,3},{1,2},{2,1},{3,0},{4,7},{5,6},{6,5},{7,4},{8,11},{9,10},{10,... | collective-permute-start | bytes 196616 | tf_op jit(solution)/shard_map/ppermute | solution.py:159
  34.5 2.8 %collective-permute-start.21 = (bf16[4,4,16,128]{3,2,1,0:T(8,128)(2,1)S(1)}, bf16[4,4,16,128]{3,2,1,0:T(8,128)(2,1)S(1)}, u32[]{:S(2)}, u32[]{:S(2)}) collective-permute-start(bf16[4,4,16,128]{3,2,1,0:T(8,128)(2,1)S(1)} %get-tuple-element.35.own), channel_id=1, source_target_pairs={{0,1},{1,0},{2,3},{3,2},{4,5},{5,4},{6,7},{7,6},{8,9},{9,8},{10,11... | collective-permute-start | bytes 196616 | tf_op jit(solution)/shard_map/ppermute | solution.py:159
  37.1 1.3 %collective-permute-start.20 = (bf16[4,4,16,128]{3,2,1,0:T(8,128)(2,1)S(1)}, bf16[4,4,16,128]{3,2,1,0:T(8,128)(2,1)S(1)}, u32[]{:S(2)}, u32[]{:S(2)}) collective-permute-start(bf16[4,4,16,128]{3,2,1,0:T(8,128)(2,1)S(1)} %collective-permute-done.19.refs_1_), channel_id=1, source_target_pairs={{0,1},{1,0},{2,3},{3,2},{4,5},{5,4},{6,7},{7,6},{8,9},{9,8},{10,11... | collective-permute-start | bytes 196616 | tf_op jit(solution)/shard_map/ppermute | solution.py:159
  39.0 3.1 %collective-permute-start.22 = (bf16[32,128]{1,0:T(8,128)(2,1)S(1)}, bf16[32,128]{1,0:T(8,128)(2,1)S(1)}, u32[]{:S(2)}, u32[]{:S(2)}) collective-permute-start(bf16[32,128]{1,0:T(8,128)(2,1)S(1)} %get-tuple-element.38), channel_id=1, source_target_pairs={{0,1},{1,2},{2,3},{3,0},{4,5},{5,6},{6,7},{7,4},{8,9},{9,10},{10,1... | collective-permute-start | bytes 24584 | tf_op jit(solution)/shard_map/ppermute | solution.py:513
  39.3 3.7 %collective-permute-start.23 = (bf16[32,128]{1,0:T(8,128)(2,1)S(1)}, bf16[32,128]{1,0:T(8,128)(2,1)S(1)}, u32[]{:S(2)}, u32[]{:S(2)}) collective-permute-start(bf16[32,128]{1,0:T(8,128)(2,1)S(1)} %get-tuple-element.39), channel_id=1, source_target_pairs={{0,2},{1,3},{2,0},{3,1},{4,6},{5,7},{6,4},{7,5},{8,10},{9,11},{10,... | collective-permute-start | bytes 24584 | tf_op jit(solution)/shard_map/ppermute | solution.py:513
  40.7 2.5 %collective-permute-start.24 = (bf16[32,128]{1,0:T(8,128)(2,1)S(1)}, bf16[32,128]{1,0:T(8,128)(2,1)S(1)}, u32[]{:S(2)}, u32[]{:S(2)}) collective-permute-start(bf16[32,128]{1,0:T(8,128)(2,1)S(1)} %get-tuple-element.40), channel_id=1, source_target_pairs={{0,3},{1,0},{2,1},{3,2},{4,7},{5,4},{6,5},{7,6},{8,11},{9,8},{10,9... | collective-permute-start | bytes 24584 | tf_op jit(solution)/shard_map/ppermute | solution.py:513
  (8 other events, 98.1 us)

commit v8 on v7

--- a/solution.py
+++ b/solution.py
@@ -276,7 +276,7 @@
     first = first.reshape(height // 2, 2, columns, width)
     odd = half_of(place) == 1
     kept_ref[...] = jnp.where(odd, partial[:, 1], partial[:, 0])
-    sent_ref[...] = jnp.where(odd, partial[:, 0], partial[:, 1])
+    sent_ref[...] = jnp.where(odd, partial[:, 0], partial[:, 1]).astype(jnp.bfloat16)
     first_ref[...] = jnp.where(odd, first[:, 1], first[:, 0])
 
 
@@ -458,12 +458,12 @@
             in_parts,
             scales,
         ],
-        [((half, columns, width), f32)] * 2 + [((half, columns, width), bf16)],
+        [((half, columns, width), f32)] + [((half, columns, width), bf16)] * 2,
         scratch=[((tokens + 2 * columns, units), f32)],
         flops=2 * tokens * width * (width + 3 * units),
         room=8,
     )
-    total = kept + swap(sent, 1)
+    total = kept + swap(sent, 1).astype(f32)
     far = [swap(total.astype(bf16), mask) for mask in range(3, count, 2)]
     step = rows // 2
     windows = call(

time: 44.4 us -> 44.3 us (level)
  no operation moved by 1% of the time
where the time goes in v8:
time: 44.3 us; the launch traced here: 43.8 us
  starting transfers between devices  21.4 us (48%)
  waiting for transfers between devices  15.4 us (35%)
  Pallas kernels  5.23 us (12%)
  other arithmetic  1.3 us (3%)
    ppermute x17, waiting for transfers between devices, swap(): return lax.ppermute(cells, 'frame', [(i, i ^ mask) for i in range(count)])  10.1 us
    ppermute x17, starting transfers between devices, swap(): return lax.ppermute(cells, 'frame', [(i, i ^ mask) for i in range(count)])  9.31 us
    pallas_call x7, Pallas kernels, call(): pl.pallas_call(body, out_shape=[jax.ShapeDtypeStruct(shape, kind) for sha...  5.23 us
    ppermute x2, starting transfers between devices, by_frames(): pieces[mask] = lax.ppermute(own, ('row', 'frame'), pairs)  5.01 us
    ppermute x3, starting transfers between devices, by_frames(): windows[mask] = lax.ppermute(windows[mask], 'row', pairs)  4.29 us
    ppermute x3, waiting for transfers between devices, by_frames(): windows[mask] = lax.ppermute(windows[mask], 'row', pairs)  3.99 us
    ppermute x3, starting transfers between devices, by_frames(): outs[mask] = lax.ppermute(strips[mask], 'frame', pairs)  2.83 us
    ppermute x3, waiting for transfers between devices, by_frames(): outs[mask] = lax.ppermute(strips[mask], 'frame', pairs)  1.37 us
  transfers between devices with their start and end apart: 25, of which 16 were waited for; matrix products, arithmetic and copies ran while one was open for 3% of the time, Pallas kernels for 3%

profile of v8, /device:TPU:0, one launch (start us, length us, event | category | flops | bytes accessed | tf_op | source)
XLA Modules:
  0.0 43.8 jit_solution(2083348771558608348)
XLA Ops:
  0.5 4.5 %collective-permute-start = (bf16[32,512]{1,0:T(8,128)(2,1)}, bf16[32,512]{1,0:T(8,128)(2,1)S(1)}, u32[]{:S(2)}, u32[]{:S(2)}) collective-permute-start(bf16[32,512]{1,0:T(8,128)(2,1)} %bitcast.12), channel_id=1, source_target_pairs={{0,2},{1,6},{2,10},{3,14},{4,3},{5,7},{6,11},{7,15},{8,0},{9,4},{1... | collective-permute-start | bytes 98312 | tf_op jit(solution)/shard_map/ppermute | solution.py:436
  5.0 1.8 %collective-permute-start.8 = (bf16[128,512]{1,0:T(8,128)(2,1)}, bf16[128,512]{1,0:T(8,128)(2,1)S(1)}, u32[]{:S(2)}, u32[]{:S(2)}) collective-permute-start(bf16[128,512]{1,0:T(8,128)(2,1)} %param.12), channel_id=1, source_target_pairs={{0,3},{1,2},{2,1},{3,0},{4,7},{5,6},{6,5},{7,4},{8,11},{9,10},{10,... | collective-permute-start | bytes 393224 | tf_op jit(solution)/shard_map/ppermute | solution.py:159
  6.8 1.3 %pad_maximum_fusion.refs_4_.refs_8_ = bf16[1024,512]{1,0:T(8,128)(2,1)S(1)} fusion(bf16[512,512]{1,0:T(8,128)(2,1)} %param.16, bf16[128,512]{1,0:T(8,128)(2,1)} %param.12, bf16[384,512]{1,0:T(8,128)(2,1)} %bitcast.8), kind=kLoop, calls=%fused_computation | loop fusion | flops 3145728 | bytes 2097152 | tf_op jit(solution)/shard_map/concatenate | solution.py:437
  8.1 0.7 %collective-permute-start.2 = (bf16[32,512]{1,0:T(8,128)(2,1)S(1)}, bf16[32,512]{1,0:T(8,128)(2,1)S(1)}, u32[]{:S(2)}, u32[]{:S(2)}) collective-permute-start(bf16[32,512]{1,0:T(8,128)(2,1)S(1)} %collective-permute-done.1.refs_1_), channel_id=1, source_target_pairs={{0,1},{1,0},{2,3},{3,2},{4,5},{5,4},{6,7},{7,6},{8,9},{9,8},{10,11... | collective-permute-start | bytes 98312 | tf_op jit(solution)/shard_map/ppermute | solution.py:159
  10.0 0.7 %shard_map.100 = (bf16[128,128]{1,0:T(8,128)(2,1)S(1)}, bf16[128,512]{1,0:T(8,128)(2,1)S(1)}) custom-call(bf16[32,512]{1,0:T(8,128)(2,1)S(1)} %collective-permute-done.2.refs_0_, bf16[32,512]{1,0:T(8,128)(2,1)S(1)} %collective-permute-done.1.refs_1_, bf16[32,512]{1,0:T(8,128)(2,1)S(1)} %collective-permute-done.refs_2_, ...), custom_call_target="tpu_custom_call" | custom-call | flops 50331648 | bytes 1179648 | tf_op jit(solution)/shard_map/pallas_call | solution.py:193
  10.7 1.7 %collective-permute-start.5 = (bf16[128,128]{1,0:T(8,128)(2,1)S(1)}, bf16[128,128]{1,0:T(8,128)(2,1)S(1)}, u32[]{:S(2)}, u32[]{:S(2)}) collective-permute-start(bf16[128,128]{1,0:T(8,128)(2,1)S(1)} %get-tuple-element.26.refs_0_), channel_id=1, source_target_pairs={{0,3},{1,2},{2,1},{3,0},{4,7},{5,6},{6,5},{7,4},{8,11},{9,10},{10,... | collective-permute-start | bytes 98312 | tf_op jit(solution)/shard_map/ppermute | solution.py:159
  13.0 1.1 %collective-permute-done.5.refs_3_ = bf16[128,128]{1,0:T(8,128)(2,1)S(1)} collective-permute-done((bf16[128,128]{1,0:T(8,128)(2,1)S(1)}, bf16[128,128]{1,0:T(8,128)(2,1)S(1)}, u32[]{:S(2)}, u32[]{:S(2)}) %collective-permute-start.5) | collective-permute-done | bytes 32800 | tf_op jit(solution)/shard_map/ppermute | solution.py:159
  14.5 0.7 %collective-permute-done.6.refs_2_ = bf16[128,128]{1,0:T(8,128)(2,1)S(1)} collective-permute-done((bf16[128,128]{1,0:T(8,128)(2,1)S(1)}, bf16[128,128]{1,0:T(8,128)(2,1)S(1)}, u32[]{:S(2)}, u32[]{:S(2)}) %collective-permute-start.6) | collective-permute-done | bytes 32800 | tf_op jit(solution)/shard_map/ppermute | solution.py:159
  15.3 1.2 %shard_map.101 = (f32[4,16,512]{2,1,0:T(8,128)S(1)}, bf16[4,16,512]{2,1,0:T(8,128)(2,1)S(1)}, bf16[4,16,512]{2,1,0:T(8,128)(2,1)S(1)}) custom-call(bf16[128,128]{1,0:T(8,128)(2,1)S(1)} %get-tuple-element.26.refs_0_, bf16[128,128]{1,0:T(8,128)(2,1)S(1)} %collective-permute-done.4.refs_1_, bf16[128,128]{1,0:T(8,128)(2,1)S(1)} %collective-permute-done.6.refs_2_, ...), custom_call_target="tpu_custom_call" | custom-call | flops 268435456 | bytes 2793472 | tf_op jit(solution)/shard_map/pallas_call | solution.py:193
  16.7 1.0 %collective-permute-done.10 = bf16[4,16,512]{2,1,0:T(8,128)(2,1)S(1)} collective-permute-done((bf16[4,16,512]{2,1,0:T(8,128)(2,1)S(1)}, bf16[4,16,512]{2,1,0:T(8,128)(2,1)S(1)}, u32[]{:S(2)}, u32[]{:S(2)}) %collective-permute-start.10) | collective-permute-done | bytes 65568 | tf_op jit(solution)/shard_map/ppermute | solution.py:159
  17.8 1.7 %collective-permute-start.11 = (bf16[4,16,512]{2,1,0:T(8,128)(2,1)S(1)}, bf16[4,16,512]{2,1,0:T(8,128)(2,1)S(1)}, u32[]{:S(2)}, u32[]{:S(2)}) collective-permute-start(bf16[4,16,512]{2,1,0:T(8,128)(2,1)S(1)} %get-tuple-element.41), channel_id=1, source_target_pairs={{0,3},{1,2},{2,1},{3,0},{4,7},{5,6},{6,5},{7,4},{8,11},{9,10},{10,... | collective-permute-start | bytes 196616 | tf_op jit(solution)/shard_map/ppermute | solution.py:159
  19.5 2.4 %collective-permute-done.11.refs_3_ = bf16[4,16,512]{2,1,0:T(8,128)(2,1)S(1)} collective-permute-done((bf16[4,16,512]{2,1,0:T(8,128)(2,1)S(1)}, bf16[4,16,512]{2,1,0:T(8,128)(2,1)S(1)}, u32[]{:S(2)}, u32[]{:S(2)}) %collective-permute-start.11) | collective-permute-done | bytes 65568 | tf_op jit(solution)/shard_map/ppermute | solution.py:159
  22.5 3.5 %collective-permute-start.13 = (bf16[3,16,512]{2,1,0:T(8,128)(2,1)S(1)}, bf16[3,16,512]{2,1,0:T(8,128)(2,1)S(1)}, u32[]{:S(2)}, u32[]{:S(2)}) collective-permute-start(bf16[3,16,512]{2,1,0:T(8,128)(2,1)S(1)} %get-tuple-element.33), channel_id=1, source_target_pairs={{0,8},{4,12},{8,0},{12,4},{1,9},{5,13},{9,1},{13,5},{2,10},{6,14},... | collective-permute-start | bytes 147464 | tf_op jit(solution)/shard_map/ppermute | solution.py:479
  26.3 2.1 %collective-permute-done.12.refs_1_ = bf16[3,16,512]{2,1,0:T(8,128)(2,1)S(1)} collective-permute-done((bf16[3,16,512]{2,1,0:T(8,128)(2,1)S(1)}, bf16[3,16,512]{2,1,0:T(8,128)(2,1)S(1)}, u32[]{:S(2)}, u32[]{:S(2)}) %collective-permute-start.12) | collective-permute-done | bytes 49184 | tf_op jit(solution)/shard_map/ppermute | solution.py:479
  28.4 1.4 %collective-permute-done.13.refs_2_ = bf16[3,16,512]{2,1,0:T(8,128)(2,1)S(1)} collective-permute-done((bf16[3,16,512]{2,1,0:T(8,128)(2,1)S(1)}, bf16[3,16,512]{2,1,0:T(8,128)(2,1)S(1)}, u32[]{:S(2)}, u32[]{:S(2)}) %collective-permute-start.13) | collective-permute-done | bytes 49184 | tf_op jit(solution)/shard_map/ppermute | solution.py:479
  30.4 0.7 %collective-permute-done.17.refs_6_ = bf16[3,16,512]{2,1,0:T(8,128)(2,1)S(1)} collective-permute-done((bf16[3,16,512]{2,1,0:T(8,128)(2,1)S(1)}, bf16[3,16,512]{2,1,0:T(8,128)(2,1)S(1)}, u32[]{:S(2)}, u32[]{:S(2)}) %collective-permute-start.17) | collective-permute-done | bytes 49184 | tf_op jit(solution)/shard_map/ppermute | solution.py:159
  31.6 1.3 %shard_map.103 = (bf16[4,4,16,128]{3,2,1,0:T(8,128)(2,1)S(1)}, bf16[4,2,16,128]{3,2,1,0:T(8,128)(2,1)S(1)}) custom-call(bf16[3,16,512]{2,1,0:T(8,128)(2,1)S(1)} %get-tuple-element.31.refs_0_, bf16[3,16,512]{2,1,0:T(8,128)(2,1)S(1)} %collective-permute-done.12.refs_1_, bf16[3,16,512]{2,1,0:T(8,128)(2,1)S(1)} %collective-permute-done.13.refs_2_, ...), custom_call_target="tpu_custom_call" | custom-call | flops 905969664 | bytes 3932160 | tf_op jit(solution)/shard_map/pallas_call | solution.py:193
  32.9 1.5 %collective-permute-start.19 = (bf16[4,4,16,128]{3,2,1,0:T(8,128)(2,1)S(1)}, bf16[4,4,16,128]{3,2,1,0:T(8,128)(2,1)S(1)}, u32[]{:S(2)}, u32[]{:S(2)}) collective-permute-start(bf16[4,4,16,128]{3,2,1,0:T(8,128)(2,1)S(1)} %get-tuple-element.35.own), channel_id=1, source_target_pairs={{0,3},{1,2},{2,1},{3,0},{4,7},{5,6},{6,5},{7,4},{8,11},{9,10},{10,... | collective-permute-start | bytes 196616 | tf_op jit(solution)/shard_map/ppermute | solution.py:159
  34.5 2.5 %collective-permute-done.19.refs_1_ = bf16[4,4,16,128]{3,2,1,0:T(8,128)(2,1)S(1)} collective-permute-done((bf16[4,4,16,128]{3,2,1,0:T(8,128)(2,1)S(1)}, bf16[4,4,16,128]{3,2,1,0:T(8,128)(2,1)S(1)}, u32[]{:S(2)}, u32[]{:S(2)}) %collective-permute-start.19) | collective-permute-done | bytes 65568 | tf_op jit(solution)/shard_map/ppermute | solution.py:159
  37.2 0.7 %shard_map.104.refs_2_ = f32[128,384]{1,0:T(8,128)S(1)} custom-call(bf16[4,4,16,128]{3,2,1,0:T(8,128)(2,1)S(1)} %get-tuple-element.35.own, bf16[4,4,16,128]{3,2,1,0:T(8,128)(2,1)S(1)} %collective-permute-done.21.other, bf16[3,3,3,128,512]{4,3,2,1,0:T(8,128)(2,1)S(1)} %copy-done.1), custom_call_target="tpu_custom_call" | custom-call | flops 226492416 | bytes 3670016 | tf_op jit(solution)/shard_map/pallas_call | solution.py:193
  38.3 0.7 %shard_map.105 = (bf16[32,128]{1,0:T(8,128)(2,1)S(1)}, bf16[32,128]{1,0:T(8,128)(2,1)S(1)}, bf16[32,128]{1,0:T(8,128)(2,1)S(1)}, bf16[32,128]{1,0:T(8,128)(2,1)S(1)}) custom-call(bf16[4,4,16,128]{3,2,1,0:T(8,128)(2,1)S(1)} %collective-permute-done.20.refs_0_, bf16[4,4,16,128]{3,2,1,0:T(8,128)(2,1)S(1)} %collective-permute-done.19.refs_1_, ...), custom_call_target="tpu_custom_call" | custom-call | flops 226492416 | bytes 3899392 | tf_op jit(solution)/shard_map/pallas_call | solution.py:193
  39.2 1.4 %collective-permute-start.23 = (bf16[32,128]{1,0:T(8,128)(2,1)S(1)}, bf16[32,128]{1,0:T(8,128)(2,1)S(1)}, u32[]{:S(2)}, u32[]{:S(2)}) collective-permute-start(bf16[32,128]{1,0:T(8,128)(2,1)S(1)} %get-tuple-element.39), channel_id=1, source_target_pairs={{0,2},{1,3},{2,0},{3,1},{4,6},{5,7},{6,4},{7,5},{8,10},{9,11},{10,... | collective-permute-start | bytes 24584 | tf_op jit(solution)/shard_map/ppermute | solution.py:513
  40.6 1.2 %collective-permute-start.24 = (bf16[32,128]{1,0:T(8,128)(2,1)S(1)}, bf16[32,128]{1,0:T(8,128)(2,1)S(1)}, u32[]{:S(2)}, u32[]{:S(2)}) collective-permute-start(bf16[32,128]{1,0:T(8,128)(2,1)S(1)} %get-tuple-element.40), channel_id=1, source_target_pairs={{0,3},{1,0},{2,1},{3,2},{4,7},{5,4},{6,5},{7,6},{8,11},{9,8},{10,9... | collective-permute-start | bytes 24584 | tf_op jit(solution)/shard_map/ppermute | solution.py:513
  42.1 0.7 %collective-permute-done.23.refs_2_ = bf16[32,128]{1,0:T(8,128)(2,1)S(1)} collective-permute-done((bf16[32,128]{1,0:T(8,128)(2,1)S(1)}, bf16[32,128]{1,0:T(8,128)(2,1)S(1)}, u32[]{:S(2)}, u32[]{:S(2)}) %collective-permute-start.23) | collective-permute-done | bytes 8224 | tf_op jit(solution)/shard_map/ppermute | solution.py:513
  (53 shorter events, 7.2 us)
Async XLA Ops:
  0.0 8.0 %collective-permute-start.1 = (bf16[32,512]{1,0:T(8,128)(2,1)}, bf16[32,512]{1,0:T(8,128)(2,1)S(1)}, u32[]{:S(2)}, u32[]{:S(2)}) collective-permute-start(bf16[32,512]{1,0:T(8,128)(2,1)} %bitcast.11), channel_id=1, source_target_pairs={{0,1},{1,5},{2,9},{3,13},{4,0},{5,4},{6,8},{7,12},{8,3},{9,7},{10,... | collective-permute-start | bytes 98312 | tf_op jit(solution)/shard_map/ppermute | solution.py:436
  0.5 7.5 %collective-permute-start = (bf16[32,512]{1,0:T(8,128)(2,1)}, bf16[32,512]{1,0:T(8,128)(2,1)S(1)}, u32[]{:S(2)}, u32[]{:S(2)}) collective-permute-start(bf16[32,512]{1,0:T(8,128)(2,1)} %bitcast.12), channel_id=1, source_target_pairs={{0,2},{1,6},{2,10},{3,14},{4,3},{5,7},{6,11},{7,15},{8,0},{9,4},{1... | collective-permute-start | bytes 98312 | tf_op jit(solution)/shard_map/ppermute | solution.py:436
  5.0 7.3 %collective-permute-start.8 = (bf16[128,512]{1,0:T(8,128)(2,1)}, bf16[128,512]{1,0:T(8,128)(2,1)S(1)}, u32[]{:S(2)}, u32[]{:S(2)}) collective-permute-start(bf16[128,512]{1,0:T(8,128)(2,1)} %param.12), channel_id=1, source_target_pairs={{0,3},{1,2},{2,1},{3,0},{4,7},{5,6},{6,5},{7,4},{8,11},{9,10},{10,... | collective-permute-start | bytes 393224 | tf_op jit(solution)/shard_map/ppermute | solution.py:159
  8.1 1.6 %collective-permute-start.2 = (bf16[32,512]{1,0:T(8,128)(2,1)S(1)}, bf16[32,512]{1,0:T(8,128)(2,1)S(1)}, u32[]{:S(2)}, u32[]{:S(2)}) collective-permute-start(bf16[32,512]{1,0:T(8,128)(2,1)S(1)} %collective-permute-done.1.refs_1_), channel_id=1, source_target_pairs={{0,1},{1,0},{2,3},{3,2},{4,5},{5,4},{6,7},{7,6},{8,9},{9,8},{10,11... | collective-permute-start | bytes 98312 | tf_op jit(solution)/shard_map/ppermute | solution.py:159
  8.8 5.7 %collective-permute-start.7 = (bf16[128,512]{1,0:T(8,128)(2,1)S(1)}, bf16[128,512]{1,0:T(8,128)(2,1)S(1)}, u32[]{:S(2)}, u32[]{:S(2)}) collective-permute-start(bf16[128,512]{1,0:T(8,128)(2,1)S(1)} %copy-done.4), channel_id=1, source_target_pairs={{0,1},{1,0},{2,3},{3,2},{4,5},{5,4},{6,7},{7,6},{8,9},{9,8},{10,11... | collective-permute-start | bytes 393224 | tf_op jit(solution)/shard_map/ppermute | solution.py:159
  10.7 3.4 %collective-permute-start.5 = (bf16[128,128]{1,0:T(8,128)(2,1)S(1)}, bf16[128,128]{1,0:T(8,128)(2,1)S(1)}, u32[]{:S(2)}, u32[]{:S(2)}) collective-permute-start(bf16[128,128]{1,0:T(8,128)(2,1)S(1)} %get-tuple-element.26.refs_0_), channel_id=1, source_target_pairs={{0,3},{1,2},{2,1},{3,0},{4,7},{5,6},{6,5},{7,4},{8,11},{9,10},{10,... | collective-permute-start | bytes 98312 | tf_op jit(solution)/shard_map/ppermute | solution.py:159
  12.4 2.9 %collective-permute-start.9 = (bf16[128,512]{1,0:T(8,128)(2,1)S(1)}, bf16[128,512]{1,0:T(8,128)(2,1)S(1)}, u32[]{:S(2)}, u32[]{:S(2)}) collective-permute-start(bf16[128,512]{1,0:T(8,128)(2,1)S(1)} %collective-permute-done.8.refs_6_), channel_id=1, source_target_pairs={{0,1},{1,0},{2,3},{3,2},{4,5},{5,4},{6,7},{7,6},{8,9},{9,8},{10,11... | collective-permute-start | bytes 393224 | tf_op jit(solution)/shard_map/ppermute | solution.py:159
  12.8 1.8 %collective-permute-start.4 = (bf16[128,128]{1,0:T(8,128)(2,1)S(1)}, bf16[128,128]{1,0:T(8,128)(2,1)S(1)}, u32[]{:S(2)}, u32[]{:S(2)}) collective-permute-start(bf16[128,128]{1,0:T(8,128)(2,1)S(1)} %get-tuple-element.26.refs_0_), channel_id=1, source_target_pairs={{0,1},{1,0},{2,3},{3,2},{4,5},{5,4},{6,7},{7,6},{8,9},{9,8},{10,11... | collective-permute-start | bytes 98312 | tf_op jit(solution)/shard_map/ppermute | solution.py:159
  14.1 1.2 %collective-permute-start.6 = (bf16[128,128]{1,0:T(8,128)(2,1)S(1)}, bf16[128,128]{1,0:T(8,128)(2,1)S(1)}, u32[]{:S(2)}, u32[]{:S(2)}) collective-permute-start(bf16[128,128]{1,0:T(8,128)(2,1)S(1)} %collective-permute-done.5.refs_3_), channel_id=1, source_target_pairs={{0,1},{1,0},{2,3},{3,2},{4,5},{5,4},{6,7},{7,6},{8,9},{9,8},{10,11... | collective-permute-start | bytes 98312 | tf_op jit(solution)/shard_map/ppermute | solution.py:159
  16.5 1.3 %collective-permute-start.10 = (bf16[4,16,512]{2,1,0:T(8,128)(2,1)S(1)}, bf16[4,16,512]{2,1,0:T(8,128)(2,1)S(1)}, u32[]{:S(2)}, u32[]{:S(2)}) collective-permute-start(bf16[4,16,512]{2,1,0:T(8,128)(2,1)S(1)} %get-tuple-element.29), channel_id=1, source_target_pairs={{0,1},{1,0},{2,3},{3,2},{4,5},{5,4},{6,7},{7,6},{8,9},{9,8},{10,11... | collective-permute-start | bytes 196616 | tf_op jit(solution)/shard_map/ppermute | solution.py:159
  17.8 4.1 %collective-permute-start.11 = (bf16[4,16,512]{2,1,0:T(8,128)(2,1)S(1)}, bf16[4,16,512]{2,1,0:T(8,128)(2,1)S(1)}, u32[]{:S(2)}, u32[]{:S(2)}) collective-permute-start(bf16[4,16,512]{2,1,0:T(8,128)(2,1)S(1)} %get-tuple-element.41), channel_id=1, source_target_pairs={{0,3},{1,2},{2,1},{3,0},{4,7},{5,6},{6,5},{7,4},{8,11},{9,10},{10,... | collective-permute-start | bytes 196616 | tf_op jit(solution)/shard_map/ppermute | solution.py:159
  22.0 6.4 %collective-permute-start.12 = (bf16[3,16,512]{2,1,0:T(8,128)(2,1)S(1)}, bf16[3,16,512]{2,1,0:T(8,128)(2,1)S(1)}, u32[]{:S(2)}, u32[]{:S(2)}) collective-permute-start(bf16[3,16,512]{2,1,0:T(8,128)(2,1)S(1)} %get-tuple-element.32), channel_id=1, source_target_pairs={{0,4},{4,8},{8,12},{12,0},{1,5},{5,9},{9,13},{13,1},{2,6},{6,10},{... | collective-permute-start | bytes 147464 | tf_op jit(solution)/shard_map/ppermute | solution.py:479
  22.5 7.4 %collective-permute-start.13 = (bf16[3,16,512]{2,1,0:T(8,128)(2,1)S(1)}, bf16[3,16,512]{2,1,0:T(8,128)(2,1)S(1)}, u32[]{:S(2)}, u32[]{:S(2)}) collective-permute-start(bf16[3,16,512]{2,1,0:T(8,128)(2,1)S(1)} %get-tuple-element.33), channel_id=1, source_target_pairs={{0,8},{4,12},{8,0},{12,4},{1,9},{5,13},{9,1},{13,5},{2,10},{6,14},... | collective-permute-start | bytes 147464 | tf_op jit(solution)/shard_map/ppermute | solution.py:479
  26.0 4.3 %collective-permute-start.14 = (bf16[3,16,512]{2,1,0:T(8,128)(2,1)S(1)}, bf16[3,16,512]{2,1,0:T(8,128)(2,1)S(1)}, u32[]{:S(2)}, u32[]{:S(2)}) collective-permute-start(bf16[3,16,512]{2,1,0:T(8,128)(2,1)S(1)} %get-tuple-element.34), channel_id=1, source_target_pairs={{0,12},{4,0},{8,4},{12,8},{1,13},{5,1},{9,5},{13,9},{2,14},{6,2},{... | collective-permute-start | bytes 147464 | tf_op jit(solution)/shard_map/ppermute | solution.py:479
  26.3 4.1 %collective-permute-start.15 = (bf16[3,16,512]{2,1,0:T(8,128)(2,1)S(1)}, bf16[3,16,512]{2,1,0:T(8,128)(2,1)S(1)}, u32[]{:S(2)}, u32[]{:S(2)}) collective-permute-start(bf16[3,16,512]{2,1,0:T(8,128)(2,1)S(1)} %get-tuple-element.31.refs_0_), channel_id=1, source_target_pairs={{0,1},{1,0},{2,3},{3,2},{4,5},{5,4},{6,7},{7,6},{8,9},{9,8},{10,11... | collective-permute-start | bytes 147464 | tf_op jit(solution)/shard_map/ppermute | solution.py:159
  28.4 2.0 %collective-permute-start.16 = (bf16[3,16,512]{2,1,0:T(8,128)(2,1)S(1)}, bf16[3,16,512]{2,1,0:T(8,128)(2,1)S(1)}, u32[]{:S(2)}, u32[]{:S(2)}) collective-permute-start(bf16[3,16,512]{2,1,0:T(8,128)(2,1)S(1)} %collective-permute-done.12.refs_1_), channel_id=1, source_target_pairs={{0,1},{1,0},{2,3},{3,2},{4,5},{5,4},{6,7},{7,6},{8,9},{9,8},{10,11... | collective-permute-start | bytes 147464 | tf_op jit(solution)/shard_map/ppermute | solution.py:159
  29.9 1.2 %collective-permute-start.17 = (bf16[3,16,512]{2,1,0:T(8,128)(2,1)S(1)}, bf16[3,16,512]{2,1,0:T(8,128)(2,1)S(1)}, u32[]{:S(2)}, u32[]{:S(2)}) collective-permute-start(bf16[3,16,512]{2,1,0:T(8,128)(2,1)S(1)} %collective-permute-done.13.refs_2_), channel_id=1, source_target_pairs={{0,1},{1,0},{2,3},{3,2},{4,5},{5,4},{6,7},{7,6},{8,9},{9,8},{10,11... | collective-permute-start | bytes 147464 | tf_op jit(solution)/shard_map/ppermute | solution.py:159
  30.3 1.2 %collective-permute-start.18 = (bf16[3,16,512]{2,1,0:T(8,128)(2,1)S(1)}, bf16[3,16,512]{2,1,0:T(8,128)(2,1)S(1)}, u32[]{:S(2)}, u32[]{:S(2)}) collective-permute-start(bf16[3,16,512]{2,1,0:T(8,128)(2,1)S(1)} %collective-permute-done.14.refs_3_), channel_id=1, source_target_pairs={{0,1},{1,0},{2,3},{3,2},{4,5},{5,4},{6,7},{7,6},{8,9},{9,8},{10,11... | collective-permute-start | bytes 147464 | tf_op jit(solution)/shard_map/ppermute | solution.py:159
  32.9 4.1 %collective-permute-start.19 = (bf16[4,4,16,128]{3,2,1,0:T(8,128)(2,1)S(1)}, bf16[4,4,16,128]{3,2,1,0:T(8,128)(2,1)S(1)}, u32[]{:S(2)}, u32[]{:S(2)}) collective-permute-start(bf16[4,4,16,128]{3,2,1,0:T(8,128)(2,1)S(1)} %get-tuple-element.35.own), channel_id=1, source_target_pairs={{0,3},{1,2},{2,1},{3,0},{4,7},{5,6},{6,5},{7,4},{8,11},{9,10},{10,... | collective-permute-start | bytes 196616 | tf_op jit(solution)/shard_map/ppermute | solution.py:159
  34.4 2.8 %collective-permute-start.21 = (bf16[4,4,16,128]{3,2,1,0:T(8,128)(2,1)S(1)}, bf16[4,4,16,128]{3,2,1,0:T(8,128)(2,1)S(1)}, u32[]{:S(2)}, u32[]{:S(2)}) collective-permute-start(bf16[4,4,16,128]{3,2,1,0:T(8,128)(2,1)S(1)} %get-tuple-element.35.own), channel_id=1, source_target_pairs={{0,1},{1,0},{2,3},{3,2},{4,5},{5,4},{6,7},{7,6},{8,9},{9,8},{10,11... | collective-permute-start | bytes 196616 | tf_op jit(solution)/shard_map/ppermute | solution.py:159
  37.0 1.3 %collective-permute-start.20 = (bf16[4,4,16,128]{3,2,1,0:T(8,128)(2,1)S(1)}, bf16[4,4,16,128]{3,2,1,0:T(8,128)(2,1)S(1)}, u32[]{:S(2)}, u32[]{:S(2)}) collective-permute-start(bf16[4,4,16,128]{3,2,1,0:T(8,128)(2,1)S(1)} %collective-permute-done.19.refs_1_), channel_id=1, source_target_pairs={{0,1},{1,0},{2,3},{3,2},{4,5},{5,4},{6,7},{7,6},{8,9},{9,8},{10,11... | collective-permute-start | bytes 196616 | tf_op jit(solution)/shard_map/ppermute | solution.py:159
  39.0 3.1 %collective-permute-start.22 = (bf16[32,128]{1,0:T(8,128)(2,1)S(1)}, bf16[32,128]{1,0:T(8,128)(2,1)S(1)}, u32[]{:S(2)}, u32[]{:S(2)}) collective-permute-start(bf16[32,128]{1,0:T(8,128)(2,1)S(1)} %get-tuple-element.38), channel_id=1, source_target_pairs={{0,1},{1,2},{2,3},{3,0},{4,5},{5,6},{6,7},{7,4},{8,9},{9,10},{10,1... | collective-permute-start | bytes 24584 | tf_op jit(solution)/shard_map/ppermute | solution.py:513
  39.2 3.7 %collective-permute-start.23 = (bf16[32,128]{1,0:T(8,128)(2,1)S(1)}, bf16[32,128]{1,0:T(8,128)(2,1)S(1)}, u32[]{:S(2)}, u32[]{:S(2)}) collective-permute-start(bf16[32,128]{1,0:T(8,128)(2,1)S(1)} %get-tuple-element.39), channel_id=1, source_target_pairs={{0,2},{1,3},{2,0},{3,1},{4,6},{5,7},{6,4},{7,5},{8,10},{9,11},{10,... | collective-permute-start | bytes 24584 | tf_op jit(solution)/shard_map/ppermute | solution.py:513
  40.6 2.5 %collective-permute-start.24 = (bf16[32,128]{1,0:T(8,128)(2,1)S(1)}, bf16[32,128]{1,0:T(8,128)(2,1)S(1)}, u32[]{:S(2)}, u32[]{:S(2)}) collective-permute-start(bf16[32,128]{1,0:T(8,128)(2,1)S(1)} %get-tuple-element.40), channel_id=1, source_target_pairs={{0,3},{1,0},{2,1},{3,2},{4,7},{5,4},{6,5},{7,6},{8,11},{9,8},{10,9... | collective-permute-start | bytes 24584 | tf_op jit(solution)/shard_map/ppermute | solution.py:513
  (8 other events, 98.1 us)
